TPU v7x, 512 devices: a whole 4x4x16 slice. The times are simulated.
512 devices in a mesh: row: 32 (over x_lo, z), col: 16 (over y, x_hi, core).
Axes of the slice: x: 4 (x_hi: 2, x_lo: 2; x = x_hi * 2 + x_lo), y: 4, z: 16, core: 2. Of those that a mesh axis runs over, the one named last changes fastest.
Arguments:
- density: float32 [128, 16, 128, 128], P('row', 'col'), may hold values from -1 to 1
- columns: int32 [128, 16], replicated, may hold values from -1 to 7, as said below
Outputs:
- squared: float32 [128, 16, 128, 128], P('row', 'col')
- purified: float32 [128, 16, 128, 128], P('row', 'col')
Inputs may be any that keep to these rules, and one draw needn't show every extreme that they name: Each block row has at most one filled block in each group of 8 block columns; every diagonal block is filled (entry (r, r // 8) is r % 8); the share of filled groups differs from block row to block row.
All inputs are finite; a program needn't handle non-finite values.
Results may differ from a plain program's by a relative error of at most 0.0003.
Values sent between devices are 32-bit elements; how exact they have to be, the bound alone decides.
No kernel may reach another device: no remote copies, remote signals or barrier semaphores. Data moves between devices by JAX's collectives and lax.ppermute only.
A program may use at most 128 MiB of HBM per device.

v0:
```python
import jax
import jax.numpy as jnp
from jax import lax
from jax.sharding import PartitionSpec as P


def shifted(shard, axis, by):
    length = lax.axis_size(axis)
    return lax.ppermute(shard, axis, [(i, (i + by) % length) for i in range(length)])


def pair_terms(panel, incoming, first_row, local_rows, here_cols, here_vector, width):
    block_rows = panel.shape[0]
    group_count = panel.shape[1]
    order = panel.shape[2]
    shards = incoming.shape[0] // block_rows
    firsts = first_row + jnp.arange(shards, dtype=jnp.int32) * block_rows
    groups = firsts // width
    pick_table = (groups[:, None] == jnp.arange(group_count, dtype=jnp.int32)[None, :]).astype(
        jnp.int32
    )
    left_cols = jnp.sum(local_rows[:, None, :] * pick_table[None, :, :], axis=2)
    target = groups[None, :] * width + left_cols - firsts[None, :]
    inside = (left_cols >= 0) & (target >= 0) & (target < block_rows)
    offset = jnp.clip(target, 0, block_rows - 1)
    chosen_index = jnp.arange(shards, dtype=jnp.int32)[None, :] * block_rows + offset
    right_cols = lax.dynamic_slice_in_dim(here_vector, first_row, incoming.shape[0])
    lookup = (
        chosen_index[:, :, None] == jnp.arange(incoming.shape[0], dtype=jnp.int32)[None, None, :]
    )
    matched_cols = jnp.sum(right_cols[None, None, :] * lookup.astype(jnp.int32), axis=2)
    weight = inside & (here_cols[:, None] >= 0) & (matched_cols == here_cols[:, None])
    chosen_right = jnp.take(incoming, chosen_index.reshape(-1), axis=0).reshape(
        block_rows, shards, order, order
    )
    chosen_left = jnp.take(panel, groups, axis=1)
    scaled = chosen_left * weight[:, :, None, None].astype(jnp.float32)
    return jnp.einsum("rsab,rsbc->rac", scaled, chosen_right, precision=lax.Precision.HIGHEST)


def body(density, columns):
    block_rows = density.shape[0]
    order = density.shape[2]
    row_count = lax.axis_size("row")
    group_count = lax.axis_size("col")
    all_rows = columns.shape[0]
    width = all_rows // group_count
    row_here = lax.axis_index("row")
    col_here = lax.axis_index("col")
    here_vector = lax.dynamic_index_in_dim(columns, col_here, 1, keepdims=False)
    local_rows = lax.dynamic_slice_in_dim(columns, row_here * block_rows, block_rows, 0)
    here_cols = lax.dynamic_slice_in_dim(here_vector, row_here * block_rows, block_rows, 0)
    keep = (here_cols >= 0).astype(jnp.float32)[:, None, None, None]
    masked = density * keep
    right_part = masked[:, 0]
    first_panel = lax.all_gather(masked, "col", axis=1, tiled=True)

    def terms(panel, incoming, first_row):
        return pair_terms(panel, incoming, first_row, local_rows, here_cols, here_vector, width)

    summed = jnp.zeros((block_rows, order, order), jnp.float32)
    panel_store = jnp.zeros((all_rows, order, order), jnp.float32)

    def advance(position, carry):
        running, incoming, stored = carry
        source = (row_here + position) % row_count
        first_row = source * block_rows
        stored = lax.dynamic_update_slice_in_dim(stored, incoming, first_row, 0)
        running = running + terms(first_panel, incoming, first_row)
        incoming = shifted(incoming, "row", -1)
        return (running, incoming, stored)

    summed, incoming, panel_store = lax.fori_loop(
        0, row_count - 1, advance, (summed, right_part, panel_store)
    )
    source = (row_here + row_count - 1) % row_count
    first_row = source * block_rows
    panel_store = lax.dynamic_update_slice_in_dim(panel_store, incoming, first_row, 0)
    summed = summed + terms(first_panel, incoming, first_row)
    squared = summed[:, None] * keep
    second_panel = lax.all_gather(squared, "col", axis=1, tiled=True)
    cubed = terms(second_panel, panel_store, jnp.zeros((), jnp.int32))[:, None] * keep
    return (squared, 3.0 * squared - 2.0 * cubed)


def solution(mesh):
    return jax.shard_map(
        body,
        mesh=mesh,
        in_specs=(P("row", "col", None, None), P()),
        out_specs=(P("row", "col", None, None), P("row", "col", None, None)),
        check_vma=False,
    )
```

profile of v0, /device:TPU:1, one launch (start us, length us, event | category | flops | bytes accessed | tf_op | source)
XLA Modules:
  0.0 534.7 jit_solution(7625704763455944476)
XLA Ops:
  8.0 1.7 bitcast_multiply_fusion.12
  13.5 74.7 %all-gather.4.cloned.1.call-done = f32[4,16,128,128]{3,2,0,1:T(8,128)} async-done(((f32[4,1,128,128]{3,2,0,1:T(8,128)}), f32[4,16,128,128]{3,2,0,1:T(8,128)}) %all-gather.4.cloned.1.call-update) | async-done | bytes 4194320 | tf_op jit(solution)/shard_map/all_gather | solution.py:56
  88.3 4.3 broadcast_in_dim.104
  92.6 315.7 %while.21 = (s32[]{:T(128)}, f32[4,128,128]{2,1,0:T(8,128)S(1)}, f32[4,128,128]{2,1,0:T(8,128)S(1)}, f32[128,128,128]{2,1,0:T(8,128)}, s32[]{:T(128)}, /*index=5...) while((s32[]{:T(128)}, f32[4,128,128]{2,1,0:T(8,128)S(1)}, ...), condition=%wide.region_3.6_spmd.clone, body=%wide.region_0.5_spmd.clone.sunk | while | flops 100992336 | bytes 3676467 | solution.py:73
  92.6 5.7 %collective-permute-start = (f32[4,128,128]{2,1,0:T(8,128)S(1)}, f32[4,128,128]{2,1,0:T(8,128)S(1)}, u32[]{:S(2)}, u32[]{:S(2)}) collective-permute-start(f32[4,128,128]{2,1,0:T(8,128)S(1)} %copy.48), channel_id=1, source_target_pairs={{0,496},{16,0},{32,16},{48,32},{64,48},{80,64},{96,80},{112,96},{1... | collective-permute-start | bytes 786440 | tf_op jit(solution)/shard_map/while/body/eval_jaxpr/ppermute | solution.py:9
  100.1 1.4 convolution_add_fusion.3
  101.5 2.2 collective-permute-done
  103.7 6.2 %collective-permute-start = (f32[4,128,128]{2,1,0:T(8,128)S(1)}, f32[4,128,128]{2,1,0:T(8,128)S(1)}, u32[]{:S(2)}, u32[]{:S(2)}) collective-permute-start(f32[4,128,128]{2,1,0:T(8,128)S(1)} %copy.48), channel_id=1, source_target_pairs={{0,496},{16,0},{32,16},{48,32},{64,48},{80,64},{96,80},{112,96},{1... | collective-permute-start | bytes 786440 | tf_op jit(solution)/shard_map/while/body/eval_jaxpr/ppermute | solution.py:9
  114.5 6.2 %collective-permute-start = (f32[4,128,128]{2,1,0:T(8,128)S(1)}, f32[4,128,128]{2,1,0:T(8,128)S(1)}, u32[]{:S(2)}, u32[]{:S(2)}) collective-permute-start(f32[4,128,128]{2,1,0:T(8,128)S(1)} %copy.48), channel_id=1, source_target_pairs={{0,496},{16,0},{32,16},{48,32},{64,48},{80,64},{96,80},{112,96},{1... | collective-permute-start | bytes 786440 | tf_op jit(solution)/shard_map/while/body/eval_jaxpr/ppermute | solution.py:9
  122.5 1.4 convolution_add_fusion.3
  124.3 6.2 %collective-permute-start = (f32[4,128,128]{2,1,0:T(8,128)S(1)}, f32[4,128,128]{2,1,0:T(8,128)S(1)}, u32[]{:S(2)}, u32[]{:S(2)}) collective-permute-start(f32[4,128,128]{2,1,0:T(8,128)S(1)} %copy.48), channel_id=1, source_target_pairs={{0,496},{16,0},{32,16},{48,32},{64,48},{80,64},{96,80},{112,96},{1... | collective-permute-start | bytes 786440 | tf_op jit(solution)/shard_map/while/body/eval_jaxpr/ppermute | solution.py:9
  133.9 5.9 %collective-permute-start = (f32[4,128,128]{2,1,0:T(8,128)S(1)}, f32[4,128,128]{2,1,0:T(8,128)S(1)}, u32[]{:S(2)}, u32[]{:S(2)}) collective-permute-start(f32[4,128,128]{2,1,0:T(8,128)S(1)} %copy.48), channel_id=1, source_target_pairs={{0,496},{16,0},{32,16},{48,32},{64,48},{80,64},{96,80},{112,96},{1... | collective-permute-start | bytes 786440 | tf_op jit(solution)/shard_map/while/body/eval_jaxpr/ppermute | solution.py:9
  141.6 1.4 convolution_add_fusion.3
  143.1 5.9 %collective-permute-start = (f32[4,128,128]{2,1,0:T(8,128)S(1)}, f32[4,128,128]{2,1,0:T(8,128)S(1)}, u32[]{:S(2)}, u32[]{:S(2)}) collective-permute-start(f32[4,128,128]{2,1,0:T(8,128)S(1)} %copy.48), channel_id=1, source_target_pairs={{0,496},{16,0},{32,16},{48,32},{64,48},{80,64},{96,80},{112,96},{1... | collective-permute-start | bytes 786440 | tf_op jit(solution)/shard_map/while/body/eval_jaxpr/ppermute | solution.py:9
  150.9 1.4 convolution_add_fusion.3
  152.4 5.9 %collective-permute-start = (f32[4,128,128]{2,1,0:T(8,128)S(1)}, f32[4,128,128]{2,1,0:T(8,128)S(1)}, u32[]{:S(2)}, u32[]{:S(2)}) collective-permute-start(f32[4,128,128]{2,1,0:T(8,128)S(1)} %copy.48), channel_id=1, source_target_pairs={{0,496},{16,0},{32,16},{48,32},{64,48},{80,64},{96,80},{112,96},{1... | collective-permute-start | bytes 786440 | tf_op jit(solution)/shard_map/while/body/eval_jaxpr/ppermute | solution.py:9
  160.1 1.4 convolution_add_fusion.3
  161.6 5.9 %collective-permute-start = (f32[4,128,128]{2,1,0:T(8,128)S(1)}, f32[4,128,128]{2,1,0:T(8,128)S(1)}, u32[]{:S(2)}, u32[]{:S(2)}) collective-permute-start(f32[4,128,128]{2,1,0:T(8,128)S(1)} %copy.48), channel_id=1, source_target_pairs={{0,496},{16,0},{32,16},{48,32},{64,48},{80,64},{96,80},{112,96},{1... | collective-permute-start | bytes 786440 | tf_op jit(solution)/shard_map/while/body/eval_jaxpr/ppermute | solution.py:9
  171.2 5.9 %collective-permute-start = (f32[4,128,128]{2,1,0:T(8,128)S(1)}, f32[4,128,128]{2,1,0:T(8,128)S(1)}, u32[]{:S(2)}, u32[]{:S(2)}) collective-permute-start(f32[4,128,128]{2,1,0:T(8,128)S(1)} %copy.48), channel_id=1, source_target_pairs={{0,496},{16,0},{32,16},{48,32},{64,48},{80,64},{96,80},{112,96},{1... | collective-permute-start | bytes 786440 | tf_op jit(solution)/shard_map/while/body/eval_jaxpr/ppermute | solution.py:9
  180.4 1.5 collective-permute-done
  181.9 5.9 %collective-permute-start = (f32[4,128,128]{2,1,0:T(8,128)S(1)}, f32[4,128,128]{2,1,0:T(8,128)S(1)}, u32[]{:S(2)}, u32[]{:S(2)}) collective-permute-start(f32[4,128,128]{2,1,0:T(8,128)S(1)} %copy.48), channel_id=1, source_target_pairs={{0,496},{16,0},{32,16},{48,32},{64,48},{80,64},{96,80},{112,96},{1... | collective-permute-start | bytes 786440 | tf_op jit(solution)/shard_map/while/body/eval_jaxpr/ppermute | solution.py:9
  191.1 2.6 collective-permute-done
  193.7 6.0 %collective-permute-start = (f32[4,128,128]{2,1,0:T(8,128)S(1)}, f32[4,128,128]{2,1,0:T(8,128)S(1)}, u32[]{:S(2)}, u32[]{:S(2)}) collective-permute-start(f32[4,128,128]{2,1,0:T(8,128)S(1)} %copy.48), channel_id=1, source_target_pairs={{0,496},{16,0},{32,16},{48,32},{64,48},{80,64},{96,80},{112,96},{1... | collective-permute-start | bytes 786440 | tf_op jit(solution)/shard_map/while/body/eval_jaxpr/ppermute | solution.py:9
  201.5 1.4 convolution_add_fusion.3
  203.0 2.0 collective-permute-done
  205.0 6.2 %collective-permute-start = (f32[4,128,128]{2,1,0:T(8,128)S(1)}, f32[4,128,128]{2,1,0:T(8,128)S(1)}, u32[]{:S(2)}, u32[]{:S(2)}) collective-permute-start(f32[4,128,128]{2,1,0:T(8,128)S(1)} %copy.48), channel_id=1, source_target_pairs={{0,496},{16,0},{32,16},{48,32},{64,48},{80,64},{96,80},{112,96},{1... | collective-permute-start | bytes 786440 | tf_op jit(solution)/shard_map/while/body/eval_jaxpr/ppermute | solution.py:9
  215.6 6.2 %collective-permute-start = (f32[4,128,128]{2,1,0:T(8,128)S(1)}, f32[4,128,128]{2,1,0:T(8,128)S(1)}, u32[]{:S(2)}, u32[]{:S(2)}) collective-permute-start(f32[4,128,128]{2,1,0:T(8,128)S(1)} %copy.48), channel_id=1, source_target_pairs={{0,496},{16,0},{32,16},{48,32},{64,48},{80,64},{96,80},{112,96},{1... | collective-permute-start | bytes 786440 | tf_op jit(solution)/shard_map/while/body/eval_jaxpr/ppermute | solution.py:9
  225.1 6.3 %collective-permute-start = (f32[4,128,128]{2,1,0:T(8,128)S(1)}, f32[4,128,128]{2,1,0:T(8,128)S(1)}, u32[]{:S(2)}, u32[]{:S(2)}) collective-permute-start(f32[4,128,128]{2,1,0:T(8,128)S(1)} %copy.48), channel_id=1, source_target_pairs={{0,496},{16,0},{32,16},{48,32},{64,48},{80,64},{96,80},{112,96},{1... | collective-permute-start | bytes 786440 | tf_op jit(solution)/shard_map/while/body/eval_jaxpr/ppermute | solution.py:9
  233.3 1.4 convolution_add_fusion.3
  234.8 5.9 %collective-permute-start = (f32[4,128,128]{2,1,0:T(8,128)S(1)}, f32[4,128,128]{2,1,0:T(8,128)S(1)}, u32[]{:S(2)}, u32[]{:S(2)}) collective-permute-start(f32[4,128,128]{2,1,0:T(8,128)S(1)} %copy.48), channel_id=1, source_target_pairs={{0,496},{16,0},{32,16},{48,32},{64,48},{80,64},{96,80},{112,96},{1... | collective-permute-start | bytes 786440 | tf_op jit(solution)/shard_map/while/body/eval_jaxpr/ppermute | solution.py:9
  242.5 1.4 convolution_add_fusion.3
  244.1 5.9 %collective-permute-start = (f32[4,128,128]{2,1,0:T(8,128)S(1)}, f32[4,128,128]{2,1,0:T(8,128)S(1)}, u32[]{:S(2)}, u32[]{:S(2)}) collective-permute-start(f32[4,128,128]{2,1,0:T(8,128)S(1)} %copy.48), channel_id=1, source_target_pairs={{0,496},{16,0},{32,16},{48,32},{64,48},{80,64},{96,80},{112,96},{1... | collective-permute-start | bytes 786440 | tf_op jit(solution)/shard_map/while/body/eval_jaxpr/ppermute | solution.py:9
  253.3 5.9 %collective-permute-start = (f32[4,128,128]{2,1,0:T(8,128)S(1)}, f32[4,128,128]{2,1,0:T(8,128)S(1)}, u32[]{:S(2)}, u32[]{:S(2)}) collective-permute-start(f32[4,128,128]{2,1,0:T(8,128)S(1)} %copy.48), channel_id=1, source_target_pairs={{0,496},{16,0},{32,16},{48,32},{64,48},{80,64},{96,80},{112,96},{1... | collective-permute-start | bytes 786440 | tf_op jit(solution)/shard_map/while/body/eval_jaxpr/ppermute | solution.py:9
  262.6 5.9 %collective-permute-start = (f32[4,128,128]{2,1,0:T(8,128)S(1)}, f32[4,128,128]{2,1,0:T(8,128)S(1)}, u32[]{:S(2)}, u32[]{:S(2)}) collective-permute-start(f32[4,128,128]{2,1,0:T(8,128)S(1)} %copy.48), channel_id=1, source_target_pairs={{0,496},{16,0},{32,16},{48,32},{64,48},{80,64},{96,80},{112,96},{1... | collective-permute-start | bytes 786440 | tf_op jit(solution)/shard_map/while/body/eval_jaxpr/ppermute | solution.py:9
  270.3 1.4 convolution_add_fusion.3
  272.3 5.9 %collective-permute-start = (f32[4,128,128]{2,1,0:T(8,128)S(1)}, f32[4,128,128]{2,1,0:T(8,128)S(1)}, u32[]{:S(2)}, u32[]{:S(2)}) collective-permute-start(f32[4,128,128]{2,1,0:T(8,128)S(1)} %copy.48), channel_id=1, source_target_pairs={{0,496},{16,0},{32,16},{48,32},{64,48},{80,64},{96,80},{112,96},{1... | collective-permute-start | bytes 786440 | tf_op jit(solution)/shard_map/while/body/eval_jaxpr/ppermute | solution.py:9
  281.5 1.6 collective-permute-done
  283.2 5.9 %collective-permute-start = (f32[4,128,128]{2,1,0:T(8,128)S(1)}, f32[4,128,128]{2,1,0:T(8,128)S(1)}, u32[]{:S(2)}, u32[]{:S(2)}) collective-permute-start(f32[4,128,128]{2,1,0:T(8,128)S(1)} %copy.48), channel_id=1, source_target_pairs={{0,496},{16,0},{32,16},{48,32},{64,48},{80,64},{96,80},{112,96},{1... | collective-permute-start | bytes 786440 | tf_op jit(solution)/shard_map/while/body/eval_jaxpr/ppermute | solution.py:9
  291.0 1.4 convolution_add_fusion.3
  292.4 2.8 collective-permute-done
  295.3 6.1 %collective-permute-start = (f32[4,128,128]{2,1,0:T(8,128)S(1)}, f32[4,128,128]{2,1,0:T(8,128)S(1)}, u32[]{:S(2)}, u32[]{:S(2)}) collective-permute-start(f32[4,128,128]{2,1,0:T(8,128)S(1)} %copy.48), channel_id=1, source_target_pairs={{0,496},{16,0},{32,16},{48,32},{64,48},{80,64},{96,80},{112,96},{1... | collective-permute-start | bytes 786440 | tf_op jit(solution)/shard_map/while/body/eval_jaxpr/ppermute | solution.py:9
  303.2 1.4 convolution_add_fusion.3
  304.6 2.0 collective-permute-done
  306.7 6.2 %collective-permute-start = (f32[4,128,128]{2,1,0:T(8,128)S(1)}, f32[4,128,128]{2,1,0:T(8,128)S(1)}, u32[]{:S(2)}, u32[]{:S(2)}) collective-permute-start(f32[4,128,128]{2,1,0:T(8,128)S(1)} %copy.48), channel_id=1, source_target_pairs={{0,496},{16,0},{32,16},{48,32},{64,48},{80,64},{96,80},{112,96},{1... | collective-permute-start | bytes 786440 | tf_op jit(solution)/shard_map/while/body/eval_jaxpr/ppermute | solution.py:9
  314.7 1.4 convolution_add_fusion.3
  317.3 6.2 %collective-permute-start = (f32[4,128,128]{2,1,0:T(8,128)S(1)}, f32[4,128,128]{2,1,0:T(8,128)S(1)}, u32[]{:S(2)}, u32[]{:S(2)}) collective-permute-start(f32[4,128,128]{2,1,0:T(8,128)S(1)} %copy.48), channel_id=1, source_target_pairs={{0,496},{16,0},{32,16},{48,32},{64,48},{80,64},{96,80},{112,96},{1... | collective-permute-start | bytes 786440 | tf_op jit(solution)/shard_map/while/body/eval_jaxpr/ppermute | solution.py:9
  325.3 1.4 convolution_add_fusion.3
  326.8 6.3 %collective-permute-start = (f32[4,128,128]{2,1,0:T(8,128)S(1)}, f32[4,128,128]{2,1,0:T(8,128)S(1)}, u32[]{:S(2)}, u32[]{:S(2)}) collective-permute-start(f32[4,128,128]{2,1,0:T(8,128)S(1)} %copy.48), channel_id=1, source_target_pairs={{0,496},{16,0},{32,16},{48,32},{64,48},{80,64},{96,80},{112,96},{1... | collective-permute-start | bytes 786440 | tf_op jit(solution)/shard_map/while/body/eval_jaxpr/ppermute | solution.py:9
  336.5 5.9 %collective-permute-start = (f32[4,128,128]{2,1,0:T(8,128)S(1)}, f32[4,128,128]{2,1,0:T(8,128)S(1)}, u32[]{:S(2)}, u32[]{:S(2)}) collective-permute-start(f32[4,128,128]{2,1,0:T(8,128)S(1)} %copy.48), channel_id=1, source_target_pairs={{0,496},{16,0},{32,16},{48,32},{64,48},{80,64},{96,80},{112,96},{1... | collective-permute-start | bytes 786440 | tf_op jit(solution)/shard_map/while/body/eval_jaxpr/ppermute | solution.py:9
  345.7 5.9 %collective-permute-start = (f32[4,128,128]{2,1,0:T(8,128)S(1)}, f32[4,128,128]{2,1,0:T(8,128)S(1)}, u32[]{:S(2)}, u32[]{:S(2)}) collective-permute-start(f32[4,128,128]{2,1,0:T(8,128)S(1)} %copy.48), channel_id=1, source_target_pairs={{0,496},{16,0},{32,16},{48,32},{64,48},{80,64},{96,80},{112,96},{1... | collective-permute-start | bytes 786440 | tf_op jit(solution)/shard_map/while/body/eval_jaxpr/ppermute | solution.py:9
  355.0 5.9 %collective-permute-start = (f32[4,128,128]{2,1,0:T(8,128)S(1)}, f32[4,128,128]{2,1,0:T(8,128)S(1)}, u32[]{:S(2)}, u32[]{:S(2)}) collective-permute-start(f32[4,128,128]{2,1,0:T(8,128)S(1)} %copy.48), channel_id=1, source_target_pairs={{0,496},{16,0},{32,16},{48,32},{64,48},{80,64},{96,80},{112,96},{1... | collective-permute-start | bytes 786440 | tf_op jit(solution)/shard_map/while/body/eval_jaxpr/ppermute | solution.py:9
  364.2 5.9 %collective-permute-start = (f32[4,128,128]{2,1,0:T(8,128)S(1)}, f32[4,128,128]{2,1,0:T(8,128)S(1)}, u32[]{:S(2)}, u32[]{:S(2)}) collective-permute-start(f32[4,128,128]{2,1,0:T(8,128)S(1)} %copy.48), channel_id=1, source_target_pairs={{0,496},{16,0},{32,16},{48,32},{64,48},{80,64},{96,80},{112,96},{1... | collective-permute-start | bytes 786440 | tf_op jit(solution)/shard_map/while/body/eval_jaxpr/ppermute | solution.py:9
  372.0 1.4 convolution_add_fusion.3
  374.0 5.9 %collective-permute-start = (f32[4,128,128]{2,1,0:T(8,128)S(1)}, f32[4,128,128]{2,1,0:T(8,128)S(1)}, u32[]{:S(2)}, u32[]{:S(2)}) collective-permute-start(f32[4,128,128]{2,1,0:T(8,128)S(1)} %copy.48), channel_id=1, source_target_pairs={{0,496},{16,0},{32,16},{48,32},{64,48},{80,64},{96,80},{112,96},{1... | collective-permute-start | bytes 786440 | tf_op jit(solution)/shard_map/while/body/eval_jaxpr/ppermute | solution.py:9
  383.2 1.7 collective-permute-done
  384.9 5.9 %collective-permute-start = (f32[4,128,128]{2,1,0:T(8,128)S(1)}, f32[4,128,128]{2,1,0:T(8,128)S(1)}, u32[]{:S(2)}, u32[]{:S(2)}) collective-permute-start(f32[4,128,128]{2,1,0:T(8,128)S(1)} %copy.48), channel_id=1, source_target_pairs={{0,496},{16,0},{32,16},{48,32},{64,48},{80,64},{96,80},{112,96},{1... | collective-permute-start | bytes 786440 | tf_op jit(solution)/shard_map/while/body/eval_jaxpr/ppermute | solution.py:9
  394.1 2.8 collective-permute-done
  396.9 6.1 %collective-permute-start = (f32[4,128,128]{2,1,0:T(8,128)S(1)}, f32[4,128,128]{2,1,0:T(8,128)S(1)}, u32[]{:S(2)}, u32[]{:S(2)}) collective-permute-start(f32[4,128,128]{2,1,0:T(8,128)S(1)} %copy.48), channel_id=1, source_target_pairs={{0,496},{16,0},{32,16},{48,32},{64,48},{80,64},{96,80},{112,96},{1... | collective-permute-start | bytes 786440 | tf_op jit(solution)/shard_map/while/body/eval_jaxpr/ppermute | solution.py:9
  406.3 2.0 collective-permute-done
  408.9 2.1 fusion.18
  412.7 7.7 %gather_fusion.2 = f32[128,128,128]{2,1,0:T(8,128)} fusion(f32[128,128,128]{2,1,0:T(8,128)} %constant_dynamic-update-slice_fusion.1, s32[1024]{0:T(1024)S(1)} %pad_clamp_fusion.1), kind=kCustom, calls=%fused_computation.3 | custom fusion | bytes 16777728 | tf_op jit(solution)/shard_map/jit(_take)/gather | solution.py:33
  420.4 85.3 %all-gather.6.cloned.1.call-done = f32[4,2048,128]{2,1,0:T(8,128)} async-done(((f32[4,128,128]{2,1,0:T(8,128)}), f32[4,2048,128]{2,1,0:T(8,128)}) %all-gather.6.cloned.1.call-update) | async-done | bytes 4194320 | tf_op jit(solution)/shard_map/all_gather | solution.py:81
  505.6 6.5 %gather_fusion.1 = f32[32,4,128,128]{3,2,1,0:T(8,128)} fusion(f32[4,16,128,128]{3,2,1,0:T(8,128)} %bitcast.93, s32[1024]{0:T(1024)S(1)} %pad_clamp_fusion.2), kind=kCustom, calls=%fused_computation.2 | custom fusion | bytes 16777344 | tf_op jit(solution)/shard_map/jit(_take)/gather | solution.py:36
  512.2 15.6 %fusion.23 = f32[4,1,128,128]{3,2,1,0:T(8,128)} fusion(f32[4,32,128,128]{3,2,1,0:T(8,128)} %bitcast.92, pred[4,32]{0,1:T(8,128)(4,1)S(1)} %copy.24, f32[32,4,128,128]{3,2,1,0:T(8,128)} %gather_fusion.1, f32[4,32]{0,1:T(8,128)S(1)} %copy.23, pred[32]{0:T(512)(128)(4,1)S(1)} %compare_and_fusion.3, f32[4,128,128]{2,1,0:T(8,128)S(1)} %copy-done, ...), kind=kOutput, calls=%fused_computation.42 | convolution fusion | flops 3227779072 | bytes 17302192 | tf_op jit(solution)/shard_map/rsab,rsbc->rac/dot_general | solution.py:38
  (420 shorter events, 90.5 us)
Async XLA Ops:
  7.2 81.1 %all-gather.4.cloned.1.call-start = ((), (), s32[]{:S(2)}) async-start(), calls=%async_computation | async-start | bytes 4456448 | tf_op jit(solution)/shard_map/all_gather | solution.py:56
  9.8 495.9 %all-gather.6.cloned.1.call-start = ((), (), s32[]{:S(2)}) async-start(), calls=%async_computation.1 | async-start | bytes 4456448 | tf_op jit(solution)/shard_map/all_gather | solution.py:81
  92.6 11.1 %collective-permute-start = (f32[4,128,128]{2,1,0:T(8,128)S(1)}, f32[4,128,128]{2,1,0:T(8,128)S(1)}, u32[]{:S(2)}, u32[]{:S(2)}) collective-permute-start(f32[4,128,128]{2,1,0:T(8,128)S(1)} %copy.48), channel_id=1, source_target_pairs={{0,496},{16,0},{32,16},{48,32},{64,48},{80,64},{96,80},{112,96},{1... | collective-permute-start | bytes 786440 | tf_op jit(solution)/shard_map/while/body/eval_jaxpr/ppermute | solution.py:9
  103.7 10.7 %collective-permute-start = (f32[4,128,128]{2,1,0:T(8,128)S(1)}, f32[4,128,128]{2,1,0:T(8,128)S(1)}, u32[]{:S(2)}, u32[]{:S(2)}) collective-permute-start(f32[4,128,128]{2,1,0:T(8,128)S(1)} %copy.48), channel_id=1, source_target_pairs={{0,496},{16,0},{32,16},{48,32},{64,48},{80,64},{96,80},{112,96},{1... | collective-permute-start | bytes 786440 | tf_op jit(solution)/shard_map/while/body/eval_jaxpr/ppermute | solution.py:9
  114.5 9.8 %collective-permute-start = (f32[4,128,128]{2,1,0:T(8,128)S(1)}, f32[4,128,128]{2,1,0:T(8,128)S(1)}, u32[]{:S(2)}, u32[]{:S(2)}) collective-permute-start(f32[4,128,128]{2,1,0:T(8,128)S(1)} %copy.48), channel_id=1, source_target_pairs={{0,496},{16,0},{32,16},{48,32},{64,48},{80,64},{96,80},{112,96},{1... | collective-permute-start | bytes 786440 | tf_op jit(solution)/shard_map/while/body/eval_jaxpr/ppermute | solution.py:9
  124.3 9.5 %collective-permute-start = (f32[4,128,128]{2,1,0:T(8,128)S(1)}, f32[4,128,128]{2,1,0:T(8,128)S(1)}, u32[]{:S(2)}, u32[]{:S(2)}) collective-permute-start(f32[4,128,128]{2,1,0:T(8,128)S(1)} %copy.48), channel_id=1, source_target_pairs={{0,496},{16,0},{32,16},{48,32},{64,48},{80,64},{96,80},{112,96},{1... | collective-permute-start | bytes 786440 | tf_op jit(solution)/shard_map/while/body/eval_jaxpr/ppermute | solution.py:9
  133.9 9.2 %collective-permute-start = (f32[4,128,128]{2,1,0:T(8,128)S(1)}, f32[4,128,128]{2,1,0:T(8,128)S(1)}, u32[]{:S(2)}, u32[]{:S(2)}) collective-permute-start(f32[4,128,128]{2,1,0:T(8,128)S(1)} %copy.48), channel_id=1, source_target_pairs={{0,496},{16,0},{32,16},{48,32},{64,48},{80,64},{96,80},{112,96},{1... | collective-permute-start | bytes 786440 | tf_op jit(solution)/shard_map/while/body/eval_jaxpr/ppermute | solution.py:9
  143.1 9.2 %collective-permute-start = (f32[4,128,128]{2,1,0:T(8,128)S(1)}, f32[4,128,128]{2,1,0:T(8,128)S(1)}, u32[]{:S(2)}, u32[]{:S(2)}) collective-permute-start(f32[4,128,128]{2,1,0:T(8,128)S(1)} %copy.48), channel_id=1, source_target_pairs={{0,496},{16,0},{32,16},{48,32},{64,48},{80,64},{96,80},{112,96},{1... | collective-permute-start | bytes 786440 | tf_op jit(solution)/shard_map/while/body/eval_jaxpr/ppermute | solution.py:9
  152.4 9.2 %collective-permute-start = (f32[4,128,128]{2,1,0:T(8,128)S(1)}, f32[4,128,128]{2,1,0:T(8,128)S(1)}, u32[]{:S(2)}, u32[]{:S(2)}) collective-permute-start(f32[4,128,128]{2,1,0:T(8,128)S(1)} %copy.48), channel_id=1, source_target_pairs={{0,496},{16,0},{32,16},{48,32},{64,48},{80,64},{96,80},{112,96},{1... | collective-permute-start | bytes 786440 | tf_op jit(solution)/shard_map/while/body/eval_jaxpr/ppermute | solution.py:9
  161.6 9.6 %collective-permute-start = (f32[4,128,128]{2,1,0:T(8,128)S(1)}, f32[4,128,128]{2,1,0:T(8,128)S(1)}, u32[]{:S(2)}, u32[]{:S(2)}) collective-permute-start(f32[4,128,128]{2,1,0:T(8,128)S(1)} %copy.48), channel_id=1, source_target_pairs={{0,496},{16,0},{32,16},{48,32},{64,48},{80,64},{96,80},{112,96},{1... | collective-permute-start | bytes 786440 | tf_op jit(solution)/shard_map/while/body/eval_jaxpr/ppermute | solution.py:9
  171.2 10.7 %collective-permute-start = (f32[4,128,128]{2,1,0:T(8,128)S(1)}, f32[4,128,128]{2,1,0:T(8,128)S(1)}, u32[]{:S(2)}, u32[]{:S(2)}) collective-permute-start(f32[4,128,128]{2,1,0:T(8,128)S(1)} %copy.48), channel_id=1, source_target_pairs={{0,496},{16,0},{32,16},{48,32},{64,48},{80,64},{96,80},{112,96},{1... | collective-permute-start | bytes 786440 | tf_op jit(solution)/shard_map/while/body/eval_jaxpr/ppermute | solution.py:9
  181.9 11.8 %collective-permute-start = (f32[4,128,128]{2,1,0:T(8,128)S(1)}, f32[4,128,128]{2,1,0:T(8,128)S(1)}, u32[]{:S(2)}, u32[]{:S(2)}) collective-permute-start(f32[4,128,128]{2,1,0:T(8,128)S(1)} %copy.48), channel_id=1, source_target_pairs={{0,496},{16,0},{32,16},{48,32},{64,48},{80,64},{96,80},{112,96},{1... | collective-permute-start | bytes 786440 | tf_op jit(solution)/shard_map/while/body/eval_jaxpr/ppermute | solution.py:9
  193.7 11.2 %collective-permute-start = (f32[4,128,128]{2,1,0:T(8,128)S(1)}, f32[4,128,128]{2,1,0:T(8,128)S(1)}, u32[]{:S(2)}, u32[]{:S(2)}) collective-permute-start(f32[4,128,128]{2,1,0:T(8,128)S(1)} %copy.48), channel_id=1, source_target_pairs={{0,496},{16,0},{32,16},{48,32},{64,48},{80,64},{96,80},{112,96},{1... | collective-permute-start | bytes 786440 | tf_op jit(solution)/shard_map/while/body/eval_jaxpr/ppermute | solution.py:9
  205.0 10.6 %collective-permute-start = (f32[4,128,128]{2,1,0:T(8,128)S(1)}, f32[4,128,128]{2,1,0:T(8,128)S(1)}, u32[]{:S(2)}, u32[]{:S(2)}) collective-permute-start(f32[4,128,128]{2,1,0:T(8,128)S(1)} %copy.48), channel_id=1, source_target_pairs={{0,496},{16,0},{32,16},{48,32},{64,48},{80,64},{96,80},{112,96},{1... | collective-permute-start | bytes 786440 | tf_op jit(solution)/shard_map/while/body/eval_jaxpr/ppermute | solution.py:9
  215.6 9.5 %collective-permute-start = (f32[4,128,128]{2,1,0:T(8,128)S(1)}, f32[4,128,128]{2,1,0:T(8,128)S(1)}, u32[]{:S(2)}, u32[]{:S(2)}) collective-permute-start(f32[4,128,128]{2,1,0:T(8,128)S(1)} %copy.48), channel_id=1, source_target_pairs={{0,496},{16,0},{32,16},{48,32},{64,48},{80,64},{96,80},{112,96},{1... | collective-permute-start | bytes 786440 | tf_op jit(solution)/shard_map/while/body/eval_jaxpr/ppermute | solution.py:9
  225.1 9.7 %collective-permute-start = (f32[4,128,128]{2,1,0:T(8,128)S(1)}, f32[4,128,128]{2,1,0:T(8,128)S(1)}, u32[]{:S(2)}, u32[]{:S(2)}) collective-permute-start(f32[4,128,128]{2,1,0:T(8,128)S(1)} %copy.48), channel_id=1, source_target_pairs={{0,496},{16,0},{32,16},{48,32},{64,48},{80,64},{96,80},{112,96},{1... | collective-permute-start | bytes 786440 | tf_op jit(solution)/shard_map/while/body/eval_jaxpr/ppermute | solution.py:9
  234.8 9.2 %collective-permute-start = (f32[4,128,128]{2,1,0:T(8,128)S(1)}, f32[4,128,128]{2,1,0:T(8,128)S(1)}, u32[]{:S(2)}, u32[]{:S(2)}) collective-permute-start(f32[4,128,128]{2,1,0:T(8,128)S(1)} %copy.48), channel_id=1, source_target_pairs={{0,496},{16,0},{32,16},{48,32},{64,48},{80,64},{96,80},{112,96},{1... | collective-permute-start | bytes 786440 | tf_op jit(solution)/shard_map/while/body/eval_jaxpr/ppermute | solution.py:9
  244.1 9.2 %collective-permute-start = (f32[4,128,128]{2,1,0:T(8,128)S(1)}, f32[4,128,128]{2,1,0:T(8,128)S(1)}, u32[]{:S(2)}, u32[]{:S(2)}) collective-permute-start(f32[4,128,128]{2,1,0:T(8,128)S(1)} %copy.48), channel_id=1, source_target_pairs={{0,496},{16,0},{32,16},{48,32},{64,48},{80,64},{96,80},{112,96},{1... | collective-permute-start | bytes 786440 | tf_op jit(solution)/shard_map/while/body/eval_jaxpr/ppermute | solution.py:9
  253.3 9.2 %collective-permute-start = (f32[4,128,128]{2,1,0:T(8,128)S(1)}, f32[4,128,128]{2,1,0:T(8,128)S(1)}, u32[]{:S(2)}, u32[]{:S(2)}) collective-permute-start(f32[4,128,128]{2,1,0:T(8,128)S(1)} %copy.48), channel_id=1, source_target_pairs={{0,496},{16,0},{32,16},{48,32},{64,48},{80,64},{96,80},{112,96},{1... | collective-permute-start | bytes 786440 | tf_op jit(solution)/shard_map/while/body/eval_jaxpr/ppermute | solution.py:9
  262.6 9.8 %collective-permute-start = (f32[4,128,128]{2,1,0:T(8,128)S(1)}, f32[4,128,128]{2,1,0:T(8,128)S(1)}, u32[]{:S(2)}, u32[]{:S(2)}) collective-permute-start(f32[4,128,128]{2,1,0:T(8,128)S(1)} %copy.48), channel_id=1, source_target_pairs={{0,496},{16,0},{32,16},{48,32},{64,48},{80,64},{96,80},{112,96},{1... | collective-permute-start | bytes 786440 | tf_op jit(solution)/shard_map/while/body/eval_jaxpr/ppermute | solution.py:9
  272.3 10.8 %collective-permute-start = (f32[4,128,128]{2,1,0:T(8,128)S(1)}, f32[4,128,128]{2,1,0:T(8,128)S(1)}, u32[]{:S(2)}, u32[]{:S(2)}) collective-permute-start(f32[4,128,128]{2,1,0:T(8,128)S(1)} %copy.48), channel_id=1, source_target_pairs={{0,496},{16,0},{32,16},{48,32},{64,48},{80,64},{96,80},{112,96},{1... | collective-permute-start | bytes 786440 | tf_op jit(solution)/shard_map/while/body/eval_jaxpr/ppermute | solution.py:9
  283.2 12.0 %collective-permute-start = (f32[4,128,128]{2,1,0:T(8,128)S(1)}, f32[4,128,128]{2,1,0:T(8,128)S(1)}, u32[]{:S(2)}, u32[]{:S(2)}) collective-permute-start(f32[4,128,128]{2,1,0:T(8,128)S(1)} %copy.48), channel_id=1, source_target_pairs={{0,496},{16,0},{32,16},{48,32},{64,48},{80,64},{96,80},{112,96},{1... | collective-permute-start | bytes 786440 | tf_op jit(solution)/shard_map/while/body/eval_jaxpr/ppermute | solution.py:9
  295.3 11.4 %collective-permute-start = (f32[4,128,128]{2,1,0:T(8,128)S(1)}, f32[4,128,128]{2,1,0:T(8,128)S(1)}, u32[]{:S(2)}, u32[]{:S(2)}) collective-permute-start(f32[4,128,128]{2,1,0:T(8,128)S(1)} %copy.48), channel_id=1, source_target_pairs={{0,496},{16,0},{32,16},{48,32},{64,48},{80,64},{96,80},{112,96},{1... | collective-permute-start | bytes 786440 | tf_op jit(solution)/shard_map/while/body/eval_jaxpr/ppermute | solution.py:9
  306.7 10.6 %collective-permute-start = (f32[4,128,128]{2,1,0:T(8,128)S(1)}, f32[4,128,128]{2,1,0:T(8,128)S(1)}, u32[]{:S(2)}, u32[]{:S(2)}) collective-permute-start(f32[4,128,128]{2,1,0:T(8,128)S(1)} %copy.48), channel_id=1, source_target_pairs={{0,496},{16,0},{32,16},{48,32},{64,48},{80,64},{96,80},{112,96},{1... | collective-permute-start | bytes 786440 | tf_op jit(solution)/shard_map/while/body/eval_jaxpr/ppermute | solution.py:9
  317.3 9.5 %collective-permute-start = (f32[4,128,128]{2,1,0:T(8,128)S(1)}, f32[4,128,128]{2,1,0:T(8,128)S(1)}, u32[]{:S(2)}, u32[]{:S(2)}) collective-permute-start(f32[4,128,128]{2,1,0:T(8,128)S(1)} %copy.48), channel_id=1, source_target_pairs={{0,496},{16,0},{32,16},{48,32},{64,48},{80,64},{96,80},{112,96},{1... | collective-permute-start | bytes 786440 | tf_op jit(solution)/shard_map/while/body/eval_jaxpr/ppermute | solution.py:9
  326.8 9.7 %collective-permute-start = (f32[4,128,128]{2,1,0:T(8,128)S(1)}, f32[4,128,128]{2,1,0:T(8,128)S(1)}, u32[]{:S(2)}, u32[]{:S(2)}) collective-permute-start(f32[4,128,128]{2,1,0:T(8,128)S(1)} %copy.48), channel_id=1, source_target_pairs={{0,496},{16,0},{32,16},{48,32},{64,48},{80,64},{96,80},{112,96},{1... | collective-permute-start | bytes 786440 | tf_op jit(solution)/shard_map/while/body/eval_jaxpr/ppermute | solution.py:9
  336.5 9.2 %collective-permute-start = (f32[4,128,128]{2,1,0:T(8,128)S(1)}, f32[4,128,128]{2,1,0:T(8,128)S(1)}, u32[]{:S(2)}, u32[]{:S(2)}) collective-permute-start(f32[4,128,128]{2,1,0:T(8,128)S(1)} %copy.48), channel_id=1, source_target_pairs={{0,496},{16,0},{32,16},{48,32},{64,48},{80,64},{96,80},{112,96},{1... | collective-permute-start | bytes 786440 | tf_op jit(solution)/shard_map/while/body/eval_jaxpr/ppermute | solution.py:9
  345.7 9.2 %collective-permute-start = (f32[4,128,128]{2,1,0:T(8,128)S(1)}, f32[4,128,128]{2,1,0:T(8,128)S(1)}, u32[]{:S(2)}, u32[]{:S(2)}) collective-permute-start(f32[4,128,128]{2,1,0:T(8,128)S(1)} %copy.48), channel_id=1, source_target_pairs={{0,496},{16,0},{32,16},{48,32},{64,48},{80,64},{96,80},{112,96},{1... | collective-permute-start | bytes 786440 | tf_op jit(solution)/shard_map/while/body/eval_jaxpr/ppermute | solution.py:9
  355.0 9.2 %collective-permute-start = (f32[4,128,128]{2,1,0:T(8,128)S(1)}, f32[4,128,128]{2,1,0:T(8,128)S(1)}, u32[]{:S(2)}, u32[]{:S(2)}) collective-permute-start(f32[4,128,128]{2,1,0:T(8,128)S(1)} %copy.48), channel_id=1, source_target_pairs={{0,496},{16,0},{32,16},{48,32},{64,48},{80,64},{96,80},{112,96},{1... | collective-permute-start | bytes 786440 | tf_op jit(solution)/shard_map/while/body/eval_jaxpr/ppermute | solution.py:9
  364.2 9.8 %collective-permute-start = (f32[4,128,128]{2,1,0:T(8,128)S(1)}, f32[4,128,128]{2,1,0:T(8,128)S(1)}, u32[]{:S(2)}, u32[]{:S(2)}) collective-permute-start(f32[4,128,128]{2,1,0:T(8,128)S(1)} %copy.48), channel_id=1, source_target_pairs={{0,496},{16,0},{32,16},{48,32},{64,48},{80,64},{96,80},{112,96},{1... | collective-permute-start | bytes 786440 | tf_op jit(solution)/shard_map/while/body/eval_jaxpr/ppermute | solution.py:9
  374.0 10.8 %collective-permute-start = (f32[4,128,128]{2,1,0:T(8,128)S(1)}, f32[4,128,128]{2,1,0:T(8,128)S(1)}, u32[]{:S(2)}, u32[]{:S(2)}) collective-permute-start(f32[4,128,128]{2,1,0:T(8,128)S(1)} %copy.48), channel_id=1, source_target_pairs={{0,496},{16,0},{32,16},{48,32},{64,48},{80,64},{96,80},{112,96},{1... | collective-permute-start | bytes 786440 | tf_op jit(solution)/shard_map/while/body/eval_jaxpr/ppermute | solution.py:9
  384.9 12.0 %collective-permute-start = (f32[4,128,128]{2,1,0:T(8,128)S(1)}, f32[4,128,128]{2,1,0:T(8,128)S(1)}, u32[]{:S(2)}, u32[]{:S(2)}) collective-permute-start(f32[4,128,128]{2,1,0:T(8,128)S(1)} %copy.48), channel_id=1, source_target_pairs={{0,496},{16,0},{32,16},{48,32},{64,48},{80,64},{96,80},{112,96},{1... | collective-permute-start | bytes 786440 | tf_op jit(solution)/shard_map/while/body/eval_jaxpr/ppermute | solution.py:9
  396.9 11.4 %collective-permute-start = (f32[4,128,128]{2,1,0:T(8,128)S(1)}, f32[4,128,128]{2,1,0:T(8,128)S(1)}, u32[]{:S(2)}, u32[]{:S(2)}) collective-permute-start(f32[4,128,128]{2,1,0:T(8,128)S(1)} %copy.48), channel_id=1, source_target_pairs={{0,496},{16,0},{32,16},{48,32},{64,48},{80,64},{96,80},{112,96},{1... | collective-permute-start | bytes 786440 | tf_op jit(solution)/shard_map/while/body/eval_jaxpr/ppermute | solution.py:9
  505.6 6.5 %copy-start = (f32[4,128,128]{2,1,0:T(8,128)S(1)}, f32[4,128,128]{2,1,0:T(8,128)}, u32[]{:S(2)}) copy-start(f32[4,128,128]{2,1,0:T(8,128)} %fusion.18) | copy-start | bytes 786436
Sparse Core Ops, SparseCore 0:
  11.9 76.3 all-gather.3
  411.2 94.4 all-gather.5
where the time goes:
time: 537 us; the launch traced here: 535 us
  starting transfers between devices  187 us (35%)
  waiting for transfers between devices  187 us (35%)
  local copies, waits for them, and re-layouts  65.6 us (12%)
  matrix products  62.4 us (12%)
  other arithmetic  14.7 us (3%)
  between operations  14.2 us (3%)
    ppermute x31, starting transfers between devices, shifted(): lax.ppermute(shard, axis, [(i, (i + by) % length) for i in range(length)])  187 us
    all_gather x1, waiting for transfers between devices, body(): second_panel = lax.all_gather(squared, 'col', axis=1, tiled=True)  85.3 us
    all_gather x1, waiting for transfers between devices, body(): first_panel = lax.all_gather(masked, 'col', axis=1, tiled=True)  74.7 us
    dot_general x33, matrix products, pair_terms(): jnp.einsum('rsab,rsbc->rac', scaled, chosen_right, precision=lax.Precisio...  62.4 us
    ppermute x31, waiting for transfers between devices, shifted(): lax.ppermute(shard, axis, [(i, (i + by) % length) for i in range(length)])  27.1 us
    gather x33, local copies, waits for them, and re-layouts, pair_terms(): jnp.take(incoming, chosen_index.reshape(-1), axis=0)  25.8 us
    dynamic_update_slice x31, local copies, waits for them, and re-layouts, advance(): stored = lax.dynamic_update_slice_in_dim(stored, incoming, first_row, 0)  22.6 us
  transfers between devices with their start and end apart: 33, of which 19 were waited for; matrix products, arithmetic and copies ran while one was open for 21% of the time, Pallas kernels for 0%

commit v1 on v0

v1 whole, which is shorter than its diff:
```python
import functools

import jax
import jax.numpy as jnp
from jax import lax
from jax.experimental import pallas as pl
from jax.experimental.pallas import tpu as pltpu
from jax.sharding import PartitionSpec as P

F32 = jnp.float32
I32 = jnp.int32
VMEM = pl.BlockSpec(memory_space=pltpu.VMEM)
SMEM = pl.BlockSpec(memory_space=pltpu.SMEM)
PARAMS = pltpu.CompilerParams(vmem_limit_bytes=48 << 20)
SIZES = (8, 10, 12, 14, 18, 64)


def iota(shape, dim):
    return lax.broadcasted_iota(I32, shape, dim)


def eq(a, b):
    return (a == b).astype(F32)


def dot(a, b):
    return jnp.dot(a, b, preferred_element_type=F32)


def plan_kernel(rows, row_devs, groups, width, here, cols_ref, colst_ref, right_ref, left_ref, code_ref, info_ref):
    me, g_me = here[0], here[1]
    local = rows // row_devs
    cand = local * groups
    slots = cand
    cols = cols_ref[...]
    colst = colst_ref[...]
    s_j = eq(iota((rows, groups), 0) // width, iota((rows, groups), 1))
    j_s = eq(iota((groups, rows), 1) // width, iota((groups, rows), 0))
    mine_row = jnp.sum(jnp.where(iota((groups, rows), 0) == g_me, colst, 0.0), axis=0, keepdims=True)
    mine_col = jnp.sum(jnp.where(iota((rows, groups), 1) == g_me, cols, 0.0), axis=1, keepdims=True)
    by_source = dot(s_j, colst)
    term = (
        (by_source == (iota((rows, rows), 0) % width).astype(F32))
        & (mine_col == mine_row)
        & (mine_row >= 0)
    ).astype(F32)
    term = dot(j_s, term)
    source = iota((groups, rows), 0).astype(F32) * width + colst
    source = source.astype(I32)
    away = jnp.where((source // local) != (iota((groups, rows), 1) // local), term, 0.0)
    before = (iota((groups, groups), 1) < iota((groups, groups), 0)).astype(F32)
    count = jnp.sum(away, axis=0, keepdims=True)
    r0, r1 = iota((rows, rows), 0), iota((rows, rows), 1)
    earlier = ((r0 // local == r1 // local) & (r0 < r1)).astype(F32)
    rank = dot(before, away) + dot(jnp.broadcast_to(count, (8, rows)), earlier)[:1]
    rank = jnp.where(away > 0, rank, -1.0)
    slot = iota((slots, rows), 0).astype(F32)
    source_f = source.astype(F32)
    found = jnp.zeros((slots, rows), F32)
    for j in range(groups):
        found = found + jnp.where(rank[j : j + 1] == slot, source_f[j : j + 1], 0.0)
    fold = eq(iota((rows, row_devs), 0) // local, iota((rows, row_devs), 1))
    right_ref[...] = dot(found, fold).astype(I32)
    c0 = iota((cand, rows), 0)
    row_val = dot(eq(iota((cand, rows), 1), me * local + c0 // groups), cols)
    c1 = iota((cand, groups), 0)
    g1 = iota((cand, groups), 1)
    own = jnp.sum(jnp.where(g1 == c1 % groups, row_val, 0.0), axis=1, keepdims=True)
    q_1 = iota((cand, 1), 0) // groups
    j_1 = iota((cand, 1), 0) % groups
    s_1 = j_1 * width + own.astype(I32)
    s_val = dot(eq(iota((cand, rows), 1), s_1), cols)
    terms = ((own >= 0) & (row_val >= 0) & (s_val == row_val)).astype(F32)
    lefts = jnp.where(c1 % groups != g1, terms, 0.0)
    lower = (iota((cand, cand), 1) < iota((cand, cand), 0)).astype(F32)
    rank_l = dot(lower, lefts)
    marked = jnp.where(lefts > 0, rank_l, -1.0)
    piece = j_1 * local + q_1
    piece_f = piece.astype(F32)
    slot_g = iota((slots, groups), 0).astype(F32)
    got = jnp.zeros((slots, groups), F32)
    for k in range(cand):
        got = got + jnp.where(marked[k : k + 1] == slot_g, float((k % groups) * local + k // groups), 0.0)
    left_ref[...] = got.astype(I32)
    pick = g1 == g_me
    mine = jnp.sum(jnp.where(pick, terms, 0.0), axis=1, keepdims=True)
    l_rank = jnp.sum(jnp.where(pick, rank_l, 0.0), axis=1, keepdims=True)
    is_away = (s_1 // local != me).astype(F32)
    wide = iota((cand, 128), 1)
    both = jnp.where(wide == 0, mine, jnp.where(wide == 1, mine * is_away, 0.0))
    ranks = dot(lower, both)
    order = jnp.sum(jnp.where(wide == 0, ranks, 0.0), axis=1, keepdims=True)
    r_rank = jnp.sum(jnp.where(wide == 1, ranks, 0.0), axis=1, keepdims=True)
    l_at = jnp.where(j_1 == g_me, slots + q_1, l_rank.astype(I32))
    r_at = jnp.where(is_away > 0, r_rank.astype(I32), slots + s_1 % local)
    code = (q_1 + 4 * piece + 256 * l_at + 32768 * r_at).astype(F32)
    hot = (mine > 0) & (order == wide.astype(F32))
    code_ref[...] = jnp.sum(jnp.where(hot, code, 0.0), axis=0, keepdims=True).astype(I32)
    values = rows // groups
    copy = eq(iota((groups, rows), 1) % groups, iota((groups, rows), 0))
    has = eq(dot(cols, copy), (iota((rows, rows), 1) // groups).astype(F32))
    filled = eq(dot(cols, j_s), (r1 % width).astype(F32))
    far = jnp.where(r0 // local != r1 // local, filled, 0.0)
    group_of = eq(iota((row_devs, rows), 1) // local, iota((row_devs, rows), 0))
    back = eq(iota((rows, groups), 0) % groups, iota((rows, groups), 1))
    need_r = dot(dot(group_of, dot(far, has) * has), back)
    need_l = dot(dot(group_of, (dot(filled, has) - 1.0) * has), back)
    most = jnp.max(jnp.maximum(need_r, need_l), axis=(0, 1), keepdims=True)
    number = jnp.sum(mine, axis=(0, 1), keepdims=True)
    info_ref[...] = jnp.where(iota((1, 128), 1) == 0, number, most).astype(I32)


def pack_kernel(size, table, pieces, out):
    def one(d, _):
        for slot in range(size):
            out[d, slot] = pieces[table[slot, d]]
        return 0

    lax.fori_loop(0, out.shape[0], one, 0)


def halves(block):
    high = block.astype(jnp.bfloat16)
    return high, (block - high.astype(F32)).astype(jnp.bfloat16)


def product(left, right):
    lh, ll = halves(left)
    rh, rl = halves(right)
    return dot(lh, rh) + (dot(lh, rl) + dot(ll, rh))


def square_kernel(size, code, info, x, panel, came, squared, spread, rights):
    rows = came.shape[2]

    def unpack(c, _):
        for h in range(came.shape[0]):
            rights[c, h * rows : (h + 1) * rows, :] = came[h, c]
        return 0

    lax.fori_loop(0, size, unpack, 0)
    local = x.shape[0]
    rights[size : size + local] = x[...]
    squared[...] = jnp.zeros_like(squared)

    def one(t, _):
        word = code[0, t]
        q, piece, r_at = word % 4, (word // 4) % 64, word // 32768
        r_at = jnp.where(r_at >= 64, r_at - 64 + size, r_at)
        squared[q] += product(panel[piece], rights[r_at])
        return 0

    lax.fori_loop(0, info[0, 0], one, 0)
    tall = spread.shape[2]
    for k in range(spread.shape[0]):
        spread[k] = squared[:, k * tall : (k + 1) * tall, :]


def cube_kernel(size, code, info, squared, came, rights, purified, lefts):
    rows = came.shape[2]
    local = squared.shape[0]

    def unpack(c, _):
        for h in range(came.shape[0]):
            lefts[c, h * rows : (h + 1) * rows, :] = came[h, c]
        return 0

    lax.fori_loop(0, size, unpack, 0)
    lefts[size : size + local] = squared[...]
    purified[...] = 3.0 * squared[...]

    def one(t, _):
        word = code[0, t]
        q, l_at, r_at = word % 4, (word // 256) % 128, word // 32768
        l_at = jnp.where(l_at >= 64, l_at - 64 + size, l_at)
        r_at = jnp.where(r_at >= 64, r_at - 64 + size, r_at)
        purified[q] += -2.0 * product(lefts[l_at], rights[r_at])
        return 0

    lax.fori_loop(0, info[0, 0], one, 0)


def shape(*dims, dtype=F32):
    return jax.ShapeDtypeStruct(dims, dtype)


def branch(size, x, right, left, code, info):
    local, order, _ = x.shape
    row_devs = lax.axis_size("row")
    groups = lax.axis_size("col")
    fine, tall = order // row_devs, order // groups
    panel = lax.all_gather(x, "col", axis=0, tiled=True)
    spread = x.reshape(local, row_devs, fine, order).transpose(1, 0, 2, 3)
    held = lax.all_to_all(spread, "row", 0, 0, tiled=True)
    held = held.reshape(row_devs * local, fine, order)
    out = pl.pallas_call(
        functools.partial(pack_kernel, size),
        out_shape=shape(row_devs, size, fine, order),
        in_specs=[SMEM, VMEM],
        out_specs=VMEM,
        compiler_params=PARAMS,
        name="pack_right",
    )(right, held)
    came = lax.all_to_all(out, "row", 0, 0, tiled=True)
    squared, spread, rights = pl.pallas_call(
        functools.partial(square_kernel, size),
        out_shape=(
            shape(local, order, order),
            shape(groups, local, tall, order),
            shape(size + local, order, order),
        ),
        in_specs=[SMEM, SMEM, VMEM, VMEM, VMEM],
        out_specs=(VMEM, VMEM, VMEM),
        compiler_params=PARAMS,
        name="square",
    )(code, info, x, panel, came)
    held = lax.all_to_all(spread, "col", 0, 0, tiled=True)
    held = held.reshape(groups * local, tall, order)
    out = pl.pallas_call(
        functools.partial(pack_kernel, size),
        out_shape=shape(groups, size, tall, order),
        in_specs=[SMEM, VMEM],
        out_specs=VMEM,
        compiler_params=PARAMS,
        name="pack_left",
    )(left, held)
    came = lax.all_to_all(out, "col", 0, 0, tiled=True)
    purified = pl.pallas_call(
        functools.partial(cube_kernel, size),
        out_shape=shape(local, order, order),
        in_specs=[SMEM, SMEM, VMEM, VMEM, VMEM],
        out_specs=VMEM,
        scratch_shapes=[pltpu.VMEM((size + local, order, order), F32)],
        compiler_params=PARAMS,
        name="cube",
    )(code, info, squared, came, rights)
    return squared, purified


def body(density, columns):
    row_devs = lax.axis_size("row")
    rows, groups = columns.shape
    width = rows // groups
    local = density.shape[0]
    cand = local * groups
    here = jnp.stack([lax.axis_index("row"), lax.axis_index("col")]).astype(I32)
    cols = columns.astype(F32)
    right, left, code, info = pl.pallas_call(
        functools.partial(plan_kernel, rows, row_devs, groups, width),
        out_shape=(
            shape(cand, row_devs, dtype=I32),
            shape(cand, groups, dtype=I32),
            shape(1, 128, dtype=I32),
            shape(1, 128, dtype=I32),
        ),
        in_specs=[SMEM, VMEM, VMEM],
        out_specs=(VMEM, VMEM, VMEM, VMEM),
        compiler_params=PARAMS,
        name="plan",
    )(here, cols, cols.T)
    most = info[0, 1]
    which = sum((most > size).astype(I32) for size in SIZES[:-1])
    x = density[:, 0]
    squared, purified = lax.switch(
        which, [functools.partial(branch, size) for size in SIZES], x, right, left, code, info
    )
    return squared[:, None], purified[:, None]


def solution(mesh):
    return jax.shard_map(
        body,
        mesh=mesh,
        in_specs=(P("row", "col", None, None), P()),
        out_specs=(P("row", "col", None, None), P("row", "col", None, None)),
        check_vma=False,
    )
```

time: 537 us -> 145 us (0.27)
  starting transfers between devices: 187 us -> 0.04 us
  waiting for transfers between devices: 187 us -> 4.61 us
  blocking collectives: 0 us -> 107 us
  matrix products: 62.4 us -> 0 us
  local copies, waits for them, and re-layouts: 65.6 us -> 4.57 us
  other arithmetic: 14.7 us -> 0.77 us
  Pallas kernels: 0 us -> 9.82 us
    ppermute x31 -> x0, starting transfers between devices: 187 us -> none  [shifted(): lax.ppermute(shard, axis, [(i, (i + by) % length) for i in range(length)])]
    all_gather x2 -> x1, waiting for transfers between devices: 160 us -> 3.93 us  [branch(): panel = lax.all_gather(x, 'col', axis=0, tiled=True)]
    all_to_all x0 -> x4, blocking collectives: none -> 107 us  [the longest x1 40.3 us: branch(): came = lax.all_to_all(out, 'row', 0, 0, tiled=True)]
    dot_general x33 -> x0, matrix products: 62.4 us -> none  [pair_terms(): jnp.einsum('rsab,rsbc->rac', scaled, chosen_right, precision=lax.Precisio...]
    gather x34 -> x0, local copies, waits for them, and re-layouts: 32.3 us -> none  [the longest x33 25.8 us: pair_terms(): jnp.take(incoming, chosen_index.reshape(-1), axis=0)]
    ppermute x31 -> x0, waiting for transfers between devices: 27.1 us -> none  [shifted(): lax.ppermute(shard, axis, [(i, (i + by) % length) for i in range(length)])]
    dynamic_update_slice x32 -> x0, local copies, waits for them, and re-layouts: 23.3 us -> none  [the longest x31 22.6 us: advance(): stored = lax.dynamic_update_slice_in_dim(stored, incoming, first_row, 0)]
    reduce_sum x66 -> x0, other arithmetic: 9.91 us -> none  [the longest x33 6.11 us: pair_terms(): jnp.sum(right_cols[None, None, :] * lookup.astype(jnp.int32), axis=2)]
  transfers between devices with their start and end apart: 33 -> 1, of which waited for: 19 -> 1; matrix products, arithmetic and copies ran while one was open for 21% -> 1% of each run, Pallas kernels for 0% -> 1%
where the time goes in v1:
time: 145 us
  blocking collectives  107 us (74%)
  between operations  17.3 us (12%)
  Pallas kernels  9.82 us (7%)
  waiting for transfers between devices  4.61 us (3%)
  local copies, waits for them, and re-layouts  4.57 us (3%)
    all_to_all x1, blocking collectives, branch(): came = lax.all_to_all(out, 'row', 0, 0, tiled=True)  40.3 us
    all_to_all x1, blocking collectives, branch(): held = lax.all_to_all(spread, 'row', 0, 0, tiled=True)  36.8 us
    all_to_all x1, blocking collectives, branch(): came = lax.all_to_all(out, 'col', 0, 0, tiled=True)  16.7 us
    all_to_all x1, blocking collectives, branch(): held = lax.all_to_all(spread, 'col', 0, 0, tiled=True)  13.7 us
    all_gather x1, waiting for transfers between devices, branch(): panel = lax.all_gather(x, 'col', axis=0, tiled=True)  3.93 us
  transfers between devices with their start and end apart: 1, of which 1 were waited for; matrix products, arithmetic and copies ran while one was open for 1% of the time, Pallas kernels for 1%

profile of v1, /device:TPU:1, one launch (start us, length us, event | category | flops | bytes accessed | tf_op | source)
XLA Modules:
  0.0 144.6 jit_solution(11782692569045790167)
XLA Ops:
  7.2 0.1 pad_add_fusion.here
  7.2 0.7 convert_bitcast_fusion
  7.9 0.1 copy.18.cols_ref
  8.0 2.1 %plan.1 = (s32[64,32]{1,0:T(8,128)S(1)}, s32[64,16]{1,0:T(8,128)S(1)}, s32[1,128]{1,0:T(1,128)S(1)}, s32[1,128]{1,0:T(1,128)S(1)}) custom-call(s32[2]{0:T(128)S(1)} %pad_add_fusion.here, f32[128,16]{1,0:T(8,128)S(1)} %copy.18.cols_ref, f32[16,128]{1,0:T(8,128)S(1)} %get-tuple-element.146.colst_ref), custom_call_target="tpu_custom_call" | custom-call | tf_op jit(solution)/shard_map/plan/pallas_call | solution.py:248
  10.2 0.6 slice.3
  14.0 123.1 %conditional.1 = (f32[4,128,128]{2,1,0:T(8,128)}, f32[4,1,128,128]{3,2,1,0:T(8,128)S(1)}) conditional(s32[]{:T(128)} %bitcast.45, (f32[4,128,128]{2,1,0:T(8,128)}, f32[4,1,128,128]{3,2,1,0:T(8,128)}, s32[64,32]{1,0:T(8,128)S(1)}, s32[1,128]{1,0:T(1,128)S(1)}, s32[1,128]{1,0:T(1,128)S(1)}, ...), branch_computations={%region_0.0_spmd, %region_1.0_spmd, %region_2.0_spmd, %region_3.0_... | conditional | bytes 70516912 | solution.py:264
  14.0 0.0 all-gather.9.cloned.1.call-start
  14.1 0.7 all-gather.9.cloned.1.call-update
  14.7 1.0 copy.33
  15.7 36.8 %all_to_all.100 = f32[32,4,4,128]{3,2,1,0:T(4,128)S(1)} all-to-all(f32[32,4,4,128]{3,2,1,0:T(4,128)S(1)} %bitcast.98), channel_id=1, replica_groups=mesh['row'=32,'col'=16] {'row'}, dimensions={0} | all-to-all | bytes 524288 | tf_op jit(solution)/shard_map/cond/branch_1_fun/all_to_all | solution.py:194
  52.5 1.6 %pack_right.7 = f32[32,10,4,128]{3,2,1,0:T(4,128)S(1)} custom-call(s32[64,32]{1,0:T(8,128)S(1)} %get-tuple-element.85.table, f32[128,4,128]{2,1,0:T(4,128)S(1)} %bitcast.67), custom_call_target="tpu_custom_call" | custom-call | tf_op jit(solution)/shard_map/cond/branch_1_fun/pack_right/pallas_call | solution.py:196
  54.1 40.3 %all_to_all.101.came = f32[32,10,4,128]{3,2,1,0:T(4,128)S(1)} all-to-all(f32[32,10,4,128]{3,2,1,0:T(4,128)S(1)} %pack_right.7), channel_id=1, replica_groups=mesh['row'=32,'col'=16] {'row'}, dimensions={0} | all-to-all | bytes 1310720 | tf_op jit(solution)/shard_map/cond/branch_1_fun/all_to_all | solution.py:204
  94.4 3.9 %all-gather.9.cloned.1.call-done.panel = f32[64,128,128]{2,1,0:T(8,128)} async-done(((f32[4,128,128]{2,1,0:T(8,128)}), f32[64,128,128]{2,1,0:T(8,128)}) %all-gather.9.cloned.1.call-update) | async-done | bytes 4194320 | tf_op jit(solution)/shard_map/cond/branch_1_fun/all_gather | solution.py:192
  98.3 0.0 copy-start.2
  98.3 2.2 %copy-done.2 = f32[64,128,128]{2,1,0:T(8,128)S(1)} copy-done((f32[64,128,128]{2,1,0:T(8,128)S(1)}, f32[64,128,128]{2,1,0:T(8,128)}, u32[]{:S(2)}) %copy-start.2) | copy-done | bytes 4194328 | tf_op jit(solution)/shard_map/cond
  100.5 2.8 %square.7 = (f32[4,128,128]{2,1,0:T(8,128)}, f32[16,4,8,128]{3,2,1,0:T(8,128)S(1)}, f32[14,128,128]{2,1,0:T(8,128)S(1)}) custom-call(s32[1,128]{1,0:T(1,128)S(1)} %get-tuple-element.82.code, s32[1,128]{1,0:T(1,128)S(1)} %get-tuple-element.83.info, f32[4,128,128]{2,1,0:T(8,128)} %bitcast.84, f32[64,128,128]{2,1,0:T(8,128)S(1)} %copy-done.2, ...), custom_call_target="tpu_custom_call" | custom-call | tf_op jit(solution)/shard_map/cond/branch_1_fun/square/pallas_call | solution.py:205
  103.3 13.7 %all_to_all.102 = f32[16,4,8,128]{3,2,1,0:T(8,128)S(1)} all-to-all(f32[16,4,8,128]{3,2,1,0:T(8,128)S(1)} %get-tuple-element.89), channel_id=1, replica_groups=mesh['row'=32,'col'=16] {'col'}, dimensions={0} | all-to-all | bytes 524288 | tf_op jit(solution)/shard_map/cond/branch_1_fun/all_to_all | solution.py:217
  117.0 1.3 pack_left.7
  118.3 16.7 %all_to_all.103.came = f32[16,10,8,128]{3,2,1,0:T(8,128)S(1)} all-to-all(f32[16,10,8,128]{3,2,1,0:T(8,128)S(1)} %pack_left.7), channel_id=1, replica_groups=mesh['row'=32,'col'=16] {'col'}, dimensions={0} | all-to-all | bytes 1310720 | tf_op jit(solution)/shard_map/cond/branch_1_fun/all_to_all | solution.py:227
  135.1 2.0 %cube.7 = f32[4,128,128]{2,1,0:T(8,128)S(1)} custom-call(s32[1,128]{1,0:T(1,128)S(1)} %get-tuple-element.82.code, s32[1,128]{1,0:T(1,128)S(1)} %get-tuple-element.83.info, f32[4,128,128]{2,1,0:T(8,128)} %get-tuple-element.150.squared, f32[16,10,8,128]{3,2,1,0:T(8,128)S(1)} %all_to_all.103.came, f32[14,128,128]{2,1,0:T(8,128)S(1)} %get-tuple-element.90.rights), custom_call_target="tpu_custom_call" | custom-call | tf_op jit(solution)/shard_map/cond/branch_1_fun/cube/pallas_call | solution.py:228
  137.1 0.0 copy-start.7
  137.1 0.7 copy-done.7
Async XLA Ops:
  14.0 84.3 %all-gather.9.cloned.1.call-start = ((), (), s32[]{:S(2)}) async-start(), calls=%async_computation.25 | async-start | bytes 4456448 | tf_op jit(solution)/shard_map/cond/branch_1_fun/all_gather | solution.py:192
  98.3 2.2 %copy-start.2 = (f32[64,128,128]{2,1,0:T(8,128)S(1)}, f32[64,128,128]{2,1,0:T(8,128)}, u32[]{:S(2)}) copy-start(f32[64,128,128]{2,1,0:T(8,128)} %all-gather.9.cloned.1.call-done.panel) | copy-start | bytes 12582916 | tf_op jit(solution)/shard_map/cond
  137.1 0.7 copy-start.7
Sparse Core Ops, SparseCore 0:
  18.2 80.0 all-gather.8

commit v2 on v1

--- a/solution.py
+++ b/solution.py
@@ -10,9 +10,11 @@
 F32 = jnp.float32
 I32 = jnp.int32
 VMEM = pl.BlockSpec(memory_space=pltpu.VMEM)
+HBM = pl.BlockSpec(memory_space=pltpu.HBM)
 SMEM = pl.BlockSpec(memory_space=pltpu.SMEM)
-PARAMS = pltpu.CompilerParams(vmem_limit_bytes=48 << 20)
-SIZES = (8, 10, 12, 14, 18, 64)
+WIDE = pltpu.CompilerParams(vmem_limit_bytes=57 << 20)
+PARAMS = pltpu.CompilerParams(vmem_limit_bytes=24 << 20)
+SIZES = (6, 7, 8, 9, 10, 11, 12, 13, 14, 16, 20, 64)
 
 
 def iota(shape, dim):
@@ -105,9 +107,14 @@
     back = eq(iota((rows, groups), 0) % groups, iota((rows, groups), 1))
     need_r = dot(dot(group_of, dot(far, has) * has), back)
     need_l = dot(dot(group_of, (dot(filled, has) - 1.0) * has), back)
-    most = jnp.max(jnp.maximum(need_r, need_l), axis=(0, 1), keepdims=True)
     number = jnp.sum(mine, axis=(0, 1), keepdims=True)
-    info_ref[...] = jnp.where(iota((1, 128), 1) == 0, number, most).astype(I32)
+    place = iota((1, 128), 1)
+    info = jnp.where(place == 0, number, 0.0)
+    for at, need in ((1, need_r), (2, need_l)):
+        most = jnp.max(need, axis=(0, 1), keepdims=True)
+        which = sum((most > size).astype(F32) for size in SIZES[:-1])
+        info = info + jnp.where(place == at, which, 0.0)
+    info_ref[...] = info.astype(I32)
 
 
 def pack_kernel(size, table, pieces, out):
@@ -130,119 +137,162 @@
     return dot(lh, rh) + (dot(lh, rl) + dot(ll, rh))
 
 
-def square_kernel(size, code, info, x, panel, came, squared, spread, rights):
-    rows = came.shape[2]
-
-    def unpack(c, _):
+def unpack(size, came, blocks):
+    tall = came.shape[2]
+
+    def one(slot, _):
         for h in range(came.shape[0]):
-            rights[c, h * rows : (h + 1) * rows, :] = came[h, c]
-        return 0
-
-    lax.fori_loop(0, size, unpack, 0)
+            blocks[slot, h * tall : (h + 1) * tall, :] = came[h, slot]
+        return 0
+
+    lax.fori_loop(0, size, one, 0)
+
+
+def unpack_kernel(size, came, blocks, buffer, sems):
+    def out(slot):
+        return pltpu.make_async_copy(buffer.at[slot], blocks.at[slot], sems.at[slot])
+
+    unpack(size, came, buffer)
+
+    def begin(slot, _):
+        out(slot).start()
+        return 0
+
+    def end(slot, _):
+        out(slot).wait()
+        return 0
+
+    lax.fori_loop(0, size, begin, 0)
+    lax.fori_loop(0, size, end, 0)
+
+
+def fetch_rights(code, many, x, rights, buffer, sems):
     local = x.shape[0]
-    rights[size : size + local] = x[...]
+    far = rights.shape[0]
+
+    def begin(t, _):
+        r_at = code[0, t] // 32768
+
+        @pl.when(r_at < far)
+        def _():
+            pltpu.make_async_copy(rights.at[jnp.minimum(r_at, far - 1)], buffer.at[t], sems.at[t]).start()
+
+        @pl.when(r_at >= far)
+        def _():
+            pltpu.make_async_copy(x.at[jnp.clip(r_at - far, 0, local - 1)], buffer.at[t], sems.at[t]).start()
+
+        return 0
+
+    lax.fori_loop(0, many, begin, 0)
+
+
+def square_kernel(code, info, x, panel, rights, squared, spread, lefts, buffer, left_sems, right_sems):
+    many = info[0, 0]
+
+    def fetch(t):
+        return pltpu.make_async_copy(panel.at[(code[0, t] // 4) % 64], lefts.at[t], left_sems.at[t])
+
+    def begin(t, _):
+        fetch(t).start()
+        return 0
+
+    lax.fori_loop(0, many, begin, 0)
+    fetch_rights(code, many, x, rights, buffer, right_sems)
     squared[...] = jnp.zeros_like(squared)
 
     def one(t, _):
-        word = code[0, t]
-        q, piece, r_at = word % 4, (word // 4) % 64, word // 32768
-        r_at = jnp.where(r_at >= 64, r_at - 64 + size, r_at)
-        squared[q] += product(panel[piece], rights[r_at])
-        return 0
-
-    lax.fori_loop(0, info[0, 0], one, 0)
+        fetch(t).wait()
+        pltpu.make_async_copy(rights.at[0], buffer.at[t], right_sems.at[t]).wait()
+        squared[code[0, t] % 4] += product(lefts[t], buffer[t])
+        return 0
+
+    lax.fori_loop(0, many, one, 0)
     tall = spread.shape[2]
     for k in range(spread.shape[0]):
         spread[k] = squared[:, k * tall : (k + 1) * tall, :]
 
 
-def cube_kernel(size, code, info, squared, came, rights, purified, lefts):
-    rows = came.shape[2]
-    local = squared.shape[0]
-
-    def unpack(c, _):
-        for h in range(came.shape[0]):
-            lefts[c, h * rows : (h + 1) * rows, :] = came[h, c]
-        return 0
-
-    lax.fori_loop(0, size, unpack, 0)
+def cube_kernel(size, code, info, x, squared, came, rights, purified, lefts, buffer, sems):
+    local = x.shape[0]
+    far = rights.shape[0]
+    many = info[0, 0]
+    fetch_rights(code, many, x, rights, buffer, sems)
+    unpack(size, came, lefts)
     lefts[size : size + local] = squared[...]
     purified[...] = 3.0 * squared[...]
 
     def one(t, _):
         word = code[0, t]
-        q, l_at, r_at = word % 4, (word // 256) % 128, word // 32768
-        l_at = jnp.where(l_at >= 64, l_at - 64 + size, l_at)
-        r_at = jnp.where(r_at >= 64, r_at - 64 + size, r_at)
-        purified[q] += -2.0 * product(lefts[l_at], rights[r_at])
-        return 0
-
-    lax.fori_loop(0, info[0, 0], one, 0)
+        l_at = (word // 256) % 128
+        pltpu.make_async_copy(rights.at[0], buffer.at[t], sems.at[t]).wait()
+        left = lefts[jnp.where(l_at >= far, l_at - far + size, l_at)]
+        purified[word % 4] += -2.0 * product(left, buffer[t])
+        return 0
+
+    lax.fori_loop(0, many, one, 0)
 
 
 def shape(*dims, dtype=F32):
     return jax.ShapeDtypeStruct(dims, dtype)
 
 
-def branch(size, x, right, left, code, info):
+def deliver(size, axis, table, held):
+    _, tall, order = held.shape
+    out = pl.pallas_call(
+        functools.partial(pack_kernel, size),
+        out_shape=shape(lax.axis_size(axis), size, tall, order),
+        in_specs=[SMEM, VMEM],
+        out_specs=VMEM,
+        compiler_params=PARAMS,
+        name="pack",
+    )(table, held)
+    return lax.all_to_all(out, axis, 0, 0, tiled=True)
+
+
+def right_branch(size, table, held):
+    came = deliver(size, "row", table, held)
+    order = came.shape[3]
+    return pl.pallas_call(
+        functools.partial(unpack_kernel, size),
+        out_shape=shape(table.shape[0], order, order),
+        in_specs=[VMEM],
+        out_specs=HBM,
+        scratch_shapes=[pltpu.VMEM((size, order, order), F32), pltpu.SemaphoreType.DMA((size,))],
+        compiler_params=PARAMS,
+        name="unpack",
+    )(came)
+
+
+def left_branch(size, table, held, code, info, x, squared, rights):
+    came = deliver(size, "col", table, held)
     local, order, _ = x.shape
+    return pl.pallas_call(
+        functools.partial(cube_kernel, size),
+        out_shape=shape(local, order, order),
+        in_specs=[SMEM, SMEM, VMEM, VMEM, VMEM, HBM],
+        out_specs=VMEM,
+        scratch_shapes=[
+            pltpu.VMEM((size + local, order, order), F32),
+            pltpu.VMEM((rights.shape[0], order, order), F32),
+            pltpu.SemaphoreType.DMA((rights.shape[0],)),
+        ],
+        compiler_params=PARAMS,
+        name="cube",
+    )(code, info, x, squared, came, rights)
+
+
+def body(density, columns):
     row_devs = lax.axis_size("row")
-    groups = lax.axis_size("col")
+    rows, groups = columns.shape
+    width = rows // groups
+    local, _, order, _ = density.shape
+    cand = local * groups
     fine, tall = order // row_devs, order // groups
+    x = density[:, 0]
     panel = lax.all_gather(x, "col", axis=0, tiled=True)
     spread = x.reshape(local, row_devs, fine, order).transpose(1, 0, 2, 3)
     held = lax.all_to_all(spread, "row", 0, 0, tiled=True)
     held = held.reshape(row_devs * local, fine, order)
-    out = pl.pallas_call(
-        functools.partial(pack_kernel, size),
-        out_shape=shape(row_devs, size, fine, order),
-        in_specs=[SMEM, VMEM],
-        out_specs=VMEM,
-        compiler_params=PARAMS,
-        name="pack_right",
-    )(right, held)
-    came = lax.all_to_all(out, "row", 0, 0, tiled=True)
-    squared, spread, rights = pl.pallas_call(
-        functools.partial(square_kernel, size),
-        out_shape=(
-            shape(local, order, order),
-            shape(groups, local, tall, order),
-            shape(size + local, order, order),
-        ),
-        in_specs=[SMEM, SMEM, VMEM, VMEM, VMEM],
-        out_specs=(VMEM, VMEM, VMEM),
-        compiler_params=PARAMS,
-        name="square",
-    )(code, info, x, panel, came)
-    held = lax.all_to_all(spread, "col", 0, 0, tiled=True)
-    held = held.reshape(groups * local, tall, order)
-    out = pl.pallas_call(
-        functools.partial(pack_kernel, size),
-        out_shape=shape(groups, size, tall, order),
-        in_specs=[SMEM, VMEM],
-        out_specs=VMEM,
-        compiler_params=PARAMS,
-        name="pack_left",
-    )(left, held)
-    came = lax.all_to_all(out, "col", 0, 0, tiled=True)
-    purified = pl.pallas_call(
-        functools.partial(cube_kernel, size),
-        out_shape=shape(local, order, order),
-        in_specs=[SMEM, SMEM, VMEM, VMEM, VMEM],
-        out_specs=VMEM,
-        scratch_shapes=[pltpu.VMEM((size + local, order, order), F32)],
-        compiler_params=PARAMS,
-        name="cube",
-    )(code, info, squared, came, rights)
-    return squared, purified
-
-
-def body(density, columns):
-    row_devs = lax.axis_size("row")
-    rows, groups = columns.shape
-    width = rows // groups
-    local = density.shape[0]
-    cand = local * groups
     here = jnp.stack([lax.axis_index("row"), lax.axis_index("col")]).astype(I32)
     cols = columns.astype(F32)
     right, left, code, info = pl.pallas_call(
@@ -258,11 +308,35 @@
         compiler_params=PARAMS,
         name="plan",
     )(here, cols, cols.T)
-    most = info[0, 1]
-    which = sum((most > size).astype(I32) for size in SIZES[:-1])
-    x = density[:, 0]
-    squared, purified = lax.switch(
-        which, [functools.partial(branch, size) for size in SIZES], x, right, left, code, info
+    rights = lax.switch(
+        info[0, 1], [functools.partial(right_branch, size) for size in SIZES], right, held
+    )
+    squared, spread = pl.pallas_call(
+        square_kernel,
+        out_shape=(shape(local, order, order), shape(groups, local, tall, order)),
+        in_specs=[SMEM, SMEM, VMEM, HBM, HBM],
+        out_specs=(VMEM, VMEM),
+        scratch_shapes=[
+            pltpu.VMEM((cand, order, order), F32),
+            pltpu.VMEM((cand, order, order), F32),
+            pltpu.SemaphoreType.DMA((cand,)),
+            pltpu.SemaphoreType.DMA((cand,)),
+        ],
+        compiler_params=WIDE,
+        name="square",
+    )(code, info, x, panel, rights)
+    held = lax.all_to_all(spread, "col", 0, 0, tiled=True)
+    held = held.reshape(groups * local, tall, order)
+    purified = lax.switch(
+        info[0, 2],
+        [functools.partial(left_branch, size) for size in SIZES],
+        left,
+        held,
+        code,
+        info,
+        x,
+        squared,
+        rights,
     )
     return squared[:, None], purified[:, None]
 

time: 145 us -> 145 us (level)
  blocking collectives: 107 us -> 59.8 us
  starting transfers between devices: 0.04 us -> 25.2 us
  waiting for transfers between devices: 4.61 us -> 24.6 us
  Pallas kernels: 9.82 us -> 15.7 us
  between operations: 17.3 us -> 15.3 us
  local copies, waits for them, and re-layouts: 4.57 us -> 3.09 us
    all_to_all x4 -> x2, blocking collectives: 107 us -> 59.8 us  [deliver(): return lax.all_to_all(out, axis, 0, 0, tiled=True)]
    all_to_all x0 -> x2, starting transfers between devices: none -> 25.2 us  [the longest x1 17 us: body(): held = lax.all_to_all(spread, 'row', 0, 0, tiled=True)]
    all_to_all x0 -> x2, waiting for transfers between devices: none -> 23.9 us  [the longest x1 15.8 us: body(): held = lax.all_to_all(spread, 'row', 0, 0, tiled=True)]
    pallas_call x4 -> x5, Pallas kernels: 7.71 us -> 13.6 us  [the longest x1 5.25 us: body(): pl.pallas_call(square_kernel, out_shape=(shape(local, order, order), shap...]
    all_gather x1, waiting for transfers between devices: 3.93 us -> 0.02 us  [body(): panel = lax.all_gather(x, 'col', axis=0, tiled=True)]
    cond x2 -> x0, local copies, waits for them, and re-layouts: 2.19 us -> none
  transfers between devices with their start and end apart: 1 -> 3, of which waited for: 1 -> 2; matrix products, arithmetic and copies ran while one was open for 1% -> 2% of each run, Pallas kernels for 1% -> 3%
where the time goes in v2:
time: 145 us
  blocking collectives  59.8 us (41%)
  starting transfers between devices  25.2 us (17%)
  waiting for transfers between devices  24.6 us (17%)
  Pallas kernels  15.7 us (11%)
  between operations  15.3 us (11%)
  local copies, waits for them, and re-layouts  3.09 us (2%)
    all_to_all x2, blocking collectives, deliver(): return lax.all_to_all(out, axis, 0, 0, tiled=True)  59.8 us
    all_to_all x1, starting transfers between devices, body(): held = lax.all_to_all(spread, 'row', 0, 0, tiled=True)  17 us
    all_to_all x1, waiting for transfers between devices, body(): held = lax.all_to_all(spread, 'row', 0, 0, tiled=True)  15.8 us
    all_to_all x1, starting transfers between devices, body(): held = lax.all_to_all(spread, 'col', 0, 0, tiled=True)  8.23 us
    all_to_all x1, waiting for transfers between devices, body(): held = lax.all_to_all(spread, 'col', 0, 0, tiled=True)  8.11 us
    pallas_call x1, Pallas kernels, body(): pl.pallas_call(square_kernel, out_shape=(shape(local, order, order), shap...  5.25 us
    pallas_call x1, Pallas kernels, left_branch(): pl.pallas_call(functools.partial(cube_kernel, size), out_shape=shape(loca...  4.13 us
    pallas_call x2, Pallas kernels, deliver(): pl.pallas_call(functools.partial(pack_kernel, size), out_shape=shape(lax....  3.05 us
  transfers between devices with their start and end apart: 3, of which 2 were waited for; matrix products, arithmetic and copies ran while one was open for 2% of the time, Pallas kernels for 3%

profile of v2, /device:TPU:1, one launch (start us, length us, event | category | flops | bytes accessed | tf_op | source)
XLA Modules:
  0.0 144.7 jit_solution(4032880693147833333)
XLA Ops:
  7.2 0.0 all-gather.3.cloned.1.call-start
  7.2 0.7 all-gather.3.cloned.1.call-update
  7.9 1.7 %copy.26 = f32[4,32,4,128]{3,2,0,1:T(4,128)} copy(f32[4,32,4,128]{3,2,1,0:T(4,128)} %bitcast.64) | data formatting | bytes 524288 | tf_op jit(solution)/shard_map/reshape;squeeze | solution.py:293
  9.6 17.0 %all-to-all-start.24 = ((f32[32,4,4,128]{3,2,1,0:T(4,128)}), f32[32,4,4,128]{3,2,1,0:T(4,128)S(1)}, u32[]{:S(2)}, u32[]{:S(2)}) async-start(f32[32,4,4,128]{3,2,1,0:T(4,128)} %bitcast.63), calls=%async_computation.24 | async-start | bytes 524288 | tf_op jit(solution)/shard_map/all_to_all | solution.py:294
  26.6 0.7 convert_bitcast_fusion
  27.3 0.1 copy.9.cols_ref
  27.4 0.1 pad_add_fusion.here
  27.4 2.1 %plan.1 = (s32[64,32]{1,0:T(8,128)S(1)}, s32[64,16]{1,0:T(8,128)S(1)}, s32[1,128]{1,0:T(1,128)S(1)}, s32[1,128]{1,0:T(1,128)S(1)}) custom-call(s32[2]{0:T(128)S(1)} %pad_add_fusion.here, f32[128,16]{1,0:T(8,128)S(1)} %copy.9.cols_ref, f32[16,128]{1,0:T(8,128)S(1)} %get-tuple-element.382.colst_ref), custom_call_target="tpu_custom_call" | custom-call | tf_op jit(solution)/shard_map/plan/pallas_call | solution.py:298
  29.6 0.6 fusion
  30.8 15.8 %all-to-all-done.24 = f32[32,4,4,128]{3,2,1,0:T(4,128)S(1)} async-done(((f32[32,4,4,128]{3,2,1,0:T(4,128)}), f32[32,4,4,128]{3,2,1,0:T(4,128)S(1)}, u32[]{:S(2)}, u32[]{:S(2)}) %all-to-all-start.24) | async-done | bytes 262176 | tf_op jit(solution)/shard_map/all_to_all | solution.py:294
  46.6 0.0 copy-start.2
  46.6 45.4 %conditional.2 = (f32[64,128,128]{2,1,0:T(8,128)}) conditional(s32[]{:T(128)} %bitcast.53, (s32[64,32]{1,0:T(8,128)S(1)}, f32[128,4,128]{2,1,0:T(4,128)S(1)}) %tuple.149, (s32[64,32]{1,0:T(8,128)S(1)}, f32[128,4,128]{2,1,0:T(4,128)S(1)}) %tuple.150, (s32[64,32]{1,0:T(8,128)S(1)}, ...), branch_computations={%region_0.0_spmd, %region_1.0_spmd, %region_2.0_spmd, %region_3.0_... | conditional | bytes 8388616 | solution.py:311
  46.6 1.7 %pack.29 = f32[32,11,4,128]{3,2,1,0:T(4,128)S(1)} custom-call(s32[64,32]{1,0:T(8,128)S(1)} %get-tuple-element.265.table, f32[128,4,128]{2,1,0:T(4,128)S(1)} %get-tuple-element.266.pieces), custom_call_target="tpu_custom_call" | custom-call | tf_op jit(solution)/shard_map/cond/branch_5_fun/pack/pallas_call | solution.py:241
  48.2 42.6 %all_to_all.111.came = f32[32,11,4,128]{3,2,1,0:T(4,128)S(1)} all-to-all(f32[32,11,4,128]{3,2,1,0:T(4,128)S(1)} %pack.29), channel_id=1, replica_groups=mesh['row'=32,'col'=16] {'row'}, dimensions={0} | all-to-all | bytes 1441792 | tf_op jit(solution)/shard_map/cond/branch_5_fun/all_to_all | solution.py:249
  90.8 1.2 unpack.17
  92.0 0.0 all-gather.3.cloned.1.call-done
  92.0 0.0 copy-done.2
  92.0 5.3 %square.1 = (f32[4,128,128]{2,1,0:T(8,128)}, f32[16,4,8,128]{3,2,1,0:T(8,128)}) custom-call(s32[1,128]{1,0:T(1,128)S(1)} %get-tuple-element.371.code, s32[1,128]{1,0:T(1,128)S(1)} %get-tuple-element.372.info, f32[4,128,128]{2,1,0:T(8,128)S(1)} %bitcast.65, f32[64,128,128]{2,1,0:T(8,128)} %bitcast.102, f32[64,128,128]{2,1,0:T(8,128)} %get-tuple-element.398.rights), custom_call_target="tpu_custom_call" | custom-call | tf_op jit(solution)/shard_map/square/pallas_call | solution.py:314
  97.3 8.2 %all-to-all-start.25 = ((f32[16,4,8,128]{3,2,1,0:T(8,128)}), f32[16,4,8,128]{3,2,1,0:T(8,128)S(1)}, u32[]{:S(2)}, u32[]{:S(2)}) async-start(f32[16,4,8,128]{3,2,1,0:T(8,128)} %get-tuple-element.375), calls=%async_computation.25 | async-start | bytes 524288 | tf_op jit(solution)/shard_map/all_to_all | solution.py:328
  106.1 8.1 %all-to-all-done.25 = f32[16,4,8,128]{3,2,1,0:T(8,128)S(1)} async-done(((f32[16,4,8,128]{3,2,1,0:T(8,128)}), f32[16,4,8,128]{3,2,1,0:T(8,128)S(1)}, u32[]{:S(2)}, u32[]{:S(2)}) %all-to-all-start.25) | async-done | bytes 262176 | tf_op jit(solution)/shard_map/all_to_all | solution.py:328
  114.2 22.9 %conditional.3 = (f32[4,1,128,128]{3,2,1,0:T(8,128)S(1)}) conditional(s32[]{:T(128)} %bitcast.59, (f32[16,4,8,128]{3,2,1,0:T(8,128)S(1)}, s32[64,16]{1,0:T(8,128)S(1)}, s32[1,128]{1,0:T(1,128)S(1)}, s32[1,128]{1,0:T(1,128)S(1)}, f32[4,128,128]{2,1,0:T(8,128)S(1)}, /*index=5*/f32[4,128,128]{2,1,0:T(8,128)}, ...), branch_computations={%region_12.0_spmd, %region_13.0_spmd, %region_14.0_spmd, %region_1... | conditional | bytes 25165860 | solution.py:330
  114.2 1.4 pack.41
  115.6 17.2 %all_to_all.123.came = f32[16,11,8,128]{3,2,1,0:T(8,128)S(1)} all-to-all(f32[16,11,8,128]{3,2,1,0:T(8,128)S(1)} %pack.41), channel_id=1, replica_groups=mesh['row'=32,'col'=16] {'col'}, dimensions={0} | all-to-all | bytes 1441792 | tf_op jit(solution)/shard_map/cond/branch_5_fun/all_to_all | solution.py:249
  132.8 4.1 %cube.17 = f32[4,128,128]{2,1,0:T(8,128)S(1)} custom-call(s32[1,128]{1,0:T(1,128)S(1)} %get-tuple-element.314.code, s32[1,128]{1,0:T(1,128)S(1)} %get-tuple-element.315.info, f32[4,128,128]{2,1,0:T(8,128)S(1)} %get-tuple-element.316.x, f32[4,128,128]{2,1,0:T(8,128)} %get-tuple-element.317.squared, f32[16,11,8,128]{3,2,1,0:T(8,128)S(1)} %all_to_all.123.came, ...), custom_call_target="tpu_custom_call" | custom-call | tf_op jit(solution)/shard_map/cond/branch_5_fun/cube/pallas_call | solution.py:269
  137.1 0.0 copy-start.3
  137.2 0.7 copy-done.3
Async XLA Ops:
  7.2 84.9 %all-gather.3.cloned.1.call-start = ((), (), s32[]{:S(2)}) async-start(), calls=%async_computation.26 | async-start | bytes 4456448 | tf_op jit(solution)/shard_map/all_gather | solution.py:292
  9.6 37.0 %all-to-all-start.24 = ((f32[32,4,4,128]{3,2,1,0:T(4,128)}), f32[32,4,4,128]{3,2,1,0:T(4,128)S(1)}, u32[]{:S(2)}, u32[]{:S(2)}) async-start(f32[32,4,4,128]{3,2,1,0:T(4,128)} %bitcast.63), calls=%async_computation.24 | async-start | bytes 524288 | tf_op jit(solution)/shard_map/all_to_all | solution.py:294
  46.6 45.5 %copy-start.2 = (f32[4,1,128,128]{3,2,1,0:T(8,128)S(1)}, f32[4,1,128,128]{3,2,1,0:T(8,128)}, u32[]{:S(2)}) copy-start(f32[4,1,128,128]{3,2,1,0:T(8,128)} %param.26) | copy-start | bytes 786436
  97.3 16.9 %all-to-all-start.25 = ((f32[16,4,8,128]{3,2,1,0:T(8,128)}), f32[16,4,8,128]{3,2,1,0:T(8,128)S(1)}, u32[]{:S(2)}, u32[]{:S(2)}) async-start(f32[16,4,8,128]{3,2,1,0:T(8,128)} %get-tuple-element.375), calls=%async_computation.25 | async-start | bytes 524288 | tf_op jit(solution)/shard_map/all_to_all | solution.py:328
  137.1 0.7 copy-start.3
Sparse Core Ops, SparseCore 0:
  11.3 80.5 all-gather.2

commit v3 on v2

--- a/solution.py
+++ b/solution.py
@@ -12,9 +12,10 @@
 VMEM = pl.BlockSpec(memory_space=pltpu.VMEM)
 HBM = pl.BlockSpec(memory_space=pltpu.HBM)
 SMEM = pl.BlockSpec(memory_space=pltpu.SMEM)
-WIDE = pltpu.CompilerParams(vmem_limit_bytes=57 << 20)
 PARAMS = pltpu.CompilerParams(vmem_limit_bytes=24 << 20)
-SIZES = (6, 7, 8, 9, 10, 11, 12, 13, 14, 16, 20, 64)
+SIZES = (6, 7, 8, 9, 10, 11, 12, 13, 14, 16, 20)
+EVERY = 64
+STEP = 2
 
 
 def iota(shape, dim):
@@ -95,9 +96,14 @@
     r_rank = jnp.sum(jnp.where(wide == 1, ranks, 0.0), axis=1, keepdims=True)
     l_at = jnp.where(j_1 == g_me, slots + q_1, l_rank.astype(I32))
     r_at = jnp.where(is_away > 0, r_rank.astype(I32), slots + s_1 % local)
-    code = (q_1 + 4 * piece + 256 * l_at + 32768 * r_at).astype(F32)
+    half = (j_1 // 2) % 2 != (g_me // 2) % 2
+    panel_at = ((j_1 // 4) * 2 + j_1 % 2) * 2 + half.astype(I32)
+    panel_at = panel_at * local + q_1
+    code = (q_1 + 8 * panel_at + 512 * l_at + 65536 * r_at).astype(F32)
+    idle = float(local + 512 * slots + 65536 * slots)
     hot = (mine > 0) & (order == wide.astype(F32))
-    code_ref[...] = jnp.sum(jnp.where(hot, code, 0.0), axis=0, keepdims=True).astype(I32)
+    code = jnp.sum(jnp.where(hot, code - idle, 0.0), axis=0, keepdims=True) + idle
+    code_ref[...] = code.astype(I32)
     values = rows // groups
     copy = eq(iota((groups, rows), 1) % groups, iota((groups, rows), 0))
     has = eq(dot(cols, copy), (iota((rows, rows), 1) // groups).astype(F32))
@@ -109,11 +115,12 @@
     need_l = dot(dot(group_of, (dot(filled, has) - 1.0) * has), back)
     number = jnp.sum(mine, axis=(0, 1), keepdims=True)
     place = iota((1, 128), 1)
-    info = jnp.where(place == 0, number, 0.0)
-    for at, need in ((1, need_r), (2, need_l)):
-        most = jnp.max(need, axis=(0, 1), keepdims=True)
-        which = sum((most > size).astype(F32) for size in SIZES[:-1])
-        info = info + jnp.where(place == at, which, 0.0)
+    which_r, which_l = (
+        sum((jnp.max(need, axis=(0, 1), keepdims=True) > size).astype(F32) for size in SIZES)
+        for need in (need_r, need_l)
+    )
+    which_l = jnp.where(which_r == len(SIZES), which_r, which_l)
+    info = jnp.where(place == 0, number, jnp.where(place == 1, which_r, which_l))
     info_ref[...] = info.astype(I32)
 
 
@@ -126,15 +133,16 @@
     lax.fori_loop(0, out.shape[0], one, 0)
 
 
-def halves(block):
+def halves(block, axis):
     high = block.astype(jnp.bfloat16)
-    return high, (block - high.astype(F32)).astype(jnp.bfloat16)
+    low = (block - high.astype(F32)).astype(jnp.bfloat16)
+    return jnp.concatenate([high, low], axis=axis)
 
 
 def product(left, right):
-    lh, ll = halves(left)
-    rh, rl = halves(right)
-    return dot(lh, rh) + (dot(lh, rl) + dot(ll, rh))
+    n = left.shape[0]
+    full = dot(halves(left, 0), halves(right, 1))
+    return full[:n, :n] + (full[:n, n:] + full[n:, :n])
 
 
 def unpack(size, came, blocks):
@@ -148,88 +156,64 @@
     lax.fori_loop(0, size, one, 0)
 
 
-def unpack_kernel(size, came, blocks, buffer, sems):
-    def out(slot):
-        return pltpu.make_async_copy(buffer.at[slot], blocks.at[slot], sems.at[slot])
-
-    unpack(size, came, buffer)
-
-    def begin(slot, _):
-        out(slot).start()
+def unpack_kernel(size, came, x, blocks):
+    unpack(size, came, blocks)
+    blocks[blocks.shape[0] - x.shape[0] :] = x[...]
+
+
+def place(at, room):
+    return jnp.where(at >= EVERY, at - EVERY + room, jnp.minimum(at, room - 1))
+
+
+def add_terms(code, steps, total, blocks_of):
+    def one(step, _):
+        words = [code[0, step * STEP + k] for k in range(STEP)]
+        terms = [product(*blocks_of(step * STEP + k, words[k])) for k in range(STEP)]
+        for word, term in zip(words, terms):
+            total[word % 8] += term
         return 0
 
-    def end(slot, _):
-        out(slot).wait()
-        return 0
-
-    lax.fori_loop(0, size, begin, 0)
-    lax.fori_loop(0, size, end, 0)
-
-
-def fetch_rights(code, many, x, rights, buffer, sems):
-    local = x.shape[0]
-    far = rights.shape[0]
-
-    def begin(t, _):
-        r_at = code[0, t] // 32768
-
-        @pl.when(r_at < far)
-        def _():
-            pltpu.make_async_copy(rights.at[jnp.minimum(r_at, far - 1)], buffer.at[t], sems.at[t]).start()
-
-        @pl.when(r_at >= far)
-        def _():
-            pltpu.make_async_copy(x.at[jnp.clip(r_at - far, 0, local - 1)], buffer.at[t], sems.at[t]).start()
-
-        return 0
-
-    lax.fori_loop(0, many, begin, 0)
-
-
-def square_kernel(code, info, x, panel, rights, squared, spread, lefts, buffer, left_sems, right_sems):
-    many = info[0, 0]
+    lax.fori_loop(0, steps, one, 0)
+
+
+def square_kernel(code, info, panel, rights, squared, spread, lefts, total, sems):
+    local = squared.shape[0]
+    steps = (info[0, 0] + STEP - 1) // STEP
+    room = rights.shape[0] - local
 
     def fetch(t):
-        return pltpu.make_async_copy(panel.at[(code[0, t] // 4) % 64], lefts.at[t], left_sems.at[t])
+        return pltpu.make_async_copy(panel.at[(code[0, t] // 8) % 64], lefts.at[t], sems.at[t])
 
     def begin(t, _):
         fetch(t).start()
         return 0
 
-    lax.fori_loop(0, many, begin, 0)
-    fetch_rights(code, many, x, rights, buffer, right_sems)
-    squared[...] = jnp.zeros_like(squared)
-
-    def one(t, _):
+    lax.fori_loop(0, steps * STEP, begin, 0)
+    total[...] = jnp.zeros_like(total)
+
+    def blocks_of(t, word):
         fetch(t).wait()
-        pltpu.make_async_copy(rights.at[0], buffer.at[t], right_sems.at[t]).wait()
-        squared[code[0, t] % 4] += product(lefts[t], buffer[t])
-        return 0
-
-    lax.fori_loop(0, many, one, 0)
+        return lefts[t], rights[place(word // 65536, room)]
+
+    add_terms(code, steps, total, blocks_of)
+    squared[...] = total[:local]
     tall = spread.shape[2]
     for k in range(spread.shape[0]):
         spread[k] = squared[:, k * tall : (k + 1) * tall, :]
 
 
-def cube_kernel(size, code, info, x, squared, came, rights, purified, lefts, buffer, sems):
-    local = x.shape[0]
-    far = rights.shape[0]
-    many = info[0, 0]
-    fetch_rights(code, many, x, rights, buffer, sems)
+def cube_kernel(size, code, info, squared, came, rights, purified, lefts, total):
+    local = squared.shape[0]
+    room = rights.shape[0] - local
     unpack(size, came, lefts)
     lefts[size : size + local] = squared[...]
-    purified[...] = 3.0 * squared[...]
-
-    def one(t, _):
-        word = code[0, t]
-        l_at = (word // 256) % 128
-        pltpu.make_async_copy(rights.at[0], buffer.at[t], sems.at[t]).wait()
-        left = lefts[jnp.where(l_at >= far, l_at - far + size, l_at)]
-        purified[word % 4] += -2.0 * product(left, buffer[t])
-        return 0
-
-    lax.fori_loop(0, many, one, 0)
+    total[...] = jnp.zeros_like(total)
+
+    def blocks_of(t, word):
+        return lefts[place((word // 512) % 128, size)], rights[place(word // 65536, room)]
+
+    add_terms(code, (info[0, 0] + STEP - 1) // STEP, total, blocks_of)
+    purified[...] = 3.0 * squared[...] - 2.0 * total[:local]
 
 
 def shape(*dims, dtype=F32):
@@ -249,36 +233,58 @@
     return lax.all_to_all(out, axis, 0, 0, tiled=True)
 
 
-def right_branch(size, table, held):
+def get_rights(size, room, table, held, x):
     came = deliver(size, "row", table, held)
-    order = came.shape[3]
+    local, order, _ = x.shape
     return pl.pallas_call(
         functools.partial(unpack_kernel, size),
-        out_shape=shape(table.shape[0], order, order),
-        in_specs=[VMEM],
-        out_specs=HBM,
-        scratch_shapes=[pltpu.VMEM((size, order, order), F32), pltpu.SemaphoreType.DMA((size,))],
+        out_shape=shape(room + local, order, order),
+        in_specs=[VMEM, VMEM],
+        out_specs=VMEM,
         compiler_params=PARAMS,
         name="unpack",
-    )(came)
-
-
-def left_branch(size, table, held, code, info, x, squared, rights):
-    came = deliver(size, "col", table, held)
+    )(came, x)
+
+
+def no_rights(room, table, held, x):
+    return jnp.zeros((room + x.shape[0], *x.shape[1:]), F32)
+
+
+def finish(size, tables, held, code, info, x, panel, rights):
+    right, left = tables
     local, order, _ = x.shape
-    return pl.pallas_call(
+    groups = lax.axis_size("col")
+    tall = order // groups
+    if size == EVERY:
+        rights = get_rights(EVERY, EVERY, right, held, x)
+    squared, spread = pl.pallas_call(
+        square_kernel,
+        out_shape=(shape(local, order, order), shape(groups, local, tall, order)),
+        in_specs=[SMEM, SMEM, HBM, VMEM],
+        out_specs=(VMEM, VMEM),
+        scratch_shapes=[
+            pltpu.VMEM((EVERY, order, order), F32),
+            pltpu.VMEM((local + 1, order, order), F32),
+            pltpu.SemaphoreType.DMA((EVERY,)),
+        ],
+        compiler_params=PARAMS,
+        name="square",
+    )(code, info, panel, rights)
+    held = lax.all_to_all(spread, "col", 0, 0, tiled=True)
+    came = deliver(size, "col", left, held.reshape(groups * local, tall, order))
+    purified = pl.pallas_call(
         functools.partial(cube_kernel, size),
         out_shape=shape(local, order, order),
-        in_specs=[SMEM, SMEM, VMEM, VMEM, VMEM, HBM],
+        in_specs=[SMEM, SMEM, VMEM, VMEM, VMEM],
         out_specs=VMEM,
         scratch_shapes=[
             pltpu.VMEM((size + local, order, order), F32),
-            pltpu.VMEM((rights.shape[0], order, order), F32),
-            pltpu.SemaphoreType.DMA((rights.shape[0],)),
+            pltpu.VMEM((local + 1, order, order), F32),
         ],
         compiler_params=PARAMS,
         name="cube",
-    )(code, info, x, squared, came, rights)
+    )(code, info, squared, came, rights)
+    return squared, purified
 
 
 def body(density, columns):
@@ -289,7 +295,6 @@
     cand = local * groups
     fine, tall = order // row_devs, order // groups
     x = density[:, 0]
-    panel = lax.all_gather(x, "col", axis=0, tiled=True)
     spread = x.reshape(local, row_devs, fine, order).transpose(1, 0, 2, 3)
     held = lax.all_to_all(spread, "row", 0, 0, tiled=True)
     held = held.reshape(row_devs * local, fine, order)
@@ -308,34 +313,29 @@
         compiler_params=PARAMS,
         name="plan",
     )(here, cols, cols.T)
+    mate = lax.ppermute(x, "col", [(k, k ^ 2) for k in range(groups)])
+    alike = [[k for k in range(groups) if (k // 2) % 2 == half] for half in range(2)]
+    mate, held, _ = lax.optimization_barrier((mate, held, info))
+    panel = lax.all_gather(
+        jnp.concatenate([x, mate]), "col", axis=0, tiled=True, axis_index_groups=alike
+    )
+    room = SIZES[-1]
     rights = lax.switch(
-        info[0, 1], [functools.partial(right_branch, size) for size in SIZES], right, held
-    )
-    squared, spread = pl.pallas_call(
-        square_kernel,
-        out_shape=(shape(local, order, order), shape(groups, local, tall, order)),
-        in_specs=[SMEM, SMEM, VMEM, HBM, HBM],
-        out_specs=(VMEM, VMEM),
-        scratch_shapes=[
-            pltpu.VMEM((cand, order, order), F32),
-            pltpu.VMEM((cand, order, order), F32),
-            pltpu.SemaphoreType.DMA((cand,)),
-            pltpu.SemaphoreType.DMA((cand,)),
-        ],
-        compiler_params=WIDE,
-        name="square",
-    )(code, info, x, panel, rights)
-    held = lax.all_to_all(spread, "col", 0, 0, tiled=True)
-    held = held.reshape(groups * local, tall, order)
-    purified = lax.switch(
+        info[0, 1],
+        [functools.partial(get_rights, size, room) for size in SIZES] + [functools.partial(no_rights, room)],
+        right,
+        held,
+        x,
+    )
+    squared, purified = lax.switch(
         info[0, 2],
-        [functools.partial(left_branch, size) for size in SIZES],
-        left,
+        [functools.partial(finish, size) for size in (*SIZES, EVERY)],
+        (right, left),
         held,
         code,
         info,
         x,
-        squared,
+        panel,
         rights,
     )
     return squared[:, None], purified[:, None]

time: 145 us -> 146 us (level); the launches traced: 145 us -> 143 us
  blocking collectives: 59.8 us -> 78 us
  waiting for transfers between devices: 24.6 us -> 12.6 us
  Pallas kernels: 15.7 us -> 9.84 us
  starting transfers between devices: 25.2 us -> 21.4 us
  other arithmetic: 0.78 us -> 2.57 us
    all_to_all x0 -> x1, blocking collectives: none -> 19 us  [finish(): held = lax.all_to_all(spread, 'col', 0, 0, tiled=True)]
    all_to_all x1 -> x0, starting transfers between devices: 8.23 us -> none  [body(): held = lax.all_to_all(spread, 'col', 0, 0, tiled=True)]
    all_to_all x1 -> x0, waiting for transfers between devices: 8.11 us -> none  [body(): held = lax.all_to_all(spread, 'col', 0, 0, tiled=True)]
    all_to_all x1, waiting for transfers between devices: 15.8 us -> 8.72 us  [body(): held = lax.all_to_all(spread, 'row', 0, 0, tiled=True)]
    pallas_call x3, Pallas kernels: 10.5 us -> 4.68 us  [the longest x1 3.14 us: finish(): pl.pallas_call(square_kernel, out_shape=(shape(local, order, order), shap...]
    ppermute x0 -> x1, starting transfers between devices: none -> 4.36 us  [body(): mate = lax.ppermute(x, 'col', [(k, k ^ 2) for k in range(groups)])]
    ppermute x0 -> x1, waiting for transfers between devices: none -> 3.85 us  [body(): mate = lax.ppermute(x, 'col', [(k, k ^ 2) for k in range(groups)])]
    concatenate x0 -> x1, other arithmetic: none -> 1.79 us  [body(): jnp.concatenate([x, mate])]
  transfers between devices with their start and end apart: 3 -> 3, of which waited for: 2 -> 2; matrix products, arithmetic and copies ran while one was open for 2% -> 1% of each run, Pallas kernels for 3% -> 3%
where the time goes in v3:
time: 146 us; the launch traced here: 143 us
  blocking collectives  78 us (53%)
  starting transfers between devices  21.4 us (15%)
  between operations  15.4 us (11%)
  waiting for transfers between devices  12.6 us (9%)
  Pallas kernels  9.84 us (7%)
  local copies, waits for them, and re-layouts  3.15 us (2%)
  other arithmetic  2.57 us (2%)
    all_to_all x2, blocking collectives, deliver(): return lax.all_to_all(out, axis, 0, 0, tiled=True)  59 us
    all_to_all x1, blocking collectives, finish(): held = lax.all_to_all(spread, 'col', 0, 0, tiled=True)  19 us
    all_to_all x1, starting transfers between devices, body(): held = lax.all_to_all(spread, 'row', 0, 0, tiled=True)  17 us
    all_to_all x1, waiting for transfers between devices, body(): held = lax.all_to_all(spread, 'row', 0, 0, tiled=True)  8.72 us
    ppermute x1, starting transfers between devices, body(): mate = lax.ppermute(x, 'col', [(k, k ^ 2) for k in range(groups)])  4.36 us
    ppermute x1, waiting for transfers between devices, body(): mate = lax.ppermute(x, 'col', [(k, k ^ 2) for k in range(groups)])  3.85 us
    pallas_call x1, Pallas kernels, finish(): pl.pallas_call(square_kernel, out_shape=(shape(local, order, order), shap...  3.14 us
    pallas_call x2, Pallas kernels, deliver(): pl.pallas_call(functools.partial(pack_kernel, size), out_shape=shape(lax....  3.05 us
  transfers between devices with their start and end apart: 3, of which 2 were waited for; matrix products, arithmetic and copies ran while one was open for 1% of the time, Pallas kernels for 3%

profile of v3, /device:TPU:1, one launch (start us, length us, event | category | flops | bytes accessed | tf_op | source)
XLA Modules:
  0.0 143.2 jit_solution(6950558082709169643)
XLA Ops:
  7.2 0.0 copy-start.1
  7.2 1.8 %copy.23 = f32[4,32,4,128]{3,2,0,1:T(4,128)} copy(f32[4,32,4,128]{3,2,1,0:T(4,128)} %bitcast.73) | data formatting | bytes 524288 | tf_op jit(solution)/shard_map/reshape;squeeze | solution.py:298
  8.9 17.0 %all-to-all-start.36 = ((f32[32,4,4,128]{3,2,1,0:T(4,128)}), f32[32,4,4,128]{3,2,1,0:T(4,128)S(1)}, u32[]{:S(2)}, u32[]{:S(2)}) async-start(f32[32,4,4,128]{3,2,1,0:T(4,128)} %bitcast.60), calls=%async_computation.36 | async-start | bytes 524288 | tf_op jit(solution)/shard_map/all_to_all | solution.py:299
  25.9 0.0 all-gather.2.cloned.1.call-start
  25.9 4.4 %collective-permute-start = (f32[4,128,128]{2,1,0:T(8,128)}, f32[4,128,128]{2,1,0:T(8,128)S(1)}, u32[]{:S(2)}, u32[]{:S(2)}) collective-permute-start(f32[4,128,128]{2,1,0:T(8,128)} %bitcast.74), channel_id=1, source_target_pairs={{0,2},{1,3},{2,0},{3,1},{4,6},{5,7},{6,4},{7,5},{8,10},{9,11},{10,... | collective-permute-start | bytes 786440 | tf_op jit(solution)/shard_map/ppermute | solution.py:316
  30.3 0.7 convert_bitcast_fusion
  31.0 0.1 copy.7.cols_ref
  31.1 0.1 pad_add_fusion.here
  31.2 2.1 %plan.1 = (s32[64,32]{1,0:T(8,128)S(1)}, s32[64,16]{1,0:T(8,128)S(1)}, s32[1,128]{1,0:T(1,128)S(1)}, s32[1,128]{1,0:T(1,128)S(1)}) custom-call(s32[2]{0:T(128)S(1)} %pad_add_fusion.here, f32[128,16]{1,0:T(8,128)S(1)} %copy.7.cols_ref, f32[16,128]{1,0:T(8,128)S(1)} %get-tuple-element.346.colst_ref), custom_call_target="tpu_custom_call" | custom-call | tf_op jit(solution)/shard_map/plan/pallas_call | solution.py:303
  33.3 3.9 %collective-permute-done = f32[4,128,128]{2,1,0:T(8,128)S(1)} collective-permute-done((f32[4,128,128]{2,1,0:T(8,128)}, f32[4,128,128]{2,1,0:T(8,128)S(1)}, u32[]{:S(2)}, u32[]{:S(2)}) %collective-permute-start) | collective-permute-done | bytes 262176 | tf_op jit(solution)/shard_map/ppermute | solution.py:316
  37.2 8.7 %all-to-all-done.36 = f32[32,4,4,128]{3,2,1,0:T(4,128)S(1)} async-done(((f32[32,4,4,128]{3,2,1,0:T(4,128)}), f32[32,4,4,128]{3,2,1,0:T(4,128)S(1)}, u32[]{:S(2)}, u32[]{:S(2)}) %all-to-all-start.36) | async-done | bytes 262176 | tf_op jit(solution)/shard_map/all_to_all | solution.py:299
  45.9 1.8 %pad_maximum_fusion = f32[8,128,128]{2,1,0:T(8,128)} fusion(f32[4,128,128]{2,1,0:T(8,128)S(1)} %collective-permute-done, f32[4,128,128]{2,1,0:T(8,128)} %bitcast.75), kind=kLoop, calls=%fused_computation | loop fusion | flops 131072 | bytes 1048576 | tf_op jit(solution)/shard_map/concatenate | solution.py:320
  47.7 0.0 all-gather.2.cloned.1.call-update
  47.7 0.6 fusion
  49.6 0.0 copy-done.1
  49.6 43.7 %conditional.2 = (f32[24,128,128]{2,1,0:T(8,128)S(1)}) conditional(s32[]{:T(128)} %bitcast.56, (s32[64,32]{1,0:T(8,128)S(1)}, f32[128,4,128]{2,1,0:T(4,128)S(1)}, f32[4,128,128]{2,1,0:T(8,128)S(1)}) %tuple.165, (s32[64,32]{1,0:T(8,128)S(1)}, f32[128,4,128]{2,1,0:T(4,128)S(1)}, ...), branch_computations={%region_0.0_spmd, %region_1.0_spmd, %region_2.0_spmd, %region_3.0_... | conditional | bytes 2621448 | solution.py:323
  49.7 1.7 %pack.29 = f32[32,11,4,128]{3,2,1,0:T(4,128)S(1)} custom-call(s32[64,32]{1,0:T(8,128)S(1)} %get-tuple-element.219.table, f32[128,4,128]{2,1,0:T(4,128)S(1)} %get-tuple-element.220.pieces), custom_call_target="tpu_custom_call" | custom-call | tf_op jit(solution)/shard_map/cond/branch_5_fun/pack/pallas_call | solution.py:225
  51.3 41.7 %all_to_all.154.came = f32[32,11,4,128]{3,2,1,0:T(4,128)S(1)} all-to-all(f32[32,11,4,128]{3,2,1,0:T(4,128)S(1)} %pack.29), channel_id=1, replica_groups=mesh['row'=32,'col'=16] {'row'}, dimensions={0} | all-to-all | bytes 1441792 | tf_op jit(solution)/shard_map/cond/branch_5_fun/all_to_all | solution.py:233
  93.1 0.2 unpack.17
  93.3 0.0 all-gather.2.cloned.1.call-done
  93.3 42.3 %conditional.3 = (f32[4,128,128]{2,1,0:T(8,128)}, f32[4,1,128,128]{3,2,1,0:T(8,128)S(1)}) conditional(s32[]{:T(128)} %bitcast.51, (s32[1,128]{1,0:T(1,128)S(1)}, s32[1,128]{1,0:T(1,128)S(1)}, f32[64,128,128]{2,1,0:T(8,128)}, f32[24,128,128]{2,1,0:T(8,128)S(1)}, s32[64,16]{1,0:T(8,128)S(1)}) %tuple.108, ...), branch_computations={%region_12.0_spmd, %region_13.0_spmd, %region_14.0_spmd, %region_1... | conditional | bytes 34078764 | solution.py:330
  93.4 3.1 %square.17 = (f32[4,128,128]{2,1,0:T(8,128)}, f32[16,4,8,128]{3,2,1,0:T(8,128)S(1)}) custom-call(s32[1,128]{1,0:T(1,128)S(1)} %get-tuple-element.272.code, s32[1,128]{1,0:T(1,128)S(1)} %get-tuple-element.273.info, f32[64,128,128]{2,1,0:T(8,128)} %get-tuple-element.274.panel, f32[24,128,128]{2,1,0:T(8,128)S(1)} %get-tuple-element.275.rights), custom_call_target="tpu_custom_call" | custom-call | tf_op jit(solution)/shard_map/cond/branch_5_fun/square/pallas_call | solution.py:260
  96.5 19.0 %all_to_all.170 = f32[16,4,8,128]{3,2,1,0:T(8,128)S(1)} all-to-all(f32[16,4,8,128]{3,2,1,0:T(8,128)S(1)} %get-tuple-element.278), channel_id=1, replica_groups=mesh['row'=32,'col'=16] {'col'}, dimensions={0} | all-to-all | bytes 524288 | tf_op jit(solution)/shard_map/cond/branch_5_fun/all_to_all | solution.py:273
  115.5 1.4 pack.40
  116.9 17.2 %all_to_all.171.came = f32[16,11,8,128]{3,2,1,0:T(8,128)S(1)} all-to-all(f32[16,11,8,128]{3,2,1,0:T(8,128)S(1)} %pack.40), channel_id=1, replica_groups=mesh['row'=32,'col'=16] {'col'}, dimensions={0} | all-to-all | bytes 1441792 | tf_op jit(solution)/shard_map/cond/branch_5_fun/all_to_all | solution.py:233
  134.1 1.3 cube.17
  135.7 0.0 copy-start.2
  135.7 0.7 copy-done.2
Async XLA Ops:
  7.2 42.4 %copy-start.1 = (f32[4,1,128,128]{3,2,1,0:T(8,128)S(1)}, f32[4,1,128,128]{3,2,1,0:T(8,128)}, u32[]{:S(2)}) copy-start(f32[4,1,128,128]{3,2,1,0:T(8,128)} %param.26) | copy-start | bytes 786436
  8.9 37.0 %all-to-all-start.36 = ((f32[32,4,4,128]{3,2,1,0:T(4,128)}), f32[32,4,4,128]{3,2,1,0:T(4,128)S(1)}, u32[]{:S(2)}, u32[]{:S(2)}) async-start(f32[32,4,4,128]{3,2,1,0:T(4,128)} %bitcast.60), calls=%async_computation.36 | async-start | bytes 524288 | tf_op jit(solution)/shard_map/all_to_all | solution.py:299
  25.9 67.4 %all-gather.2.cloned.1.call-start = ((), (), s32[]{:S(2)}) async-start(), calls=%async_computation.37 | async-start | bytes 4718592 | tf_op jit(solution)/shard_map/all_gather | solution.py:319
  25.9 11.2 %collective-permute-start = (f32[4,128,128]{2,1,0:T(8,128)}, f32[4,128,128]{2,1,0:T(8,128)S(1)}, u32[]{:S(2)}, u32[]{:S(2)}) collective-permute-start(f32[4,128,128]{2,1,0:T(8,128)} %bitcast.74), channel_id=1, source_target_pairs={{0,2},{1,3},{2,0},{3,1},{4,6},{5,7},{6,4},{7,5},{8,10},{9,11},{10,... | collective-permute-start | bytes 786440 | tf_op jit(solution)/shard_map/ppermute | solution.py:316
  135.7 0.7 copy-start.2
Sparse Core Ops, SparseCore 0:
  47.8 34.3 all-gather.1

commit v4 on v3

--- a/solution.py
+++ b/solution.py
@@ -13,8 +13,8 @@
 HBM = pl.BlockSpec(memory_space=pltpu.HBM)
 SMEM = pl.BlockSpec(memory_space=pltpu.SMEM)
 PARAMS = pltpu.CompilerParams(vmem_limit_bytes=24 << 20)
-SIZES = (6, 7, 8, 9, 10, 11, 12, 13, 14, 16, 20)
-EVERY = 64
+SIZES = (6, 7, 8, 9, 10, 11, 12, 13, 14, 16, 20, 64)
+EVERY = SIZES[-1]
 STEP = 2
 
 
@@ -114,14 +114,9 @@
     need_r = dot(dot(group_of, dot(far, has) * has), back)
     need_l = dot(dot(group_of, (dot(filled, has) - 1.0) * has), back)
     number = jnp.sum(mine, axis=(0, 1), keepdims=True)
-    place = iota((1, 128), 1)
-    which_r, which_l = (
-        sum((jnp.max(need, axis=(0, 1), keepdims=True) > size).astype(F32) for size in SIZES)
-        for need in (need_r, need_l)
-    )
-    which_l = jnp.where(which_r == len(SIZES), which_r, which_l)
-    info = jnp.where(place == 0, number, jnp.where(place == 1, which_r, which_l))
-    info_ref[...] = info.astype(I32)
+    most = jnp.max(jnp.maximum(need_r, need_l), axis=(0, 1), keepdims=True)
+    which = sum((most > size).astype(F32) for size in SIZES[:-1])
+    info_ref[...] = jnp.where(iota((1, 128), 1) == 0, number, which).astype(I32)
 
 
 def pack_kernel(size, table, pieces, out):
@@ -154,11 +149,6 @@
         return 0
 
     lax.fori_loop(0, size, one, 0)
-
-
-def unpack_kernel(size, came, x, blocks):
-    unpack(size, came, blocks)
-    blocks[blocks.shape[0] - x.shape[0] :] = x[...]
 
 
 def place(at, room):
@@ -176,26 +166,34 @@
     lax.fori_loop(0, steps, one, 0)
 
 
-def square_kernel(code, info, panel, rights, squared, spread, lefts, total, sems):
-    local = squared.shape[0]
-    steps = (info[0, 0] + STEP - 1) // STEP
-    room = rights.shape[0] - local
-
-    def fetch(t):
+def fetch_kernel(code, info, panel, lefts, sems):
+    many = (info[0, 0] + STEP - 1) // STEP * STEP
+
+    def copy(t):
         return pltpu.make_async_copy(panel.at[(code[0, t] // 8) % 64], lefts.at[t], sems.at[t])
 
     def begin(t, _):
-        fetch(t).start()
-        return 0
-
-    lax.fori_loop(0, steps * STEP, begin, 0)
+        copy(t).start()
+        return 0
+
+    def end(t, _):
+        copy(t).wait()
+        return 0
+
+    lax.fori_loop(0, many, begin, 0)
+    lax.fori_loop(0, many, end, 0)
+
+
+def square_kernel(size, code, info, x, lefts, came, squared, spread, rights, total):
+    local = x.shape[0]
+    unpack(size, came, rights)
+    rights[size:] = x[...]
     total[...] = jnp.zeros_like(total)
 
     def blocks_of(t, word):
-        fetch(t).wait()
-        return lefts[t], rights[place(word // 65536, room)]
-
-    add_terms(code, steps, total, blocks_of)
+        return lefts[t], rights[place(word // 65536, size)]
+
+    add_terms(code, (info[0, 0] + STEP - 1) // STEP, total, blocks_of)
     squared[...] = total[:local]
     tall = spread.shape[2]
     for k in range(spread.shape[0]):
@@ -204,13 +202,12 @@
 
 def cube_kernel(size, code, info, squared, came, rights, purified, lefts, total):
     local = squared.shape[0]
-    room = rights.shape[0] - local
     unpack(size, came, lefts)
     lefts[size : size + local] = squared[...]
     total[...] = jnp.zeros_like(total)
 
     def blocks_of(t, word):
-        return lefts[place((word // 512) % 128, size)], rights[place(word // 65536, room)]
+        return lefts[place((word // 512) % 128, size)], rights[place(word // 65536, size)]
 
     add_terms(code, (info[0, 0] + STEP - 1) // STEP, total, blocks_of)
     purified[...] = 3.0 * squared[...] - 2.0 * total[:local]
@@ -233,43 +230,35 @@
     return lax.all_to_all(out, axis, 0, 0, tiled=True)
 
 
-def get_rights(size, room, table, held, x):
-    came = deliver(size, "row", table, held)
-    local, order, _ = x.shape
-    return pl.pallas_call(
-        functools.partial(unpack_kernel, size),
-        out_shape=shape(room + local, order, order),
-        in_specs=[VMEM, VMEM],
-        out_specs=VMEM,
-        compiler_params=PARAMS,
-        name="unpack",
-    )(came, x)
-
-
-def no_rights(room, table, held, x):
-    return jnp.zeros((room + x.shape[0], *x.shape[1:]), F32)
-
-
-def finish(size, tables, held, code, info, x, panel, rights):
+def branch(size, tables, code, info, x, both, held, alike):
     right, left = tables
     local, order, _ = x.shape
     groups = lax.axis_size("col")
     tall = order // groups
-    if size == EVERY:
-        rights = get_rights(EVERY, EVERY, right, held, x)
-    squared, spread = pl.pallas_call(
-        square_kernel,
-        out_shape=(shape(local, order, order), shape(groups, local, tall, order)),
-        in_specs=[SMEM, SMEM, HBM, VMEM],
-        out_specs=(VMEM, VMEM),
-        scratch_shapes=[
-            pltpu.VMEM((EVERY, order, order), F32),
-            pltpu.VMEM((local + 1, order, order), F32),
-            pltpu.SemaphoreType.DMA((EVERY,)),
-        ],
+    panel = lax.all_gather(both, "col", axis=0, tiled=True, axis_index_groups=alike)
+    came = deliver(size, "row", right, held)
+    lefts = pl.pallas_call(
+        fetch_kernel,
+        out_shape=shape(size + local + 1, order, order),
+        in_specs=[SMEM, SMEM, HBM],
+        out_specs=VMEM,
+        scratch_shapes=[pltpu.SemaphoreType.DMA((size + local + 1,))],
+        compiler_params=PARAMS,
+        name="fetch",
+    )(code, info, panel)
+    squared, spread, rights = pl.pallas_call(
+        functools.partial(square_kernel, size),
+        out_shape=(
+            shape(local, order, order),
+            shape(groups, local, tall, order),
+            shape(size + local, order, order),
+        ),
+        in_specs=[SMEM, SMEM, VMEM, VMEM, VMEM],
+        out_specs=(VMEM, VMEM, VMEM),
+        scratch_shapes=[pltpu.VMEM((local + 1, order, order), F32)],
         compiler_params=PARAMS,
         name="square",
-    )(code, info, panel, rights)
+    )(code, info, x, lefts, came)
     held = lax.all_to_all(spread, "col", 0, 0, tiled=True)
     came = deliver(size, "col", left, held.reshape(groups * local, tall, order))
     purified = pl.pallas_call(
@@ -315,28 +304,17 @@
     )(here, cols, cols.T)
     mate = lax.ppermute(x, "col", [(k, k ^ 2) for k in range(groups)])
     alike = [[k for k in range(groups) if (k // 2) % 2 == half] for half in range(2)]
-    mate, held, _ = lax.optimization_barrier((mate, held, info))
-    panel = lax.all_gather(
-        jnp.concatenate([x, mate]), "col", axis=0, tiled=True, axis_index_groups=alike
-    )
-    room = SIZES[-1]
-    rights = lax.switch(
-        info[0, 1],
-        [functools.partial(get_rights, size, room) for size in SIZES] + [functools.partial(no_rights, room)],
-        right,
-        held,
-        x,
-    )
+    both = jnp.concatenate([x, mate])
+    which, both, held = lax.optimization_barrier((info[0, 1], both, held))
     squared, purified = lax.switch(
-        info[0, 2],
-        [functools.partial(finish, size) for size in (*SIZES, EVERY)],
+        which,
+        [functools.partial(branch, size, alike=alike) for size in SIZES],
         (right, left),
-        held,
         code,
         info,
         x,
-        panel,
-        rights,
+        both,
+        held,
     )
     return squared[:, None], purified[:, None]
 

time: 146 us -> 140 us (0.959); the launches traced: 143 us -> 139 us
  blocking collectives: 78 us -> 36.4 us
  waiting for transfers between devices: 12.6 us -> 41 us
  starting transfers between devices: 21.4 us -> 27.8 us
  local copies, waits for them, and re-layouts: 3.15 us -> 5.27 us
    all_to_all x2 -> x1, blocking collectives: 59 us -> 16.7 us  [deliver(): return lax.all_to_all(out, axis, 0, 0, tiled=True)]
    all_gather x1, waiting for transfers between devices: 0.02 us -> 29.3 us  [branch(): lax.all_gather(both, 'col', axis=0, tiled=True, axis_index_groups=alike)]
    all_to_all x0 -> x1, starting transfers between devices: none -> 6.44 us  [deliver(): return lax.all_to_all(out, axis, 0, 0, tiled=True)]
    cond x0 -> x4, local copies, waits for them, and re-layouts: none -> 2.19 us
    all_to_all x1, waiting for transfers between devices: 8.72 us -> 7.01 us  [body(): held = lax.all_to_all(spread, 'row', 0, 0, tiled=True)]
  transfers between devices with their start and end apart: 3 -> 4, of which waited for: 2 -> 4; matrix products, arithmetic and copies ran while one was open for 1% -> 2% of each run, Pallas kernels for 3% -> 4%
where the time goes in v4:
time: 140 us; the launch traced here: 139 us
  waiting for transfers between devices  41 us (29%)
  blocking collectives  36.4 us (26%)
  starting transfers between devices  27.8 us (20%)
  between operations  14.7 us (10%)
  Pallas kernels  10.6 us (8%)
  local copies, waits for them, and re-layouts  5.27 us (4%)
  other arithmetic  2.57 us (2%)
    all_gather x1, waiting for transfers between devices, branch(): lax.all_gather(both, 'col', axis=0, tiled=True, axis_index_groups=alike)  29.3 us
    all_to_all x1, blocking collectives, branch(): held = lax.all_to_all(spread, 'col', 0, 0, tiled=True)  19.7 us
    all_to_all x1, starting transfers between devices, body(): held = lax.all_to_all(spread, 'row', 0, 0, tiled=True)  17 us
    all_to_all x1, blocking collectives, deliver(): return lax.all_to_all(out, axis, 0, 0, tiled=True)  16.7 us
    all_to_all x1, waiting for transfers between devices, body(): held = lax.all_to_all(spread, 'row', 0, 0, tiled=True)  7.01 us
    all_to_all x1, starting transfers between devices, deliver(): return lax.all_to_all(out, axis, 0, 0, tiled=True)  6.44 us
    ppermute x1, starting transfers between devices, body(): mate = lax.ppermute(x, 'col', [(k, k ^ 2) for k in range(groups)])  4.36 us
    pallas_call x2, Pallas kernels, deliver(): pl.pallas_call(functools.partial(pack_kernel, size), out_shape=shape(lax....  3.84 us
  transfers between devices with their start and end apart: 4, of which 4 were waited for; matrix products, arithmetic and copies ran while one was open for 2% of the time, Pallas kernels for 4%

profile of v4, /device:TPU:1, one launch (start us, length us, event | category | flops | bytes accessed | tf_op | source)
XLA Modules:
  0.0 138.8 jit_solution(12646744904313911602)
XLA Ops:
  7.2 1.7 %copy.23 = f32[4,32,4,128]{3,2,0,1:T(4,128)} copy(f32[4,32,4,128]{3,2,1,0:T(4,128)} %bitcast.72) | data formatting | bytes 524288 | tf_op jit(solution)/shard_map/reshape;squeeze | solution.py:287
  8.9 17.0 %all-to-all-start.36 = ((f32[32,4,4,128]{3,2,1,0:T(4,128)}), f32[32,4,4,128]{3,2,1,0:T(4,128)S(1)}, u32[]{:S(2)}, u32[]{:S(2)}) async-start(f32[32,4,4,128]{3,2,1,0:T(4,128)} %bitcast.59), calls=%async_computation.36 | async-start | bytes 524288 | tf_op jit(solution)/shard_map/all_to_all | solution.py:288
  25.8 4.4 %collective-permute-start = (f32[4,128,128]{2,1,0:T(8,128)}, f32[4,128,128]{2,1,0:T(8,128)S(1)}, u32[]{:S(2)}, u32[]{:S(2)}) collective-permute-start(f32[4,128,128]{2,1,0:T(8,128)} %bitcast.73), channel_id=1, source_target_pairs={{0,2},{1,3},{2,0},{3,1},{4,6},{5,7},{6,4},{7,5},{8,10},{9,11},{10,... | collective-permute-start | bytes 786440 | tf_op jit(solution)/shard_map/ppermute | solution.py:305
  30.2 0.7 convert_bitcast_fusion
  30.9 0.1 copy.7.cols_ref
  31.0 0.1 pad_add_fusion.here
  31.1 2.1 %plan.1 = (s32[64,32]{1,0:T(8,128)S(1)}, s32[64,16]{1,0:T(8,128)S(1)}, s32[1,128]{1,0:T(1,128)S(1)}, s32[1,128]{1,0:T(1,128)S(1)}) custom-call(s32[2]{0:T(128)S(1)} %pad_add_fusion.here, f32[128,16]{1,0:T(8,128)S(1)} %copy.7.cols_ref, f32[16,128]{1,0:T(8,128)S(1)} %get-tuple-element.314.colst_ref), custom_call_target="tpu_custom_call" | custom-call | tf_op jit(solution)/shard_map/plan/pallas_call | solution.py:292
  33.2 0.6 slice.3
  33.8 3.2 %collective-permute-done = f32[4,128,128]{2,1,0:T(8,128)S(1)} collective-permute-done((f32[4,128,128]{2,1,0:T(8,128)}, f32[4,128,128]{2,1,0:T(8,128)S(1)}, u32[]{:S(2)}, u32[]{:S(2)}) %collective-permute-start) | collective-permute-done | bytes 262176 | tf_op jit(solution)/shard_map/ppermute | solution.py:305
  37.0 1.8 %pad_maximum_fusion = f32[8,128,128]{2,1,0:T(8,128)} fusion(f32[4,128,128]{2,1,0:T(8,128)S(1)} %collective-permute-done, f32[4,128,128]{2,1,0:T(8,128)} %bitcast.74), kind=kLoop, calls=%fused_computation | loop fusion | flops 131072 | bytes 1048576 | tf_op jit(solution)/shard_map/concatenate | solution.py:307
  38.8 7.0 %all-to-all-done.36 = f32[32,4,4,128]{3,2,1,0:T(4,128)S(1)} async-done(((f32[32,4,4,128]{3,2,1,0:T(4,128)}), f32[32,4,4,128]{3,2,1,0:T(4,128)S(1)}, u32[]{:S(2)}, u32[]{:S(2)}) %all-to-all-start.36) | async-done | bytes 262176 | tf_op jit(solution)/shard_map/all_to_all | solution.py:288
  46.5 84.7 %conditional.1 = (f32[4,128,128]{2,1,0:T(8,128)}, f32[4,1,128,128]{3,2,1,0:T(8,128)S(1)}) conditional(s32[]{:T(128)} %clamp.3, (f32[8,128,128]{2,1,0:T(8,128)}, s32[1,128]{1,0:T(1,128)S(1)}, s32[1,128]{1,0:T(1,128)S(1)}, s32[64,32]{1,0:T(8,128)S(1)}, f32[128,4,128]{2,1,0:T(4,128)S(1)}, ...), branch_computations={%region_0.0_spmd, %region_1.0_spmd, %region_2.0_spmd, %region_3.0_... | conditional | bytes 106430696 | solution.py:309
  46.5 0.0 copy-start.19
  46.5 0.0 all-gather.21.cloned.1.call-start
  46.6 0.7 all-gather.21.cloned.1.call-update
  47.3 2.5 %pack.32 = f32[32,10,4,128]{3,2,1,0:T(4,128)} custom-call(s32[64,32]{1,0:T(8,128)S(1)} %get-tuple-element.213.table, f32[128,4,128]{2,1,0:T(4,128)S(1)} %get-tuple-element.214.pieces), custom_call_target="tpu_custom_call" | custom-call | tf_op jit(solution)/shard_map/cond/branch_4_fun/pack/pallas_call | solution.py:222
  49.8 6.4 %all-to-all-start.12 = ((f32[32,10,4,128]{3,2,1,0:T(4,128)}), f32[32,10,4,128]{3,2,1,0:T(4,128)S(1)}, u32[]{:S(2)}, u32[]{:S(2)}) async-start(f32[32,10,4,128]{3,2,1,0:T(4,128)} %pack.32), calls=%async_computation.12 | async-start | bytes 1310720 | tf_op jit(solution)/shard_map/cond/branch_4_fun/all_to_all | solution.py:230
  56.2 29.3 %all-gather.21.cloned.1.call-done.panel = f32[64,128,128]{2,1,0:T(8,128)} async-done(((f32[8,128,128]{2,1,0:T(8,128)}), f32[64,128,128]{2,1,0:T(8,128)}) %all-gather.21.cloned.1.call-update) | async-done | bytes 4194320 | tf_op jit(solution)/shard_map/cond/branch_4_fun/all_gather | solution.py:238
  85.5 0.0 copy-start.8
  85.5 2.2 %copy-done.8 = f32[64,128,128]{2,1,0:T(8,128)S(1)} copy-done((f32[64,128,128]{2,1,0:T(8,128)S(1)}, f32[64,128,128]{2,1,0:T(8,128)}, u32[]{:S(2)}) %copy-start.8) | copy-done | bytes 4194328 | tf_op jit(solution)/shard_map/cond
  87.7 1.1 fetch.16.lefts
  88.9 0.7 all-to-all-done.12.came
  89.6 0.0 copy-done.19
  89.6 2.0 %square.16 = (f32[4,128,128]{2,1,0:T(8,128)}, f32[16,4,8,128]{3,2,1,0:T(8,128)S(1)}, f32[14,128,128]{2,1,0:T(8,128)S(1)}) custom-call(s32[1,128]{1,0:T(1,128)S(1)} %get-tuple-element.209.code, s32[1,128]{1,0:T(1,128)S(1)} %get-tuple-element.210.info, f32[4,128,128]{2,1,0:T(8,128)S(1)} %copy-done.19, f32[15,128,128]{2,1,0:T(8,128)S(1)} %fetch.16.lefts, ...), custom_call_target="tpu_custom_call" | custom-call | tf_op jit(solution)/shard_map/cond/branch_4_fun/square/pallas_call | solution.py:249
  91.6 19.7 %all_to_all.157 = f32[16,4,8,128]{3,2,1,0:T(8,128)S(1)} all-to-all(f32[16,4,8,128]{3,2,1,0:T(8,128)S(1)} %get-tuple-element.217), channel_id=1, replica_groups=mesh['row'=32,'col'=16] {'col'}, dimensions={0} | all-to-all | bytes 524288 | tf_op jit(solution)/shard_map/cond/branch_4_fun/all_to_all | solution.py:262
  111.3 1.3 pack.33
  112.6 16.7 %all_to_all.158.came = f32[16,10,8,128]{3,2,1,0:T(8,128)S(1)} all-to-all(f32[16,10,8,128]{3,2,1,0:T(8,128)S(1)} %pack.33), channel_id=1, replica_groups=mesh['row'=32,'col'=16] {'col'}, dimensions={0} | all-to-all | bytes 1310720 | tf_op jit(solution)/shard_map/cond/branch_4_fun/all_to_all | solution.py:230
  129.4 1.6 %cube.16 = f32[4,128,128]{2,1,0:T(8,128)S(1)} custom-call(s32[1,128]{1,0:T(1,128)S(1)} %get-tuple-element.209.code, s32[1,128]{1,0:T(1,128)S(1)} %get-tuple-element.210.info, f32[4,128,128]{2,1,0:T(8,128)} %get-tuple-element.324.squared, f32[16,10,8,128]{3,2,1,0:T(8,128)S(1)} %all_to_all.158.came, f32[14,128,128]{2,1,0:T(8,128)S(1)} %get-tuple-element.218.rights), custom_call_target="tpu_custom_call" | custom-call | tf_op jit(solution)/shard_map/cond/branch_4_fun/cube/pallas_call | solution.py:264
  131.2 0.0 copy-start.27
  131.2 0.7 copy-done.27
Async XLA Ops:
  8.9 37.0 %all-to-all-start.36 = ((f32[32,4,4,128]{3,2,1,0:T(4,128)}), f32[32,4,4,128]{3,2,1,0:T(4,128)S(1)}, u32[]{:S(2)}, u32[]{:S(2)}) async-start(f32[32,4,4,128]{3,2,1,0:T(4,128)} %bitcast.59), calls=%async_computation.36 | async-start | bytes 524288 | tf_op jit(solution)/shard_map/all_to_all | solution.py:288
  25.8 11.2 %collective-permute-start = (f32[4,128,128]{2,1,0:T(8,128)}, f32[4,128,128]{2,1,0:T(8,128)S(1)}, u32[]{:S(2)}, u32[]{:S(2)}) collective-permute-start(f32[4,128,128]{2,1,0:T(8,128)} %bitcast.73), channel_id=1, source_target_pairs={{0,2},{1,3},{2,0},{3,1},{4,6},{5,7},{6,4},{7,5},{8,10},{9,11},{10,... | collective-permute-start | bytes 786440 | tf_op jit(solution)/shard_map/ppermute | solution.py:305
  46.5 43.1 %copy-start.19 = (f32[4,128,128]{2,1,0:T(8,128)S(1)}, f32[4,128,128]{2,1,0:T(8,128)}, u32[]{:S(2)}) copy-start(f32[4,128,128]{2,1,0:T(8,128)} %get-tuple-element.211.x) | copy-start | bytes 786436 | tf_op jit(solution)/shard_map/cond
  46.5 39.0 %all-gather.21.cloned.1.call-start = ((), (), s32[]{:S(2)}) async-start(), calls=%async_computation.41 | async-start | bytes 4718592 | tf_op jit(solution)/shard_map/cond/branch_4_fun/all_gather | solution.py:238
  49.8 39.8 %all-to-all-start.12 = ((f32[32,10,4,128]{3,2,1,0:T(4,128)}), f32[32,10,4,128]{3,2,1,0:T(4,128)S(1)}, u32[]{:S(2)}, u32[]{:S(2)}) async-start(f32[32,10,4,128]{3,2,1,0:T(4,128)} %pack.32), calls=%async_computation.12 | async-start | bytes 1310720 | tf_op jit(solution)/shard_map/cond/branch_4_fun/all_to_all | solution.py:230
  85.5 2.2 %copy-start.8 = (f32[64,128,128]{2,1,0:T(8,128)S(1)}, f32[64,128,128]{2,1,0:T(8,128)}, u32[]{:S(2)}) copy-start(f32[64,128,128]{2,1,0:T(8,128)} %all-gather.21.cloned.1.call-done.panel) | copy-start | bytes 12582916 | tf_op jit(solution)/shard_map/cond
  131.2 0.7 copy-start.27
Sparse Core Ops, SparseCore 0:
  49.5 35.9 all-gather.20

commit v5 on v4

--- a/solution.py
+++ b/solution.py
@@ -120,24 +120,32 @@
 
 
 def pack_kernel(size, table, pieces, out):
-    def one(d, _):
-        for slot in range(size):
-            out[d, slot] = pieces[table[slot, d]]
-        return 0
-
-    lax.fori_loop(0, out.shape[0], one, 0)
-
-
-def halves(block, axis):
+    def one(step, _):
+        for d in [step * 4 + k for k in range(4)]:
+            for slot in range(size):
+                out[d, slot] = pieces[table[slot, d]]
+        return 0
+
+    lax.fori_loop(0, out.shape[0] // 4, one, 0)
+
+
+def spread_kernel(x, out, sems):
+    copies = [pltpu.make_async_copy(x.at[b], out.at[:, b], sems.at[b]) for b in range(x.shape[0])]
+    for copy in copies:
+        copy.start()
+    for copy in copies:
+        copy.wait()
+
+
+def halves(block):
     high = block.astype(jnp.bfloat16)
-    low = (block - high.astype(F32)).astype(jnp.bfloat16)
-    return jnp.concatenate([high, low], axis=axis)
+    return high, (block - high.astype(F32)).astype(jnp.bfloat16)
 
 
 def product(left, right):
-    n = left.shape[0]
-    full = dot(halves(left, 0), halves(right, 1))
-    return full[:n, :n] + (full[:n, n:] + full[n:, :n])
+    lh, ll = halves(left)
+    rh, rl = halves(right)
+    return dot(jnp.concatenate([lh, lh, ll], axis=1), jnp.concatenate([rh, rl, rh], axis=0))
 
 
 def unpack(size, came, blocks):
@@ -200,8 +208,10 @@
         spread[k] = squared[:, k * tall : (k + 1) * tall, :]
 
 
-def cube_kernel(size, code, info, squared, came, rights, purified, lefts, total):
+def cube_kernel(size, code, info, squared, came, rights, squared_out, purified_out, lefts, total, purified, sems):
     local = squared.shape[0]
+    first = pltpu.make_async_copy(squared, squared_out, sems.at[0])
+    first.start()
     unpack(size, came, lefts)
     lefts[size : size + local] = squared[...]
     total[...] = jnp.zeros_like(total)
@@ -211,6 +221,10 @@
 
     add_terms(code, (info[0, 0] + STEP - 1) // STEP, total, blocks_of)
     purified[...] = 3.0 * squared[...] - 2.0 * total[:local]
+    second = pltpu.make_async_copy(purified, purified_out, sems.at[1])
+    second.start()
+    first.wait()
+    second.wait()
 
 
 def shape(*dims, dtype=F32):
@@ -261,19 +275,20 @@
     )(code, info, x, lefts, came)
     held = lax.all_to_all(spread, "col", 0, 0, tiled=True)
     came = deliver(size, "col", left, held.reshape(groups * local, tall, order))
-    purified = pl.pallas_call(
+    return pl.pallas_call(
         functools.partial(cube_kernel, size),
-        out_shape=shape(local, order, order),
+        out_shape=(shape(local, order, order), shape(local, order, order)),
         in_specs=[SMEM, SMEM, VMEM, VMEM, VMEM],
-        out_specs=VMEM,
+        out_specs=(HBM, HBM),
         scratch_shapes=[
             pltpu.VMEM((size + local, order, order), F32),
             pltpu.VMEM((local + 1, order, order), F32),
+            pltpu.VMEM((local, order, order), F32),
+            pltpu.SemaphoreType.DMA((2,)),
         ],
         compiler_params=PARAMS,
         name="cube",
     )(code, info, squared, came, rights)
-    return squared, purified
 
 
 def body(density, columns):
@@ -284,7 +299,15 @@
     cand = local * groups
     fine, tall = order // row_devs, order // groups
     x = density[:, 0]
-    spread = x.reshape(local, row_devs, fine, order).transpose(1, 0, 2, 3)
+    spread = pl.pallas_call(
+        spread_kernel,
+        out_shape=shape(row_devs, local, fine, order),
+        in_specs=[HBM],
+        out_specs=HBM,
+        scratch_shapes=[pltpu.SemaphoreType.DMA((local,))],
+        compiler_params=PARAMS,
+        name="spread",
+    )(x.reshape(local, row_devs, fine, order))
     held = lax.all_to_all(spread, "row", 0, 0, tiled=True)
     held = held.reshape(row_devs * local, fine, order)
     here = jnp.stack([lax.axis_index("row"), lax.axis_index("col")]).astype(I32)

time: 140 us -> 143 us (1.021)
  Pallas kernels: 10.6 us -> 19 us
  blocking collectives: 36.4 us -> 33.5 us
  local copies, waits for them, and re-layouts: 5.27 us -> 2.88 us
    pallas_call x1 -> x2, Pallas kernels: 1.58 us -> 10.9 us  [the longest x1 9.08 us: body(): pl.pallas_call(spread_kernel, out_shape=shape(row_devs, local, fine, orde...]
    all_to_all x1, blocking collectives: 19.7 us -> 17.3 us  [branch(): held = lax.all_to_all(spread, 'col', 0, 0, tiled=True)]
    another operation x1 -> x0, local copies, waits for them, and re-layouts: 1.7 us -> none  [body(): spread = x.reshape(local, row_devs, fine, order).transpose(1, 0, 2, 3)]
  transfers between devices with their start and end apart: 4 -> 4, of which waited for: 4 -> 3; matrix products, arithmetic and copies ran while one was open for 2% -> 2% of each run, Pallas kernels for 4% -> 4%
where the time goes in v5:
time: 143 us; the launch traced here: 141 us
  waiting for transfers between devices  40.4 us (28%)
  blocking collectives  33.5 us (23%)
  starting transfers between devices  27.8 us (19%)
  Pallas kernels  19 us (13%)
  between operations  14.7 us (10%)
  local copies, waits for them, and re-layouts  2.88 us (2%)
  other arithmetic  2.57 us (2%)
    all_gather x1, waiting for transfers between devices, branch(): lax.all_gather(both, 'col', axis=0, tiled=True, axis_index_groups=alike)  29.5 us
    all_to_all x1, blocking collectives, branch(): held = lax.all_to_all(spread, 'col', 0, 0, tiled=True)  17.3 us
    all_to_all x1, starting transfers between devices, body(): held = lax.all_to_all(spread, 'row', 0, 0, tiled=True)  17 us
    all_to_all x1, blocking collectives, deliver(): return lax.all_to_all(out, axis, 0, 0, tiled=True)  16.2 us
    pallas_call x1, Pallas kernels, body(): pl.pallas_call(spread_kernel, out_shape=shape(row_devs, local, fine, orde...  9.08 us
    all_to_all x1, waiting for transfers between devices, body(): held = lax.all_to_all(spread, 'row', 0, 0, tiled=True)  7.01 us
    all_to_all x1, starting transfers between devices, deliver(): return lax.all_to_all(out, axis, 0, 0, tiled=True)  6.44 us
    ppermute x1, starting transfers between devices, body(): mate = lax.ppermute(x, 'col', [(k, k ^ 2) for k in range(groups)])  4.36 us
  transfers between devices with their start and end apart: 4, of which 3 were waited for; matrix products, arithmetic and copies ran while one was open for 2% of the time, Pallas kernels for 4%

profile of v5, /device:TPU:1, one launch (start us, length us, event | category | flops | bytes accessed | tf_op | source)
XLA Modules:
  0.0 141.2 jit_solution(4754712903710965475)
XLA Ops:
  7.2 9.1 %spread.1 = f32[32,4,4,128]{3,2,1,0:T(4,128)} custom-call(f32[4,32,4,128]{3,2,1,0:T(4,128)} %bitcast.34), custom_call_target="tpu_custom_call" | custom-call | tf_op jit(solution)/shard_map/spread/pallas_call | solution.py:302
  16.2 17.0 %all-to-all-start.36 = ((f32[32,4,4,128]{3,2,1,0:T(4,128)}), f32[32,4,4,128]{3,2,1,0:T(4,128)S(1)}, u32[]{:S(2)}, u32[]{:S(2)}) async-start(f32[32,4,4,128]{3,2,1,0:T(4,128)} %spread.1), calls=%async_computation.36 | async-start | bytes 524288 | tf_op jit(solution)/shard_map/all_to_all | solution.py:311
  33.2 4.4 %collective-permute-start = (f32[4,128,128]{2,1,0:T(8,128)}, f32[4,128,128]{2,1,0:T(8,128)S(1)}, u32[]{:S(2)}, u32[]{:S(2)}) collective-permute-start(f32[4,128,128]{2,1,0:T(8,128)} %bitcast.35), channel_id=1, source_target_pairs={{0,2},{1,3},{2,0},{3,1},{4,6},{5,7},{6,4},{7,5},{8,10},{9,11},{10,... | collective-permute-start | bytes 786440 | tf_op jit(solution)/shard_map/ppermute | solution.py:328
  37.6 0.7 convert_bitcast_fusion
  38.3 0.1 copy.5.cols_ref
  38.4 0.1 pad_add_fusion.here
  38.5 2.1 %plan.1 = (s32[64,32]{1,0:T(8,128)S(1)}, s32[64,16]{1,0:T(8,128)S(1)}, s32[1,128]{1,0:T(1,128)S(1)}, s32[1,128]{1,0:T(1,128)S(1)}) custom-call(s32[2]{0:T(128)S(1)} %pad_add_fusion.here, f32[128,16]{1,0:T(8,128)S(1)} %copy.5.cols_ref, f32[16,128]{1,0:T(8,128)S(1)} %get-tuple-element.357.colst_ref), custom_call_target="tpu_custom_call" | custom-call | tf_op jit(solution)/shard_map/plan/pallas_call | solution.py:315
  40.6 0.6 slice.3
  41.2 3.2 %collective-permute-done = f32[4,128,128]{2,1,0:T(8,128)S(1)} collective-permute-done((f32[4,128,128]{2,1,0:T(8,128)}, f32[4,128,128]{2,1,0:T(8,128)S(1)}, u32[]{:S(2)}, u32[]{:S(2)}) %collective-permute-start) | collective-permute-done | bytes 262176 | tf_op jit(solution)/shard_map/ppermute | solution.py:328
  44.4 1.8 %pad_maximum_fusion = f32[8,128,128]{2,1,0:T(8,128)} fusion(f32[4,128,128]{2,1,0:T(8,128)S(1)} %collective-permute-done, f32[4,128,128]{2,1,0:T(8,128)} %bitcast.36), kind=kLoop, calls=%fused_computation | loop fusion | flops 131072 | bytes 1048576 | tf_op jit(solution)/shard_map/concatenate | solution.py:330
  46.2 7.0 %all-to-all-done.36 = f32[32,4,4,128]{3,2,1,0:T(4,128)S(1)} async-done(((f32[32,4,4,128]{3,2,1,0:T(4,128)}), f32[32,4,4,128]{3,2,1,0:T(4,128)S(1)}, u32[]{:S(2)}, u32[]{:S(2)}) %all-to-all-start.36) | async-done | bytes 262176 | tf_op jit(solution)/shard_map/all_to_all | solution.py:311
  53.9 80.5 %conditional.1 = ((f32[4,128,128]{2,1,0:T(8,128)}, f32[4,128,128]{2,1,0:T(8,128)})) conditional(s32[]{:T(128)} %clamp.3, (f32[8,128,128]{2,1,0:T(8,128)}, s32[1,128]{1,0:T(1,128)S(1)}, s32[1,128]{1,0:T(1,128)S(1)}, s32[64,32]{1,0:T(8,128)S(1)}, f32[128,4,128]{2,1,0:T(4,128)S(1)}, /*index=5*/f32[4,128,128]{2,1,0:T(8,128)}, ...), branch_computations={%region_0.0_spmd, %region_1.0_spmd, %region_2.0_spmd, %region_3.0_... | conditional | bytes 106430688 | solution.py:332
  53.9 0.0 copy-start.18
  53.9 0.0 all-gather.19.cloned.1.call-start
  54.0 0.7 all-gather.19.cloned.1.call-update
  54.7 2.3 %pack.30 = f32[32,9,4,128]{3,2,1,0:T(4,128)} custom-call(s32[64,32]{1,0:T(8,128)S(1)} %get-tuple-element.234.table, f32[128,4,128]{2,1,0:T(4,128)S(1)} %get-tuple-element.235.pieces), custom_call_target="tpu_custom_call" | custom-call | tf_op jit(solution)/shard_map/cond/branch_3_fun/pack/pallas_call | solution.py:236
  57.0 6.4 %all-to-all-start.9 = ((f32[32,9,4,128]{3,2,1,0:T(4,128)}), f32[32,9,4,128]{3,2,1,0:T(4,128)S(1)}, u32[]{:S(2)}, u32[]{:S(2)}) async-start(f32[32,9,4,128]{3,2,1,0:T(4,128)} %pack.30), calls=%async_computation.9 | async-start | bytes 1179648 | tf_op jit(solution)/shard_map/cond/branch_3_fun/all_to_all | solution.py:244
  63.4 29.5 %all-gather.19.cloned.1.call-done.panel = f32[64,128,128]{2,1,0:T(8,128)} async-done(((f32[8,128,128]{2,1,0:T(8,128)}), f32[64,128,128]{2,1,0:T(8,128)}) %all-gather.19.cloned.1.call-update) | async-done | bytes 4194320 | tf_op jit(solution)/shard_map/cond/branch_3_fun/all_gather | solution.py:252
  92.9 0.0 copy-start.7
  92.9 2.2 %copy-done.7 = f32[64,128,128]{2,1,0:T(8,128)S(1)} copy-done((f32[64,128,128]{2,1,0:T(8,128)S(1)}, f32[64,128,128]{2,1,0:T(8,128)}, u32[]{:S(2)}) %copy-start.7) | copy-done | bytes 4194328 | tf_op jit(solution)/shard_map/cond
  95.1 1.1 fetch.15.lefts
  96.2 0.0 all-to-all-done.9.came
  96.3 0.0 copy-done.18
  96.3 1.2 square.15
  97.5 17.3 %all_to_all.155 = f32[16,4,8,128]{3,2,1,0:T(8,128)S(1)} all-to-all(f32[16,4,8,128]{3,2,1,0:T(8,128)S(1)} %get-tuple-element.238), channel_id=1, replica_groups=mesh['row'=32,'col'=16] {'col'}, dimensions={0} | all-to-all | bytes 524288 | tf_op jit(solution)/shard_map/cond/branch_3_fun/all_to_all | solution.py:276
  114.8 1.3 pack.31
  116.1 16.2 %all_to_all.156.came = f32[16,9,8,128]{3,2,1,0:T(8,128)S(1)} all-to-all(f32[16,9,8,128]{3,2,1,0:T(8,128)S(1)} %pack.31), channel_id=1, replica_groups=mesh['row'=32,'col'=16] {'col'}, dimensions={0} | all-to-all | bytes 1179648 | tf_op jit(solution)/shard_map/cond/branch_3_fun/all_to_all | solution.py:244
  132.3 1.8 %cube.15 = (f32[4,128,128]{2,1,0:T(8,128)}, f32[4,128,128]{2,1,0:T(8,128)}) custom-call(s32[1,128]{1,0:T(1,128)S(1)} %get-tuple-element.230.code, s32[1,128]{1,0:T(1,128)S(1)} %get-tuple-element.231.info, f32[4,128,128]{2,1,0:T(8,128)S(1)} %get-tuple-element.236.squared, f32[16,9,8,128]{3,2,1,0:T(8,128)S(1)} %all_to_all.156.came, ...), custom_call_target="tpu_custom_call" | custom-call | tf_op jit(solution)/shard_map/cond/branch_3_fun/cube/pallas_call | solution.py:278
Async XLA Ops:
  16.2 37.0 %all-to-all-start.36 = ((f32[32,4,4,128]{3,2,1,0:T(4,128)}), f32[32,4,4,128]{3,2,1,0:T(4,128)S(1)}, u32[]{:S(2)}, u32[]{:S(2)}) async-start(f32[32,4,4,128]{3,2,1,0:T(4,128)} %spread.1), calls=%async_computation.36 | async-start | bytes 524288 | tf_op jit(solution)/shard_map/all_to_all | solution.py:311
  33.2 11.2 %collective-permute-start = (f32[4,128,128]{2,1,0:T(8,128)}, f32[4,128,128]{2,1,0:T(8,128)S(1)}, u32[]{:S(2)}, u32[]{:S(2)}) collective-permute-start(f32[4,128,128]{2,1,0:T(8,128)} %bitcast.35), channel_id=1, source_target_pairs={{0,2},{1,3},{2,0},{3,1},{4,6},{5,7},{6,4},{7,5},{8,10},{9,11},{10,... | collective-permute-start | bytes 786440 | tf_op jit(solution)/shard_map/ppermute | solution.py:328
  53.9 42.3 %copy-start.18 = (f32[4,128,128]{2,1,0:T(8,128)S(1)}, f32[4,128,128]{2,1,0:T(8,128)}, u32[]{:S(2)}) copy-start(f32[4,128,128]{2,1,0:T(8,128)} %get-tuple-element.232.x) | copy-start | bytes 786436 | tf_op jit(solution)/shard_map/cond
  53.9 39.0 %all-gather.19.cloned.1.call-start = ((), (), s32[]{:S(2)}) async-start(), calls=%async_computation.40 | async-start | bytes 4718592 | tf_op jit(solution)/shard_map/cond/branch_3_fun/all_gather | solution.py:252
  57.0 39.3 %all-to-all-start.9 = ((f32[32,9,4,128]{3,2,1,0:T(4,128)}), f32[32,9,4,128]{3,2,1,0:T(4,128)S(1)}, u32[]{:S(2)}, u32[]{:S(2)}) async-start(f32[32,9,4,128]{3,2,1,0:T(4,128)} %pack.30), calls=%async_computation.9 | async-start | bytes 1179648 | tf_op jit(solution)/shard_map/cond/branch_3_fun/all_to_all | solution.py:244
  92.9 2.2 %copy-start.7 = (f32[64,128,128]{2,1,0:T(8,128)S(1)}, f32[64,128,128]{2,1,0:T(8,128)}, u32[]{:S(2)}) copy-start(f32[64,128,128]{2,1,0:T(8,128)} %all-gather.19.cloned.1.call-done.panel) | copy-start | bytes 12582916 | tf_op jit(solution)/shard_map/cond
Sparse Core Ops, SparseCore 0:
  56.9 35.9 all-gather.18

commit v6 on v5

--- a/solution.py
+++ b/solution.py
@@ -15,7 +15,7 @@
 PARAMS = pltpu.CompilerParams(vmem_limit_bytes=24 << 20)
 SIZES = (6, 7, 8, 9, 10, 11, 12, 13, 14, 16, 20, 64)
 EVERY = SIZES[-1]
-STEP = 2
+STEP = 4
 
 
 def iota(shape, dim):
@@ -119,21 +119,60 @@
     info_ref[...] = jnp.where(iota((1, 128), 1) == 0, number, which).astype(I32)
 
 
-def pack_kernel(size, table, pieces, out):
+def pack_kernel(size, table, pieces, out, picks, sem):
+    copy = pltpu.make_async_copy(table.at[: picks.shape[0]], picks, sem)
+    copy.start()
+    copy.wait()
+
     def one(step, _):
         for d in [step * 4 + k for k in range(4)]:
             for slot in range(size):
-                out[d, slot] = pieces[table[slot, d]]
+                out[d, slot] = pieces[picks[slot, d]]
         return 0
 
     lax.fori_loop(0, out.shape[0] // 4, one, 0)
 
 
-def spread_kernel(x, out, sems):
-    copies = [pltpu.make_async_copy(x.at[b], out.at[:, b], sems.at[b]) for b in range(x.shape[0])]
-    for copy in copies:
+def pack_out_kernel(size, table, pieces, out, picks, sem, buffer, sems):
+    copy = pltpu.make_async_copy(table.at[: picks.shape[0]], picks, sem)
+    copy.start()
+    copy.wait()
+
+    def leave(step):
+        part = pl.ds(step * 4, 4)
+        return pltpu.make_async_copy(buffer.at[part], out.at[part], sems.at[step])
+
+    def one(step, _):
+        for d in [step * 4 + k for k in range(4)]:
+            for slot in range(size):
+                buffer[d, slot] = pieces[picks[slot, d]]
+        leave(step).start()
+        return 0
+
+    def end(step, _):
+        leave(step).wait()
+        return 0
+
+    lax.fori_loop(0, out.shape[0] // 4, one, 0)
+    lax.fori_loop(0, out.shape[0] // 4, end, 0)
+
+
+def spread_kernel(x, out, blocks, buffer, in_sems, out_sems):
+    enter = [pltpu.make_async_copy(x.at[b], blocks.at[b], in_sems.at[b]) for b in range(x.shape[0])]
+    for copy in enter:
         copy.start()
-    for copy in copies:
+    for copy in enter:
+        copy.wait()
+    many = out_sems.shape[0]
+    wide = out.shape[0] // many
+    leave = []
+    for step in range(many):
+        for d in range(step * wide, (step + 1) * wide):
+            buffer[d] = blocks[:, d]
+        part = pl.ds(step * wide, wide)
+        leave.append(pltpu.make_async_copy(buffer.at[part], out.at[part], out_sems.at[step]))
+        leave[-1].start()
+    for copy in leave:
         copy.wait()
 
 
@@ -231,17 +270,29 @@
     return jax.ShapeDtypeStruct(dims, dtype)
 
 
-def deliver(size, axis, table, held):
+def packed(size, axis, table, held):
     _, tall, order = held.shape
+    many = lax.axis_size(axis)
+    scratch = [
+        pltpu.SMEM((-(-size // 8) * 8, table.shape[1]), I32),
+        pltpu.SemaphoreType.DMA,
+    ]
+    early = axis == "row"
+    if early:
+        scratch += [
+            pltpu.VMEM((many, size, tall, order), F32),
+            pltpu.SemaphoreType.DMA((many // 4,)),
+        ]
     out = pl.pallas_call(
-        functools.partial(pack_kernel, size),
-        out_shape=shape(lax.axis_size(axis), size, tall, order),
-        in_specs=[SMEM, VMEM],
-        out_specs=VMEM,
+        functools.partial(pack_out_kernel if early else pack_kernel, size),
+        out_shape=shape(many, size, tall, order),
+        in_specs=[VMEM, VMEM],
+        out_specs=HBM if early else VMEM,
+        scratch_shapes=scratch,
         compiler_params=PARAMS,
         name="pack",
     )(table, held)
-    return lax.all_to_all(out, axis, 0, 0, tiled=True)
+    return out
 
 
 def branch(size, tables, code, info, x, both, held, alike):
@@ -249,14 +300,18 @@
     local, order, _ = x.shape
     groups = lax.axis_size("col")
     tall = order // groups
+    out = packed(size, "row", right, held)
+    if size >= 10:
+        both, out = lax.optimization_barrier((both, out))
     panel = lax.all_gather(both, "col", axis=0, tiled=True, axis_index_groups=alike)
-    came = deliver(size, "row", right, held)
+    came = lax.all_to_all(out, "row", 0, 0, tiled=True)
+    panel = pltpu.with_memory_space_constraint(panel, pltpu.HBM)
     lefts = pl.pallas_call(
         fetch_kernel,
-        out_shape=shape(size + local + 1, order, order),
+        out_shape=shape(size + local + STEP - 1, order, order),
         in_specs=[SMEM, SMEM, HBM],
         out_specs=VMEM,
-        scratch_shapes=[pltpu.SemaphoreType.DMA((size + local + 1,))],
+        scratch_shapes=[pltpu.SemaphoreType.DMA((size + local + STEP - 1,))],
         compiler_params=PARAMS,
         name="fetch",
     )(code, info, panel)
@@ -274,7 +329,8 @@
         name="square",
     )(code, info, x, lefts, came)
     held = lax.all_to_all(spread, "col", 0, 0, tiled=True)
-    came = deliver(size, "col", left, held.reshape(groups * local, tall, order))
+    out = packed(size, "col", left, held.reshape(groups * local, tall, order))
+    came = lax.all_to_all(out, "col", 0, 0, tiled=True)
     return pl.pallas_call(
         functools.partial(cube_kernel, size),
         out_shape=(shape(local, order, order), shape(local, order, order)),
@@ -304,7 +360,12 @@
         out_shape=shape(row_devs, local, fine, order),
         in_specs=[HBM],
         out_specs=HBM,
-        scratch_shapes=[pltpu.SemaphoreType.DMA((local,))],
+        scratch_shapes=[
+            pltpu.VMEM((local, row_devs, fine, order), F32),
+            pltpu.VMEM((row_devs, local, fine, order), F32),
+            pltpu.SemaphoreType.DMA((local,)),
+            pltpu.SemaphoreType.DMA((4,)),
+        ],
         compiler_params=PARAMS,
         name="spread",
     )(x.reshape(local, row_devs, fine, order))

time: 143 us -> 140 us (0.979)
  Pallas kernels: 19 us -> 11.1 us
  waiting for transfers between devices: 40.4 us -> 44.9 us
  blocking collectives: 33.5 us -> 36 us
  local copies, waits for them, and re-layouts: 2.88 us -> 0.69 us
    pallas_call x1, Pallas kernels: 9.08 us -> 1.71 us  [body(): pl.pallas_call(spread_kernel, out_shape=shape(row_devs, local, fine, orde...]
    all_to_all x1, waiting for transfers between devices: 0.01 us -> 4.07 us  [branch(): came = lax.all_to_all(out, 'row', 0, 0, tiled=True)]
    cond x4 -> x2, local copies, waits for them, and re-layouts: 2.19 us -> 0.01 us
    all_to_all x1, blocking collectives: 17.3 us -> 18.8 us  [branch(): held = lax.all_to_all(spread, 'col', 0, 0, tiled=True)]
  transfers between devices with their start and end apart: 4 -> 4, of which waited for: 3 -> 4; matrix products, arithmetic and copies ran while one was open for 2% -> 2% of each run, Pallas kernels for 4% -> 3%
where the time goes in v6:
time: 140 us; the launch traced here: 138 us
  waiting for transfers between devices  44.9 us (32%)
  blocking collectives  36 us (26%)
  starting transfers between devices  27.8 us (20%)
  between operations  14.7 us (10%)
  Pallas kernels  11.1 us (8%)
  other arithmetic  2.58 us (2%)
    all_gather x1, waiting for transfers between devices, branch(): lax.all_gather(both, 'col', axis=0, tiled=True, axis_index_groups=alike)  30.6 us
    all_to_all x1, blocking collectives, branch(): held = lax.all_to_all(spread, 'col', 0, 0, tiled=True)  18.8 us
    all_to_all x1, blocking collectives, branch(): came = lax.all_to_all(out, 'col', 0, 0, tiled=True)  17.2 us
    all_to_all x1, starting transfers between devices, body(): held = lax.all_to_all(spread, 'row', 0, 0, tiled=True)  17 us
    all_to_all x1, waiting for transfers between devices, body(): held = lax.all_to_all(spread, 'row', 0, 0, tiled=True)  7 us
    all_to_all x1, starting transfers between devices, branch(): came = lax.all_to_all(out, 'row', 0, 0, tiled=True)  6.46 us
    ppermute x1, starting transfers between devices, body(): mate = lax.ppermute(x, 'col', [(k, k ^ 2) for k in range(groups)])  4.36 us
    all_to_all x1, waiting for transfers between devices, branch(): came = lax.all_to_all(out, 'row', 0, 0, tiled=True)  4.07 us
  transfers between devices with their start and end apart: 4, of which 4 were waited for; matrix products, arithmetic and copies ran while one was open for 2% of the time, Pallas kernels for 3%

profile of v6, /device:TPU:1, one launch (start us, length us, event | category | flops | bytes accessed | tf_op | source)
XLA Modules:
  0.0 138.2 jit_solution(2586517346807716988)
XLA Ops:
  7.2 1.7 %spread.1 = f32[32,4,4,128]{3,2,1,0:T(4,128)} custom-call(f32[4,32,4,128]{3,2,1,0:T(4,128)} %bitcast.34), custom_call_target="tpu_custom_call" | custom-call | tf_op jit(solution)/shard_map/spread/pallas_call | solution.py:358
  8.9 17.0 %all-to-all-start.36 = ((f32[32,4,4,128]{3,2,1,0:T(4,128)}), f32[32,4,4,128]{3,2,1,0:T(4,128)S(1)}, u32[]{:S(2)}, u32[]{:S(2)}) async-start(f32[32,4,4,128]{3,2,1,0:T(4,128)} %spread.1), calls=%async_computation.36 | async-start | bytes 524288 | tf_op jit(solution)/shard_map/all_to_all | solution.py:372
  25.9 4.4 %collective-permute-start = (f32[4,128,128]{2,1,0:T(8,128)}, f32[4,128,128]{2,1,0:T(8,128)S(1)}, u32[]{:S(2)}, u32[]{:S(2)}) collective-permute-start(f32[4,128,128]{2,1,0:T(8,128)} %bitcast.35), channel_id=1, source_target_pairs={{0,2},{1,3},{2,0},{3,1},{4,6},{5,7},{6,4},{7,5},{8,10},{9,11},{10,... | collective-permute-start | bytes 786440 | tf_op jit(solution)/shard_map/ppermute | solution.py:389
  30.2 0.7 convert_bitcast_fusion
  30.9 0.1 copy.5.cols_ref
  31.0 0.1 pad_add_fusion.here
  31.1 2.1 %plan.1 = (s32[64,32]{1,0:T(8,128)S(1)}, s32[64,16]{1,0:T(8,128)S(1)}, s32[1,128]{1,0:T(1,128)S(1)}, s32[1,128]{1,0:T(1,128)S(1)}) custom-call(s32[2]{0:T(128)S(1)} %pad_add_fusion.here, f32[128,16]{1,0:T(8,128)S(1)} %copy.5.cols_ref, f32[16,128]{1,0:T(8,128)S(1)} %get-tuple-element.373.colst_ref), custom_call_target="tpu_custom_call" | custom-call | tf_op jit(solution)/shard_map/plan/pallas_call | solution.py:376
  33.2 0.6 slice.3
  33.8 3.2 %collective-permute-done = f32[4,128,128]{2,1,0:T(8,128)S(1)} collective-permute-done((f32[4,128,128]{2,1,0:T(8,128)}, f32[4,128,128]{2,1,0:T(8,128)S(1)}, u32[]{:S(2)}, u32[]{:S(2)}) %collective-permute-start) | collective-permute-done | bytes 262176 | tf_op jit(solution)/shard_map/ppermute | solution.py:389
  37.1 1.8 %pad_maximum_fusion = f32[8,128,128]{2,1,0:T(8,128)} fusion(f32[4,128,128]{2,1,0:T(8,128)S(1)} %collective-permute-done, f32[4,128,128]{2,1,0:T(8,128)} %bitcast.36), kind=kLoop, calls=%fused_computation | loop fusion | flops 131072 | bytes 1048576 | tf_op jit(solution)/shard_map/concatenate | solution.py:391
  38.9 7.0 %all-to-all-done.36 = f32[32,4,4,128]{3,2,1,0:T(4,128)S(1)} async-done(((f32[32,4,4,128]{3,2,1,0:T(4,128)}), f32[32,4,4,128]{3,2,1,0:T(4,128)S(1)}, u32[]{:S(2)}, u32[]{:S(2)}) %all-to-all-start.36) | async-done | bytes 262176 | tf_op jit(solution)/shard_map/all_to_all | solution.py:372
  46.5 84.8 %conditional.1 = ((f32[4,128,128]{2,1,0:T(8,128)}, f32[4,128,128]{2,1,0:T(8,128)})) conditional(s32[]{:T(128)} %clamp.3, (f32[8,128,128]{2,1,0:T(8,128)}, s32[1,128]{1,0:T(1,128)S(1)}, s32[1,128]{1,0:T(1,128)S(1)}, s32[64,32]{1,0:T(8,128)S(1)}, f32[128,4,128]{2,1,0:T(4,128)S(1)}, /*index=5*/f32[4,128,128]{2,1,0:T(8,128)}, ...), branch_computations={%region_0.0_spmd, %region_1.0_spmd, %region_2.0_spmd, %region_3.0_... | conditional | bytes 90702016 | solution.py:393
  46.6 0.0 copy-start.8
  46.6 0.0 all-gather.23.cloned.1.call-start
  46.6 1.9 %pack.34 = f32[32,11,4,128]{3,2,1,0:T(4,128)} custom-call(s32[64,32]{1,0:T(8,128)S(1)} %get-tuple-element.260.table, f32[128,4,128]{2,1,0:T(4,128)S(1)} %get-tuple-element.261.pieces), custom_call_target="tpu_custom_call" | custom-call | tf_op jit(solution)/shard_map/cond/branch_5_fun/pack/pallas_call | solution.py:286
  48.5 0.0 all-gather.23.cloned.1.call-update
  48.6 6.5 %all-to-all-start.15 = ((f32[32,11,4,128]{3,2,1,0:T(4,128)}), f32[32,11,4,128]{3,2,1,0:T(4,128)S(1)}, u32[]{:S(2)}, u32[]{:S(2)}) async-start(f32[32,11,4,128]{3,2,1,0:T(4,128)} %pack.34), calls=%async_computation.15 | async-start | bytes 1441792 | tf_op jit(solution)/shard_map/cond/branch_5_fun/all_to_all | solution.py:307
  55.0 30.6 %all-gather.23.cloned.1.call-done.panel = f32[64,128,128]{2,1,0:T(8,128)} async-done(((f32[8,128,128]{2,1,0:T(8,128)}), f32[64,128,128]{2,1,0:T(8,128)}) %all-gather.23.cloned.1.call-update) | async-done | bytes 4194320 | tf_op jit(solution)/shard_map/cond/branch_5_fun/all_gather | solution.py:306
  85.6 1.7 %fetch.17.lefts = f32[18,128,128]{2,1,0:T(8,128)S(1)} custom-call(s32[1,128]{1,0:T(1,128)S(1)} %get-tuple-element.256.code, s32[1,128]{1,0:T(1,128)S(1)} %get-tuple-element.257.info, f32[64,128,128]{2,1,0:T(8,128)} %all-gather.23.cloned.1.call-done.panel), custom_call_target="tpu_custom_call" | custom-call | tf_op jit(solution)/shard_map/cond/branch_5_fun/fetch/pallas_call | solution.py:309
  87.3 4.1 %all-to-all-done.15.came = f32[32,11,4,128]{3,2,1,0:T(4,128)S(1)} async-done(((f32[32,11,4,128]{3,2,1,0:T(4,128)}), f32[32,11,4,128]{3,2,1,0:T(4,128)S(1)}, u32[]{:S(2)}, u32[]{:S(2)}) %all-to-all-start.15) | async-done | bytes 720928 | tf_op jit(solution)/shard_map/cond/branch_5_fun/all_to_all | solution.py:307
  91.4 0.0 copy-done.8
  91.4 1.1 square.17
  92.5 18.8 %all_to_all.159 = f32[16,4,8,128]{3,2,1,0:T(8,128)S(1)} all-to-all(f32[16,4,8,128]{3,2,1,0:T(8,128)S(1)} %get-tuple-element.266), channel_id=1, replica_groups=mesh['row'=32,'col'=16] {'col'}, dimensions={0} | all-to-all | bytes 524288 | tf_op jit(solution)/shard_map/cond/branch_5_fun/all_to_all | solution.py:331
  111.3 0.9 pack.35
  112.2 17.2 %all_to_all.160.came = f32[16,11,8,128]{3,2,1,0:T(8,128)S(1)} all-to-all(f32[16,11,8,128]{3,2,1,0:T(8,128)S(1)} %pack.35), channel_id=1, replica_groups=mesh['row'=32,'col'=16] {'col'}, dimensions={0} | all-to-all | bytes 1441792 | tf_op jit(solution)/shard_map/cond/branch_5_fun/all_to_all | solution.py:333
  129.5 1.7 %cube.17 = (f32[4,128,128]{2,1,0:T(8,128)}, f32[4,128,128]{2,1,0:T(8,128)}) custom-call(s32[1,128]{1,0:T(1,128)S(1)} %get-tuple-element.256.code, s32[1,128]{1,0:T(1,128)S(1)} %get-tuple-element.257.info, f32[4,128,128]{2,1,0:T(8,128)S(1)} %get-tuple-element.264.squared, f32[16,11,8,128]{3,2,1,0:T(8,128)S(1)} %all_to_all.160.came, ...), custom_call_target="tpu_custom_call" | custom-call | tf_op jit(solution)/shard_map/cond/branch_5_fun/cube/pallas_call | solution.py:334
Async XLA Ops:
  8.9 37.0 %all-to-all-start.36 = ((f32[32,4,4,128]{3,2,1,0:T(4,128)}), f32[32,4,4,128]{3,2,1,0:T(4,128)S(1)}, u32[]{:S(2)}, u32[]{:S(2)}) async-start(f32[32,4,4,128]{3,2,1,0:T(4,128)} %spread.1), calls=%async_computation.36 | async-start | bytes 524288 | tf_op jit(solution)/shard_map/all_to_all | solution.py:372
  25.9 11.2 %collective-permute-start = (f32[4,128,128]{2,1,0:T(8,128)}, f32[4,128,128]{2,1,0:T(8,128)S(1)}, u32[]{:S(2)}, u32[]{:S(2)}) collective-permute-start(f32[4,128,128]{2,1,0:T(8,128)} %bitcast.35), channel_id=1, source_target_pairs={{0,2},{1,3},{2,0},{3,1},{4,6},{5,7},{6,4},{7,5},{8,10},{9,11},{10,... | collective-permute-start | bytes 786440 | tf_op jit(solution)/shard_map/ppermute | solution.py:389
  46.6 44.8 %copy-start.8 = (f32[4,128,128]{2,1,0:T(8,128)S(1)}, f32[4,128,128]{2,1,0:T(8,128)}, u32[]{:S(2)}) copy-start(f32[4,128,128]{2,1,0:T(8,128)} %get-tuple-element.258.x) | copy-start | bytes 786436 | tf_op jit(solution)/shard_map/cond
  46.6 39.0 %all-gather.23.cloned.1.call-start = ((), (), s32[]{:S(2)}) async-start(), calls=%async_computation.42 | async-start | bytes 4718592 | tf_op jit(solution)/shard_map/cond/branch_5_fun/all_gather | solution.py:306
  48.6 42.8 %all-to-all-start.15 = ((f32[32,11,4,128]{3,2,1,0:T(4,128)}), f32[32,11,4,128]{3,2,1,0:T(4,128)S(1)}, u32[]{:S(2)}, u32[]{:S(2)}) async-start(f32[32,11,4,128]{3,2,1,0:T(4,128)} %pack.34), calls=%async_computation.15 | async-start | bytes 1441792 | tf_op jit(solution)/shard_map/cond/branch_5_fun/all_to_all | solution.py:307
Sparse Core Ops, SparseCore 0:
  49.6 35.9 all-gather.22

commit v7 on v6

--- a/solution.py
+++ b/solution.py
@@ -10,10 +10,11 @@
 F32 = jnp.float32
 I32 = jnp.int32
 VMEM = pl.BlockSpec(memory_space=pltpu.VMEM)
+ANY = pl.BlockSpec(memory_space=pl.ANY)
 HBM = pl.BlockSpec(memory_space=pltpu.HBM)
 SMEM = pl.BlockSpec(memory_space=pltpu.SMEM)
 PARAMS = pltpu.CompilerParams(vmem_limit_bytes=24 << 20)
-SIZES = (6, 7, 8, 9, 10, 11, 12, 13, 14, 16, 20, 64)
+SIZES = (8, 9, 10, 11, 12, 14, 64)
 EVERY = SIZES[-1]
 STEP = 4
 
@@ -96,8 +97,10 @@
     r_rank = jnp.sum(jnp.where(wide == 1, ranks, 0.0), axis=1, keepdims=True)
     l_at = jnp.where(j_1 == g_me, slots + q_1, l_rank.astype(I32))
     r_at = jnp.where(is_away > 0, r_rank.astype(I32), slots + s_1 % local)
-    half = (j_1 // 2) % 2 != (g_me // 2) % 2
-    panel_at = ((j_1 // 4) * 2 + j_1 % 2) * 2 + half.astype(I32)
+    other = ((j_1 + g_me) % 2).astype(I32)
+    steps = (j_1 // 4 + 4 - g_me // 4) % 4
+    half = (j_1 // 2 + g_me // 2) % 2
+    panel_at = (other * 4 + steps) * 2 + half
     panel_at = panel_at * local + q_1
     code = (q_1 + 8 * panel_at + 512 * l_at + 65536 * r_at).astype(F32)
     idle = float(local + 512 * slots + 65536 * slots)
@@ -213,18 +216,28 @@
     lax.fori_loop(0, steps, one, 0)
 
 
-def fetch_kernel(code, info, panel, lefts, sems):
+def fetch_kernel(code, info, *refs):
+    *sources, lefts, sems = refs
     many = (info[0, 0] + STEP - 1) // STEP * STEP
-
-    def copy(t):
-        return pltpu.make_async_copy(panel.at[(code[0, t] // 8) % 64], lefts.at[t], sems.at[t])
+    local = sources[0].shape[0] // 2
+    places = []
+    for core in range(2):
+        own, after, far_0, far_1, before = sources[core * 5 : core * 5 + 5]
+        places += [(own, 0), (own, local), (after, 0), (after, local)]
+        places += [(far_0, 0), (far_1, 0), (before, 0), (before, local)]
 
     def begin(t, _):
-        copy(t).start()
+        at = (code[0, t] // 8) % 64
+        for k, (source, first) in enumerate(places):
+
+            @pl.when(at // local == k)
+            def _():
+                pltpu.make_async_copy(source.at[first + at % local], lefts.at[t], sems.at[t]).start()
+
         return 0
 
     def end(t, _):
-        copy(t).wait()
+        pltpu.make_async_copy(sources[0].at[0], lefts.at[t], sems.at[t]).wait()
         return 0
 
     lax.fori_loop(0, many, begin, 0)
@@ -295,26 +308,35 @@
     return out
 
 
-def branch(size, tables, code, info, x, both, held, alike):
+def branch(size, tables, code, info, x, both, held):
     right, left = tables
     local, order, _ = x.shape
     groups = lax.axis_size("col")
     tall = order // groups
     out = packed(size, "row", right, held)
-    if size >= 10:
-        both, out = lax.optimization_barrier((both, out))
-    panel = lax.all_gather(both, "col", axis=0, tiled=True, axis_index_groups=alike)
     came = lax.all_to_all(out, "row", 0, 0, tiled=True)
-    panel = pltpu.with_memory_space_constraint(panel, pltpu.HBM)
+    ring = range(groups)
+
+    def along(block, by):
+        return lax.ppermute(block, "col", [(k, (k + 4 * by) % groups) for k in ring])
+
+    def across(block):
+        return lax.ppermute(block, "col", [(k, k ^ 1) for k in ring])
+
+    both, out = lax.optimization_barrier((both, out))
+    before, after = along(both, 1), along(both, -1)
+    far_0, far_1 = along(after[:local], -1), along(before[local:], 1)
+    mine = (both, after, far_0, far_1, before)
+    sources = (*mine, *[across(block) for block in mine])
     lefts = pl.pallas_call(
         fetch_kernel,
         out_shape=shape(size + local + STEP - 1, order, order),
-        in_specs=[SMEM, SMEM, HBM],
+        in_specs=[SMEM, SMEM, *[ANY] * len(sources)],
         out_specs=VMEM,
         scratch_shapes=[pltpu.SemaphoreType.DMA((size + local + STEP - 1,))],
         compiler_params=PARAMS,
         name="fetch",
-    )(code, info, panel)
+    )(code, info, *sources)
     squared, spread, rights = pl.pallas_call(
         functools.partial(square_kernel, size),
         out_shape=(
@@ -387,12 +409,11 @@
         name="plan",
     )(here, cols, cols.T)
     mate = lax.ppermute(x, "col", [(k, k ^ 2) for k in range(groups)])
-    alike = [[k for k in range(groups) if (k // 2) % 2 == half] for half in range(2)]
     both = jnp.concatenate([x, mate])
     which, both, held = lax.optimization_barrier((info[0, 1], both, held))
     squared, purified = lax.switch(
         which,
-        [functools.partial(branch, size, alike=alike) for size in SIZES],
+        [functools.partial(branch, size) for size in SIZES],
         (right, left),
         code,
         info,

time: 140 us -> 120 us (0.86)
  waiting for transfers between devices: 44.9 us -> 15.6 us
  starting transfers between devices: 27.8 us -> 56.6 us
  between operations: 14.7 us -> 1.52 us
  blocking collectives: 36 us -> 30.3 us
    all_gather x1 -> x0, waiting for transfers between devices: 30.6 us -> none  [branch(): lax.all_gather(both, 'col', axis=0, tiled=True, axis_index_groups=alike)]
    ppermute x0 -> x9, starting transfers between devices: none -> 29.6 us  [the longest x5 16.6 us: across(): return lax.ppermute(block, 'col', [(k, k ^ 1) for k in ring])]
    all_to_all x1, blocking collectives: 18.8 us -> 14.1 us  [branch(): held = lax.all_to_all(spread, 'col', 0, 0, tiled=True)]
    ppermute x0 -> x9, waiting for transfers between devices: none -> 4.55 us  [the longest x4 3.07 us: along(): lax.ppermute(block, 'col', [(k, (k + 4 * by) % groups) for k in ring])]
    all_to_all x1, waiting for transfers between devices: 4.07 us -> 0.01 us  [branch(): came = lax.all_to_all(out, 'row', 0, 0, tiled=True)]
  transfers between devices with their start and end apart: 4 -> 12, of which waited for: 4 -> 4; matrix products, arithmetic and copies ran while one was open for 2% -> 2% of each run, Pallas kernels for 3% -> 4%
where the time goes in v7:
time: 120 us; the launch traced here: 119 us
  starting transfers between devices  56.6 us (47%)
  blocking collectives  30.3 us (25%)
  waiting for transfers between devices  15.6 us (13%)
  Pallas kernels  12.1 us (10%)
  other arithmetic  1.76 us (1%)
  between operations  1.52 us (1%)
    all_to_all x1, starting transfers between devices, body(): held = lax.all_to_all(spread, 'row', 0, 0, tiled=True)  17 us
    ppermute x5, starting transfers between devices, across(): return lax.ppermute(block, 'col', [(k, k ^ 1) for k in ring])  16.6 us
    all_to_all x1, blocking collectives, branch(): came = lax.all_to_all(out, 'col', 0, 0, tiled=True)  16.2 us
    all_to_all x1, blocking collectives, branch(): held = lax.all_to_all(spread, 'col', 0, 0, tiled=True)  14.1 us
    ppermute x4, starting transfers between devices, along(): lax.ppermute(block, 'col', [(k, (k + 4 * by) % groups) for k in ring])  13.1 us
    all_to_all x1, waiting for transfers between devices, body(): held = lax.all_to_all(spread, 'row', 0, 0, tiled=True)  7.81 us
    all_to_all x1, starting transfers between devices, branch(): came = lax.all_to_all(out, 'row', 0, 0, tiled=True)  5.65 us
    ppermute x1, starting transfers between devices, body(): mate = lax.ppermute(x, 'col', [(k, k ^ 2) for k in range(groups)])  4.36 us
  transfers between devices with their start and end apart: 12, of which 4 were waited for; matrix products, arithmetic and copies ran while one was open for 2% of the time, Pallas kernels for 4%

profile of v7, /device:TPU:1, one launch (start us, length us, event | category | flops | bytes accessed | tf_op | source)
XLA Modules:
  0.0 119.1 jit_solution(16592716267046825682)
XLA Ops:
  0.6 1.7 %spread.1 = f32[32,4,4,128]{3,2,1,0:T(4,128)} custom-call(f32[4,32,4,128]{3,2,1,0:T(4,128)} %bitcast.24), custom_call_target="tpu_custom_call" | custom-call | tf_op jit(solution)/shard_map/spread/pallas_call | solution.py:380
  2.3 17.0 %all-to-all-start.21 = ((f32[32,4,4,128]{3,2,1,0:T(4,128)}), f32[32,4,4,128]{3,2,1,0:T(4,128)S(1)}, u32[]{:S(2)}, u32[]{:S(2)}) async-start(f32[32,4,4,128]{3,2,1,0:T(4,128)} %spread.1), calls=%async_computation.21 | async-start | bytes 524288 | tf_op jit(solution)/shard_map/all_to_all | solution.py:394
  19.3 4.4 %collective-permute-start.63 = (f32[4,128,128]{2,1,0:T(8,128)}, f32[4,128,128]{2,1,0:T(8,128)S(1)}, u32[]{:S(2)}, u32[]{:S(2)}) collective-permute-start(f32[4,128,128]{2,1,0:T(8,128)} %bitcast.25), channel_id=1, source_target_pairs={{0,2},{1,3},{2,0},{3,1},{4,6},{5,7},{6,4},{7,5},{8,10},{9,11},{10,... | collective-permute-start | bytes 786440 | tf_op jit(solution)/shard_map/ppermute | solution.py:411
  23.7 0.7 convert_bitcast_fusion
  24.4 0.1 copy.4.cols_ref
  24.5 0.1 pad_add_fusion.here
  24.6 2.1 %plan.1 = (s32[64,32]{1,0:T(8,128)S(1)}, s32[64,16]{1,0:T(8,128)S(1)}, s32[1,128]{1,0:T(1,128)S(1)}, s32[1,128]{1,0:T(1,128)S(1)}) custom-call(s32[2]{0:T(128)S(1)} %pad_add_fusion.here, f32[128,16]{1,0:T(8,128)S(1)} %copy.4.cols_ref, f32[16,128]{1,0:T(8,128)S(1)} %get-tuple-element.224.colst_ref), custom_call_target="tpu_custom_call" | custom-call | tf_op jit(solution)/shard_map/plan/pallas_call | solution.py:398
  26.7 0.6 slice.45
  27.3 3.2 %collective-permute-done.63 = f32[4,128,128]{2,1,0:T(8,128)S(1)} collective-permute-done((f32[4,128,128]{2,1,0:T(8,128)}, f32[4,128,128]{2,1,0:T(8,128)S(1)}, u32[]{:S(2)}, u32[]{:S(2)}) %collective-permute-start.63) | collective-permute-done | bytes 262176 | tf_op jit(solution)/shard_map/ppermute | solution.py:411
  30.5 1.0 pad_maximum_fusion
  31.5 7.8 %all-to-all-done.21 = f32[32,4,4,128]{3,2,1,0:T(4,128)S(1)} async-done(((f32[32,4,4,128]{3,2,1,0:T(4,128)}), f32[32,4,4,128]{3,2,1,0:T(4,128)S(1)}, u32[]{:S(2)}, u32[]{:S(2)}) %all-to-all-start.21) | async-done | bytes 262176 | tf_op jit(solution)/shard_map/all_to_all | solution.py:394
  40.0 78.9 %conditional.1 = ((f32[4,128,128]{2,1,0:T(8,128)}, f32[4,128,128]{2,1,0:T(8,128)})) conditional(s32[]{:T(128)} %clamp.3, (s32[64,32]{1,0:T(8,128)S(1)}, f32[128,4,128]{2,1,0:T(4,128)S(1)}, f32[8,128,128]{2,1,0:T(8,128)S(1)}, s32[1,128]{1,0:T(1,128)S(1)}, s32[1,128]{1,0:T(1,128)S(1)}, ...), branch_computations={%region_0.0_spmd, %region_1.0_spmd, %region_2.0_spmd, %region_3.0_... | conditional | bytes 92275200 | solution.py:414
  40.0 0.0 copy-start.4
  40.0 1.8 %pack.16 = f32[32,9,4,128]{3,2,1,0:T(4,128)} custom-call(s32[64,32]{1,0:T(8,128)S(1)} %get-tuple-element.131.table, f32[128,4,128]{2,1,0:T(4,128)S(1)} %get-tuple-element.132.pieces), custom_call_target="tpu_custom_call" | custom-call | tf_op jit(solution)/shard_map/cond/branch_1_fun/pack/pallas_call | solution.py:299
  41.8 5.7 %all-to-all-start.3 = ((f32[32,9,4,128]{3,2,1,0:T(4,128)}), f32[32,9,4,128]{3,2,1,0:T(4,128)S(1)}, u32[]{:S(2)}, u32[]{:S(2)}) async-start(f32[32,9,4,128]{3,2,1,0:T(4,128)} %pack.16), calls=%async_computation.3 | async-start | bytes 1179648 | tf_op jit(solution)/shard_map/cond/branch_1_fun/all_to_all | solution.py:317
  47.5 3.2 %collective-permute-start.11 = (f32[8,128,128]{2,1,0:T(8,128)S(1)}, f32[8,128,128]{2,1,0:T(8,128)S(1)}, u32[]{:S(2)}, u32[]{:S(2)}) collective-permute-start(f32[8,128,128]{2,1,0:T(8,128)S(1)} %get-tuple-element.133.refs_0_), channel_id=1, source_target_pairs={{0,4},{1,5},{2,6},{3,7},{4,8},{5,9},{6,10},{7,11},{8,12},{9,13},{1... | collective-permute-start | bytes 1572872 | tf_op jit(solution)/shard_map/cond/branch_1_fun/ppermute | solution.py:321
  50.7 3.4 %collective-permute-start.9 = (f32[8,128,128]{2,1,0:T(8,128)S(1)}, f32[8,128,128]{2,1,0:T(8,128)S(1)}, u32[]{:S(2)}, u32[]{:S(2)}) collective-permute-start(f32[8,128,128]{2,1,0:T(8,128)S(1)} %get-tuple-element.133.refs_0_), channel_id=1, source_target_pairs={{0,12},{1,13},{2,14},{3,15},{4,0},{5,1},{6,2},{7,3},{8,4},{9,5},{1... | collective-permute-start | bytes 1572872 | tf_op jit(solution)/shard_map/cond/branch_1_fun/ppermute | solution.py:321
  54.1 4.7 %collective-permute-start.13 = (f32[8,128,128]{2,1,0:T(8,128)S(1)}, f32[8,128,128]{2,1,0:T(8,128)S(1)}, u32[]{:S(2)}, u32[]{:S(2)}) collective-permute-start(f32[8,128,128]{2,1,0:T(8,128)S(1)} %get-tuple-element.133.refs_0_), channel_id=1, source_target_pairs={{0,1},{1,0},{2,3},{3,2},{4,5},{5,4},{6,7},{7,6},{8,9},{9,8},{10,11... | collective-permute-start | bytes 1572872 | tf_op jit(solution)/shard_map/cond/branch_1_fun/ppermute | solution.py:324
  58.8 3.1 %collective-permute-done.11.refs_4_ = f32[8,128,128]{2,1,0:T(8,128)S(1)} collective-permute-done((f32[8,128,128]{2,1,0:T(8,128)S(1)}, f32[8,128,128]{2,1,0:T(8,128)S(1)}, u32[]{:S(2)}, u32[]{:S(2)}) %collective-permute-start.11) | collective-permute-done | bytes 524320 | tf_op jit(solution)/shard_map/cond/branch_1_fun/ppermute | solution.py:321
  61.9 1.9 %collective-permute-start.12 = (f32[4,128,128]{2,1,0:T(8,128)S(1)}, f32[4,128,128]{2,1,0:T(8,128)S(1)}, u32[]{:S(2)}, u32[]{:S(2)}) collective-permute-start(f32[4,128,128]{2,1,0:T(8,128)S(1)} %slice.49), channel_id=1, source_target_pairs={{0,4},{1,5},{2,6},{3,7},{4,8},{5,9},{6,10},{7,11},{8,12},{9,13},{1... | collective-permute-start | bytes 786440 | tf_op jit(solution)/shard_map/cond/branch_1_fun/ppermute | solution.py:321
  63.8 0.0 collective-permute-done.9.refs_1_
  63.8 4.6 %collective-permute-start.10 = (f32[4,128,128]{2,1,0:T(8,128)S(1)}, f32[4,128,128]{2,1,0:T(8,128)S(1)}, u32[]{:S(2)}, u32[]{:S(2)}) collective-permute-start(f32[4,128,128]{2,1,0:T(8,128)S(1)} %slice.48), channel_id=1, source_target_pairs={{0,12},{1,13},{2,14},{3,15},{4,0},{5,1},{6,2},{7,3},{8,4},{9,5},{1... | collective-permute-start | bytes 786440 | tf_op jit(solution)/shard_map/cond/branch_1_fun/ppermute | solution.py:321
  68.4 5.6 %collective-permute-start.17 = (f32[8,128,128]{2,1,0:T(8,128)S(1)}, f32[8,128,128]{2,1,0:T(8,128)S(1)}, u32[]{:S(2)}, u32[]{:S(2)}) collective-permute-start(f32[8,128,128]{2,1,0:T(8,128)S(1)} %collective-permute-done.11.refs_4_), channel_id=1, source_target_pairs={{0,1},{1,0},{2,3},{3,2},{4,5},{5,4},{6,7},{7,6},{8,9},{9,8},{10,11... | collective-permute-start | bytes 1572872 | tf_op jit(solution)/shard_map/cond/branch_1_fun/ppermute | solution.py:324
  74.1 1.9 %collective-permute-start.14 = (f32[8,128,128]{2,1,0:T(8,128)S(1)}, f32[8,128,128]{2,1,0:T(8,128)S(1)}, u32[]{:S(2)}, u32[]{:S(2)}) collective-permute-start(f32[8,128,128]{2,1,0:T(8,128)S(1)} %collective-permute-done.9.refs_1_), channel_id=1, source_target_pairs={{0,1},{1,0},{2,3},{3,2},{4,5},{5,4},{6,7},{7,6},{8,9},{9,8},{10,11... | collective-permute-start | bytes 1572872 | tf_op jit(solution)/shard_map/cond/branch_1_fun/ppermute | solution.py:324
  76.0 0.0 collective-permute-done.12.refs_3_
  76.0 2.4 %collective-permute-start.16 = (f32[4,128,128]{2,1,0:T(8,128)S(1)}, f32[4,128,128]{2,1,0:T(8,128)S(1)}, u32[]{:S(2)}, u32[]{:S(2)}) collective-permute-start(f32[4,128,128]{2,1,0:T(8,128)S(1)} %collective-permute-done.12.refs_3_), channel_id=1, source_target_pairs={{0,1},{1,0},{2,3},{3,2},{4,5},{5,4},{6,7},{7,6},{8,9},{9,8},{10,11... | collective-permute-start | bytes 786440 | tf_op jit(solution)/shard_map/cond/branch_1_fun/ppermute | solution.py:324
  78.4 0.0 collective-permute-done.10.refs_2_
  78.4 1.9 %collective-permute-start.15 = (f32[4,128,128]{2,1,0:T(8,128)S(1)}, f32[4,128,128]{2,1,0:T(8,128)S(1)}, u32[]{:S(2)}, u32[]{:S(2)}) collective-permute-start(f32[4,128,128]{2,1,0:T(8,128)S(1)} %collective-permute-done.10.refs_2_), channel_id=1, source_target_pairs={{0,1},{1,0},{2,3},{3,2},{4,5},{5,4},{6,7},{7,6},{8,9},{9,8},{10,11... | collective-permute-start | bytes 786440 | tf_op jit(solution)/shard_map/cond/branch_1_fun/ppermute | solution.py:324
  80.3 0.0 collective-permute-done.13.refs_5_
  80.4 0.0 collective-permute-done.16.refs_8_
  80.4 0.0 collective-permute-done.17.refs_9_
  80.4 1.5 %collective-permute-done.15.refs_7_ = f32[4,128,128]{2,1,0:T(8,128)S(1)} collective-permute-done((f32[4,128,128]{2,1,0:T(8,128)S(1)}, f32[4,128,128]{2,1,0:T(8,128)S(1)}, u32[]{:S(2)}, u32[]{:S(2)}) %collective-permute-start.15) | collective-permute-done | bytes 262176 | tf_op jit(solution)/shard_map/cond/branch_1_fun/ppermute | solution.py:324
  81.8 0.0 collective-permute-done.14.refs_6_
  81.9 2.3 %fetch.8.lefts = f32[16,128,128]{2,1,0:T(8,128)S(1)} custom-call(s32[1,128]{1,0:T(1,128)S(1)} %get-tuple-element.127.code, s32[1,128]{1,0:T(1,128)S(1)} %get-tuple-element.128.info, f32[8,128,128]{2,1,0:T(8,128)S(1)} %get-tuple-element.133.refs_0_, f32[8,128,128]{2,1,0:T(8,128)S(1)} %collective-permute-done.9.refs_1_, ...), custom_call_target="tpu_custom_call" | custom-call | tf_op jit(solution)/shard_map/cond/branch_1_fun/fetch/pallas_call | solution.py:331
  84.1 0.0 all-to-all-done.3.came
  84.2 0.0 copy-done.4
  84.2 1.3 %square.8 = (f32[4,128,128]{2,1,0:T(8,128)S(1)}, f32[16,4,8,128]{3,2,1,0:T(8,128)S(1)}, f32[13,128,128]{2,1,0:T(8,128)S(1)}) custom-call(s32[1,128]{1,0:T(1,128)S(1)} %get-tuple-element.127.code, s32[1,128]{1,0:T(1,128)S(1)} %get-tuple-element.128.info, f32[4,128,128]{2,1,0:T(8,128)S(1)} %copy-done.4, f32[16,128,128]{2,1,0:T(8,128)S(1)} %fetch.8.lefts, ...), custom_call_target="tpu_custom_call" | custom-call | tf_op jit(solution)/shard_map/cond/branch_1_fun/square/pallas_call | solution.py:340
  85.5 14.1 %all_to_all.91 = f32[16,4,8,128]{3,2,1,0:T(8,128)S(1)} all-to-all(f32[16,4,8,128]{3,2,1,0:T(8,128)S(1)} %get-tuple-element.136), channel_id=1, replica_groups=mesh['row'=32,'col'=16] {'col'}, dimensions={0} | all-to-all | bytes 524288 | tf_op jit(solution)/shard_map/cond/branch_1_fun/all_to_all | solution.py:353
  99.6 0.9 pack.17
  100.5 16.2 %all_to_all.92.came = f32[16,9,8,128]{3,2,1,0:T(8,128)S(1)} all-to-all(f32[16,9,8,128]{3,2,1,0:T(8,128)S(1)} %pack.17), channel_id=1, replica_groups=mesh['row'=32,'col'=16] {'col'}, dimensions={0} | all-to-all | bytes 1179648 | tf_op jit(solution)/shard_map/cond/branch_1_fun/all_to_all | solution.py:355
  116.7 1.9 %cube.8 = (f32[4,128,128]{2,1,0:T(8,128)}, f32[4,128,128]{2,1,0:T(8,128)}) custom-call(s32[1,128]{1,0:T(1,128)S(1)} %get-tuple-element.127.code, s32[1,128]{1,0:T(1,128)S(1)} %get-tuple-element.128.info, f32[4,128,128]{2,1,0:T(8,128)S(1)} %get-tuple-element.134.squared, f32[16,9,8,128]{3,2,1,0:T(8,128)S(1)} %all_to_all.92.came, ...), custom_call_target="tpu_custom_call" | custom-call | tf_op jit(solution)/shard_map/cond/branch_1_fun/cube/pallas_call | solution.py:356
  (2 shorter events, 0.0 us)
Async XLA Ops:
  2.3 37.0 %all-to-all-start.21 = ((f32[32,4,4,128]{3,2,1,0:T(4,128)}), f32[32,4,4,128]{3,2,1,0:T(4,128)S(1)}, u32[]{:S(2)}, u32[]{:S(2)}) async-start(f32[32,4,4,128]{3,2,1,0:T(4,128)} %spread.1), calls=%async_computation.21 | async-start | bytes 524288 | tf_op jit(solution)/shard_map/all_to_all | solution.py:394
  19.3 11.2 %collective-permute-start.63 = (f32[4,128,128]{2,1,0:T(8,128)}, f32[4,128,128]{2,1,0:T(8,128)S(1)}, u32[]{:S(2)}, u32[]{:S(2)}) collective-permute-start(f32[4,128,128]{2,1,0:T(8,128)} %bitcast.25), channel_id=1, source_target_pairs={{0,2},{1,3},{2,0},{3,1},{4,6},{5,7},{6,4},{7,5},{8,10},{9,11},{10,... | collective-permute-start | bytes 786440 | tf_op jit(solution)/shard_map/ppermute | solution.py:411
  40.0 44.2 %copy-start.4 = (f32[4,128,128]{2,1,0:T(8,128)S(1)}, f32[4,128,128]{2,1,0:T(8,128)}, u32[]{:S(2)}) copy-start(f32[4,128,128]{2,1,0:T(8,128)} %get-tuple-element.129.x) | copy-start | bytes 786436 | tf_op jit(solution)/shard_map/cond
  41.8 42.3 %all-to-all-start.3 = ((f32[32,9,4,128]{3,2,1,0:T(4,128)}), f32[32,9,4,128]{3,2,1,0:T(4,128)S(1)}, u32[]{:S(2)}, u32[]{:S(2)}) async-start(f32[32,9,4,128]{3,2,1,0:T(4,128)} %pack.16), calls=%async_computation.3 | async-start | bytes 1179648 | tf_op jit(solution)/shard_map/cond/branch_1_fun/all_to_all | solution.py:317
  47.5 14.4 %collective-permute-start.11 = (f32[8,128,128]{2,1,0:T(8,128)S(1)}, f32[8,128,128]{2,1,0:T(8,128)S(1)}, u32[]{:S(2)}, u32[]{:S(2)}) collective-permute-start(f32[8,128,128]{2,1,0:T(8,128)S(1)} %get-tuple-element.133.refs_0_), channel_id=1, source_target_pairs={{0,4},{1,5},{2,6},{3,7},{4,8},{5,9},{6,10},{7,11},{8,12},{9,13},{1... | collective-permute-start | bytes 1572872 | tf_op jit(solution)/shard_map/cond/branch_1_fun/ppermute | solution.py:321
  50.7 13.1 %collective-permute-start.9 = (f32[8,128,128]{2,1,0:T(8,128)S(1)}, f32[8,128,128]{2,1,0:T(8,128)S(1)}, u32[]{:S(2)}, u32[]{:S(2)}) collective-permute-start(f32[8,128,128]{2,1,0:T(8,128)S(1)} %get-tuple-element.133.refs_0_), channel_id=1, source_target_pairs={{0,12},{1,13},{2,14},{3,15},{4,0},{5,1},{6,2},{7,3},{8,4},{9,5},{1... | collective-permute-start | bytes 1572872 | tf_op jit(solution)/shard_map/cond/branch_1_fun/ppermute | solution.py:321
  54.1 26.3 %collective-permute-start.13 = (f32[8,128,128]{2,1,0:T(8,128)S(1)}, f32[8,128,128]{2,1,0:T(8,128)S(1)}, u32[]{:S(2)}, u32[]{:S(2)}) collective-permute-start(f32[8,128,128]{2,1,0:T(8,128)S(1)} %get-tuple-element.133.refs_0_), channel_id=1, source_target_pairs={{0,1},{1,0},{2,3},{3,2},{4,5},{5,4},{6,7},{7,6},{8,9},{9,8},{10,11... | collective-permute-start | bytes 1572872 | tf_op jit(solution)/shard_map/cond/branch_1_fun/ppermute | solution.py:324
  61.9 14.1 %collective-permute-start.12 = (f32[4,128,128]{2,1,0:T(8,128)S(1)}, f32[4,128,128]{2,1,0:T(8,128)S(1)}, u32[]{:S(2)}, u32[]{:S(2)}) collective-permute-start(f32[4,128,128]{2,1,0:T(8,128)S(1)} %slice.49), channel_id=1, source_target_pairs={{0,4},{1,5},{2,6},{3,7},{4,8},{5,9},{6,10},{7,11},{8,12},{9,13},{1... | collective-permute-start | bytes 786440 | tf_op jit(solution)/shard_map/cond/branch_1_fun/ppermute | solution.py:321
  63.8 14.6 %collective-permute-start.10 = (f32[4,128,128]{2,1,0:T(8,128)S(1)}, f32[4,128,128]{2,1,0:T(8,128)S(1)}, u32[]{:S(2)}, u32[]{:S(2)}) collective-permute-start(f32[4,128,128]{2,1,0:T(8,128)S(1)} %slice.48), channel_id=1, source_target_pairs={{0,12},{1,13},{2,14},{3,15},{4,0},{5,1},{6,2},{7,3},{8,4},{9,5},{1... | collective-permute-start | bytes 786440 | tf_op jit(solution)/shard_map/cond/branch_1_fun/ppermute | solution.py:321
  68.4 12.0 %collective-permute-start.17 = (f32[8,128,128]{2,1,0:T(8,128)S(1)}, f32[8,128,128]{2,1,0:T(8,128)S(1)}, u32[]{:S(2)}, u32[]{:S(2)}) collective-permute-start(f32[8,128,128]{2,1,0:T(8,128)S(1)} %collective-permute-done.11.refs_4_), channel_id=1, source_target_pairs={{0,1},{1,0},{2,3},{3,2},{4,5},{5,4},{6,7},{7,6},{8,9},{9,8},{10,11... | collective-permute-start | bytes 1572872 | tf_op jit(solution)/shard_map/cond/branch_1_fun/ppermute | solution.py:324
  74.1 7.8 %collective-permute-start.14 = (f32[8,128,128]{2,1,0:T(8,128)S(1)}, f32[8,128,128]{2,1,0:T(8,128)S(1)}, u32[]{:S(2)}, u32[]{:S(2)}) collective-permute-start(f32[8,128,128]{2,1,0:T(8,128)S(1)} %collective-permute-done.9.refs_1_), channel_id=1, source_target_pairs={{0,1},{1,0},{2,3},{3,2},{4,5},{5,4},{6,7},{7,6},{8,9},{9,8},{10,11... | collective-permute-start | bytes 1572872 | tf_op jit(solution)/shard_map/cond/branch_1_fun/ppermute | solution.py:324
  76.0 4.4 %collective-permute-start.16 = (f32[4,128,128]{2,1,0:T(8,128)S(1)}, f32[4,128,128]{2,1,0:T(8,128)S(1)}, u32[]{:S(2)}, u32[]{:S(2)}) collective-permute-start(f32[4,128,128]{2,1,0:T(8,128)S(1)} %collective-permute-done.12.refs_3_), channel_id=1, source_target_pairs={{0,1},{1,0},{2,3},{3,2},{4,5},{5,4},{6,7},{7,6},{8,9},{9,8},{10,11... | collective-permute-start | bytes 786440 | tf_op jit(solution)/shard_map/cond/branch_1_fun/ppermute | solution.py:324
  78.4 3.4 %collective-permute-start.15 = (f32[4,128,128]{2,1,0:T(8,128)S(1)}, f32[4,128,128]{2,1,0:T(8,128)S(1)}, u32[]{:S(2)}, u32[]{:S(2)}) collective-permute-start(f32[4,128,128]{2,1,0:T(8,128)S(1)} %collective-permute-done.10.refs_2_), channel_id=1, source_target_pairs={{0,1},{1,0},{2,3},{3,2},{4,5},{5,4},{6,7},{7,6},{8,9},{9,8},{10,11... | collective-permute-start | bytes 786440 | tf_op jit(solution)/shard_map/cond/branch_1_fun/ppermute | solution.py:324
